TPU v7x, 32 devices: a whole 2x2x4 slice. The times are simulated.
32 devices in a mesh: dp: 2 (over x), expert: 4 (over y, core), shard: 4 (over z).
Axes of the slice: x: 2, y: 2, z: 4, core: 2. Of those that a mesh axis runs over, the one named last changes fastest.
Arguments:
- tokens: bfloat16 [16, 1024, 1536], P(('expert', 'shard'), 'dp'), may hold values from -6 to 6
- cotangent: bfloat16 [16, 1024, 1536], P(('expert', 'shard'), 'dp'), may hold values from -6 to 6
- gain_attn: float32 [1536], replicated, may hold values from 0.1 to 1.9
- w_query: bfloat16 [1536, 1536], P('shard')
- key_weight: bfloat16 [1536, 512], P('shard'), may hold values from -0.15625 to 0.15625
- value_weight: bfloat16 [1536, 512], P('shard'), may hold values from -0.15625 to 0.15625
- w_output: bfloat16 [1536, 1536], P('shard'), may hold values from -2 to 2
- gain_ffn: float32 [1536], replicated, may hold values from 0.1 to 1.9
- w_router: bfloat16 [1536, 32], replicated, may hold values from -0.076171875 to 0.076171875
- expert_in: bfloat16 [32, 1536, 1024], P(('expert', 'shard')), may hold values from -0.15625 to 0.15625
- expert_out: bfloat16 [32, 512, 1536], P(('expert', 'shard')), may hold values from -1 to 1
- routes: int32 [16, 1024, 8], P(('expert', 'shard'), 'dp'), may hold values from 0 to 31, all different within a row; in each aligned block of 512 rows (0 to 511, 512 to 1023, ..., all dimensions but the last counted through in order) at most 256 rows name the same one
- doc_ids: int32 [16, 1024], P(('expert', 'shard'), 'dp'), may hold values from 0 to 2, as said below
- threshold: int32 [1], replicated, may hold values from 1 to 3
Outputs:
- out: bfloat16 [16, 1024, 1536], P(('expert', 'shard'), 'dp')
- grad_tokens: bfloat16 [16, 1024, 1536], P(('expert', 'shard'), 'dp')
- grad_gain_attn: float32 [1536], P(('dp', 'expert', 'shard'))
- grad_query: float32 [1536, 1536], P(('dp', 'expert', 'shard'))
- grad_key: float32 [1536, 512], P(('dp', 'expert', 'shard'))
- grad_value: float32 [1536, 512], P(('dp', 'expert', 'shard'))
- grad_output: float32 [1536, 1536], P(('dp', 'expert', 'shard'))
- grad_gain_ffn: float32 [1536], P(('dp', 'expert', 'shard'))
- grad_router: float32 [1536, 32], P(('dp', 'expert', 'shard'))
- grad_expert_in: float32 [32, 1536, 1024], P(('expert', 'shard'), 'dp')
- grad_expert_out: float32 [32, 512, 1536], P(('expert', 'shard'), 'dp')
- largest_logits: float32 [24], replicated
- clipped_query: bfloat16 [1536, 1536], P('shard')
- clipped_key: bfloat16 [1536, 512], P('shard')
Inputs may be any that keep to these rules, and one draw needn't show every extreme that they name: `routes`: on the rows of one device no expert is named more than 256 times; the 8 ids of a token differ. `doc_ids`: each sequence holds three documents, numbered 0, 1, 2 in order of position; document 1 starts after position 0 and within the first 256 positions, document 2 starts within the last 256 positions and after the first of them.
All inputs are finite; a program needn't handle non-finite values.
Results may differ from a plain program's by a relative error of at most 0.018.
The roundings to bfloat16 on the way count: a program that leaves them out, or rounds other values in their place, can miss the bound.
Values may be sent and summed in bfloat16 or wider, within the bound.
A program may use at most 320 MiB of HBM per device.

v0:
```python
import math

import jax
import jax.numpy as jnp
from jax import lax
from jax.sharding import PartitionSpec as P

QUERY_HEADS = 24
KEY_VALUE_HEADS = 8
HEAD_DIM = 64
TOP = 8


EPSILON = 1e-06
EXCLUDED = -1e30


def rope_tables(positions, head_size):
    half_size = head_size // 2
    frequency = jnp.exp(
        jnp.arange(half_size).astype(jnp.float32) * (-2.0 * math.log(10000.0) / head_size)
    )
    angles = positions.astype(jnp.float32)[:, None] * frequency[None, :]
    return (jnp.cos(angles), jnp.sin(angles))


def apply_rotary(values, cosine_lookup, sine_lookup):
    half_size = values.shape[-1] // 2
    first_half = values[..., :half_size]
    second = values[..., half_size:]
    cosine_b = cosine_lookup[:, None, :]
    sine_b = sine_lookup[:, None, :]
    return jnp.concatenate(
        [first_half * cosine_b - second * sine_b, second * cosine_b + first_half * sine_b], axis=-1
    )


def rms_scale(values):
    return lax.rsqrt(jnp.mean(values * values, axis=-1, keepdims=True) + EPSILON)


def norm_back(grad_normed, normed, inv_rms, gain_vector):
    scaled = grad_normed * gain_vector
    return inv_rms * (scaled - normed * jnp.mean(scaled * normed, axis=-1, keepdims=True))


def contract_rows(left_side, right_side):
    return lax.dot_general(
        left_side, right_side, (((0,), (0,)), ((), ())), preferred_element_type=jnp.float32
    )


def contract_cols(left_side, right_side):
    return lax.dot_general(
        left_side, right_side, (((1,), (1,)), ((), ())), preferred_element_type=jnp.float32
    )


def on_device(
    tokens,
    cotangent,
    gain_attn,
    w_query,
    key_weight,
    value_weight,
    w_output,
    gain_ffn,
    w_router,
    expert_in,
    expert_out,
    routes,
    doc_ids,
    threshold,
):
    inputs = tokens[0].astype(jnp.float32)
    token_matrix, model_width = inputs.shape
    query_per_key = QUERY_HEADS // KEY_VALUE_HEADS
    scale_attn = rms_scale(inputs)
    normed_attn = inputs * scale_attn
    hidden_attn = (normed_attn * gain_attn).astype(jnp.bfloat16)
    full_query, full_key, full_value, full_output = (
        lax.all_gather(w_query, "shard", axis=0, tiled=True),
        lax.all_gather(key_weight, "shard", axis=0, tiled=True),
        lax.all_gather(value_weight, "shard", axis=0, tiled=True),
        lax.all_gather(w_output, "shard", axis=0, tiled=True),
    )
    own_positions = lax.axis_index("dp") * token_matrix + jnp.arange(token_matrix)
    local_cosine, local_sine = rope_tables(own_positions, HEAD_DIM)
    query_proj = jnp.dot(hidden_attn, full_query, preferred_element_type=jnp.float32)
    key_projected = jnp.dot(hidden_attn, full_key, preferred_element_type=jnp.float32)
    value_proj = jnp.dot(hidden_attn, full_value, preferred_element_type=jnp.float32)
    query_rotated = (
        apply_rotary(
            query_proj.reshape(token_matrix, QUERY_HEADS, HEAD_DIM), local_cosine, local_sine
        )
        * 0.125
    ).astype(jnp.bfloat16)
    key_rotated = (
        apply_rotary(
            key_projected.reshape(token_matrix, KEY_VALUE_HEADS, HEAD_DIM), local_cosine, local_sine
        )
        .astype(jnp.bfloat16)
        .reshape(token_matrix, KEY_VALUE_HEADS * HEAD_DIM)
    )
    value_low = value_proj.astype(jnp.bfloat16)
    own_docs = doc_ids[0]
    gathered_keys, gathered_values, docs_all = (
        lax.all_gather(key_rotated, "dp", axis=0, tiled=True),
        lax.all_gather(value_low, "dp", axis=0, tiled=True),
        lax.all_gather(own_docs, "dp", axis=0, tiled=True),
    )
    total_keys = gathered_keys.shape[0]
    allowed = (jnp.arange(total_keys)[None, :] <= own_positions[:, None]) & (
        docs_all[None, :] == own_docs[:, None]
    )
    heads_of_query = query_rotated.reshape(
        token_matrix, KEY_VALUE_HEADS, query_per_key, HEAD_DIM
    ).transpose(1, 2, 0, 3)
    heads_of_key = gathered_keys.reshape(total_keys, KEY_VALUE_HEADS, HEAD_DIM).transpose(1, 0, 2)
    heads_of_value = gathered_values.reshape(total_keys, KEY_VALUE_HEADS, HEAD_DIM).transpose(
        1, 0, 2
    )

    def attend(operands):
        query_group, key_group, value_group = operands
        scores = jnp.einsum(
            "gtd,sd->gts", query_group, key_group, preferred_element_type=jnp.float32
        )
        scores = jnp.where(allowed[None], scores, EXCLUDED)
        row_max = jnp.max(scores, axis=-1, keepdims=True)
        exponent = jnp.exp(scores - row_max)
        totals = jnp.sum(exponent, axis=-1, keepdims=True)
        attn_probs = (exponent / totals).astype(jnp.bfloat16)
        head_mix = jnp.einsum(
            "gts,sd->gtd", attn_probs, value_group, preferred_element_type=jnp.float32
        )
        return (head_mix, (row_max + jnp.log(totals))[..., 0], jnp.max(row_max[..., 0], axis=-1))

    head_mix, log_totals, head_max = lax.map(attend, (heads_of_query, heads_of_key, heads_of_value))
    largest = lax.pmax(head_max.reshape(QUERY_HEADS), ("dp", "expert", "shard"))
    attn_low = (
        head_mix.transpose(2, 0, 1, 3)
        .reshape(token_matrix, QUERY_HEADS * HEAD_DIM)
        .astype(jnp.bfloat16)
    )
    branch_attn = contract_cols(attn_low, full_output)
    residual = inputs + branch_attn
    scale_ffn = rms_scale(residual)
    normed_ffn = residual * scale_ffn
    hidden_ffn = (normed_ffn * gain_ffn).astype(jnp.bfloat16)
    expert_count = w_router.shape[1]
    local_experts = expert_in.shape[0]
    groups = expert_count // local_experts
    capacity = 2 * token_matrix * TOP // expert_count
    expert_width = expert_out.shape[1]
    router_logits = jnp.dot(hidden_ffn, w_router, preferred_element_type=jnp.float32)
    route_ids = routes[0]
    picked = (route_ids[:, :, None] == jnp.arange(expert_count)[None, None, :]).astype(jnp.float32)
    chosen = jnp.sum(picked * router_logits[:, None, :], axis=-1)
    chosen_exp = jnp.exp(chosen - jnp.max(chosen, axis=-1, keepdims=True))
    gate_weights = chosen_exp / jnp.sum(chosen_exp, axis=-1, keepdims=True)
    flat_experts = route_ids.reshape(-1)
    one_hot = (flat_experts[:, None] == jnp.arange(expert_count)[None, :]).astype(jnp.int32)
    slot_place = jnp.sum((jnp.cumsum(one_hot, axis=0) - one_hot) * one_hot, axis=1)
    slot_index = flat_experts * capacity + slot_place

    def pack_rows(row_values):
        filled = (
            jnp.zeros((expert_count * capacity, model_width), jnp.bfloat16)
            .at[slot_index]
            .set(row_values)
        )
        return filled.reshape(groups, local_experts, capacity, model_width)

    def unpack_rows(buffer):
        return buffer.reshape(expert_count * capacity, model_width)[slot_index].reshape(
            token_matrix, TOP, model_width
        )

    outgoing = pack_rows(jnp.repeat(hidden_ffn, TOP, axis=0))
    received = lax.all_to_all(
        outgoing, ("expert", "shard"), split_axis=0, concat_axis=0, tiled=True
    )
    gate_up = jnp.einsum("secd,edf->secf", received, expert_in, preferred_element_type=jnp.float32)
    gate_part = gate_up[..., :expert_width]
    up_part = gate_up[..., expert_width:]
    sigmoid_gate = jax.nn.sigmoid(gate_part)
    activated = gate_part * sigmoid_gate
    hidden_low = (activated * up_part).astype(jnp.bfloat16)
    results = jnp.einsum(
        "secf,efd->secd", hidden_low, expert_out, preferred_element_type=jnp.float32
    ).astype(jnp.bfloat16)
    returned = lax.all_to_all(results, ("expert", "shard"), split_axis=0, concat_axis=0, tiled=True)
    gathered_rows = unpack_rows(returned)
    branch_ffn = jnp.einsum(
        "tk,tkd->td", gate_weights, gathered_rows, preferred_element_type=jnp.float32
    )
    out = (residual + branch_ffn).astype(jnp.bfloat16)
    grad_out = cotangent[0].astype(jnp.float32)
    grad_gates = jnp.einsum(
        "tkd,td->tk", gathered_rows, grad_out, preferred_element_type=jnp.float32
    )
    grad_rows = (
        (gate_weights[:, :, None] * grad_out[:, None, :])
        .astype(jnp.bfloat16)
        .reshape(token_matrix * TOP, model_width)
    )
    outgoing_grads = pack_rows(grad_rows)
    grad_results = lax.all_to_all(
        outgoing_grads, ("expert", "shard"), split_axis=0, concat_axis=0, tiled=True
    )
    weight_out_grad = jnp.einsum(
        "secf,secd->efd", hidden_low, grad_results, preferred_element_type=jnp.float32
    )
    grad_hidden = jnp.einsum(
        "secd,efd->secf", grad_results, expert_out, preferred_element_type=jnp.float32
    )
    grad_gate = grad_hidden * up_part * sigmoid_gate * (1.0 + gate_part * (1.0 - sigmoid_gate))
    grad_up = grad_hidden * activated
    grad_gate_up = jnp.concatenate([grad_gate, grad_up], axis=-1).astype(jnp.bfloat16)
    weight_in_grad = jnp.einsum(
        "secd,secf->edf", received, grad_gate_up, preferred_element_type=jnp.float32
    )
    grad_received = jnp.einsum(
        "secf,edf->secd", grad_gate_up, expert_in, preferred_element_type=jnp.float32
    ).astype(jnp.bfloat16)
    grad_sent = lax.all_to_all(
        grad_received, ("expert", "shard"), split_axis=0, concat_axis=0, tiled=True
    )
    grad_in_shard, grad_out_shard = (
        lax.psum_scatter(
            weight_in_grad.astype(jnp.bfloat16), "dp", scatter_dimension=1, tiled=True
        ).astype(jnp.float32),
        lax.psum_scatter(
            weight_out_grad.astype(jnp.bfloat16), "dp", scatter_dimension=1, tiled=True
        ).astype(jnp.float32),
    )
    grad_hidden_ffn = jnp.sum(unpack_rows(grad_sent), axis=1, dtype=jnp.float32)
    grad_chosen = gate_weights * (
        grad_gates - jnp.sum(gate_weights * grad_gates, axis=-1, keepdims=True)
    )
    grad_logits = jnp.einsum("tk,tke->te", grad_chosen, picked).astype(jnp.bfloat16)
    router_grad = contract_rows(hidden_ffn, grad_logits)
    grad_hidden_ffn = grad_hidden_ffn + contract_cols(grad_logits, w_router)
    gain_ffn_grad = jnp.sum(grad_hidden_ffn * normed_ffn, axis=0)
    grad_residual = grad_out + norm_back(grad_hidden_ffn, normed_ffn, scale_ffn, gain_ffn)
    grad_branch = grad_residual.astype(jnp.bfloat16)
    output_grad = contract_rows(grad_branch, attn_low)
    attention_gradient = jnp.dot(
        grad_branch, full_output, preferred_element_type=jnp.float32
    ).astype(jnp.bfloat16)
    head_gradient = attention_gradient.reshape(
        token_matrix, KEY_VALUE_HEADS, query_per_key, HEAD_DIM
    ).transpose(1, 2, 0, 3)

    def attend_back(operands):
        query_group, key_group, value_group, grad_group, log_group = operands
        scores = jnp.einsum(
            "gtd,sd->gts", query_group, key_group, preferred_element_type=jnp.float32
        )
        attn_probs = jnp.where(allowed[None], jnp.exp(scores - log_group[..., None]), 0.0)
        grad_probs = jnp.einsum(
            "gtd,sd->gts", grad_group, value_group, preferred_element_type=jnp.float32
        )
        centre = jnp.sum(attn_probs * grad_probs, axis=-1, keepdims=True)
        grad_scores = (attn_probs * (grad_probs - centre)).astype(jnp.bfloat16)
        grad_query_group = jnp.einsum(
            "gts,sd->gtd", grad_scores, key_group, preferred_element_type=jnp.float32
        )
        grad_key_group = jnp.einsum(
            "gts,gtd->sd", grad_scores, query_group, preferred_element_type=jnp.float32
        )
        grad_value_group = jnp.einsum(
            "gts,gtd->sd",
            attn_probs.astype(jnp.bfloat16),
            grad_group,
            preferred_element_type=jnp.float32,
        )
        return (grad_query_group, grad_key_group, grad_value_group)

    grad_query_heads, key_head_gradient, value_head_gradient = lax.map(
        attend_back, (heads_of_query, heads_of_key, heads_of_value, head_gradient, log_totals)
    )
    complete_key_gradient = key_head_gradient.transpose(1, 0, 2).reshape(
        total_keys, KEY_VALUE_HEADS * HEAD_DIM
    )
    complete_value_gradient = value_head_gradient.transpose(1, 0, 2).reshape(
        total_keys, KEY_VALUE_HEADS * HEAD_DIM
    )
    local_key_gradient, value_grad_own = (
        lax.psum_scatter(
            complete_key_gradient.astype(jnp.bfloat16), "dp", scatter_dimension=0, tiled=True
        ).astype(jnp.float32),
        lax.psum_scatter(
            complete_value_gradient.astype(jnp.bfloat16), "dp", scatter_dimension=0, tiled=True
        ).astype(jnp.float32),
    )
    key_grad_low = (
        apply_rotary(
            local_key_gradient.reshape(token_matrix, KEY_VALUE_HEADS, HEAD_DIM),
            local_cosine,
            -local_sine,
        )
        .reshape(token_matrix, KEY_VALUE_HEADS * HEAD_DIM)
        .astype(jnp.bfloat16)
    )
    value_grad_low = value_grad_own.astype(jnp.bfloat16)
    query_grad_rows = grad_query_heads.transpose(2, 0, 1, 3).reshape(
        token_matrix, QUERY_HEADS, HEAD_DIM
    )
    query_grad_low = (
        (apply_rotary(query_grad_rows, local_cosine, -local_sine) * 0.125)
        .reshape(token_matrix, QUERY_HEADS * HEAD_DIM)
        .astype(jnp.bfloat16)
    )
    query_grad = contract_rows(hidden_attn, query_grad_low)
    key_grad = contract_rows(hidden_attn, key_grad_low)
    value_grad = contract_rows(hidden_attn, value_grad_low)
    grad_hidden_attn = (
        contract_cols(query_grad_low, full_query)
        + contract_cols(key_grad_low, full_key)
        + contract_cols(value_grad_low, full_value)
    )
    gain_attn_grad = jnp.sum(grad_hidden_attn * normed_attn, axis=0)
    grad_inputs = grad_residual + norm_back(grad_hidden_attn, normed_attn, scale_attn, gain_attn)
    summed = (
        lax.psum_scatter(
            gain_attn_grad, ("dp", "expert", "shard"), scatter_dimension=0, tiled=True
        ),
        lax.psum_scatter(query_grad, ("dp", "expert", "shard"), scatter_dimension=0, tiled=True),
        lax.psum_scatter(key_grad, ("dp", "expert", "shard"), scatter_dimension=0, tiled=True),
        lax.psum_scatter(value_grad, ("dp", "expert", "shard"), scatter_dimension=0, tiled=True),
        lax.psum_scatter(output_grad, ("dp", "expert", "shard"), scatter_dimension=0, tiled=True),
        lax.psum_scatter(gain_ffn_grad, ("dp", "expert", "shard"), scatter_dimension=0, tiled=True),
        lax.psum_scatter(router_grad, ("dp", "expert", "shard"), scatter_dimension=0, tiled=True),
    )
    clip_limit = threshold[0].astype(jnp.float32)
    shrink_factor = clip_limit / jnp.maximum(largest, clip_limit)
    query_scale = jnp.repeat(jnp.sqrt(shrink_factor), HEAD_DIM)
    key_shrink = jnp.repeat(
        jnp.sqrt(jnp.min(shrink_factor.reshape(KEY_VALUE_HEADS, query_per_key), axis=1)), HEAD_DIM
    )
    clipped_query = (w_query.astype(jnp.float32) * query_scale[None, :]).astype(jnp.bfloat16)
    clipped_key = (key_weight.astype(jnp.float32) * key_shrink[None, :]).astype(jnp.bfloat16)
    return (
        out[None],
        grad_inputs.astype(jnp.bfloat16)[None],
        summed[0],
        summed[1],
        summed[2],
        summed[3],
        summed[4],
        summed[5],
        summed[6],
        grad_in_shard,
        grad_out_shard,
        largest,
        clipped_query,
        clipped_key,
    )


def solution(mesh):
    return jax.shard_map(
        on_device,
        mesh=mesh,
        in_specs=(
            P(("expert", "shard"), "dp", None),
            P(("expert", "shard"), "dp", None),
            P(),
            P("shard", None),
            P("shard", None),
            P("shard", None),
            P("shard", None),
            P(),
            P(),
            P(("expert", "shard"), None, None),
            P(("expert", "shard"), None, None),
            P(("expert", "shard"), "dp", None),
            P(("expert", "shard"), "dp"),
            P(),
        ),
        out_specs=(
            P(("expert", "shard"), "dp", None),
            P(("expert", "shard"), "dp", None),
            P(("dp", "expert", "shard")),
            P(("dp", "expert", "shard"), None),
            P(("dp", "expert", "shard"), None),
            P(("dp", "expert", "shard"), None),
            P(("dp", "expert", "shard"), None),
            P(("dp", "expert", "shard")),
            P(("dp", "expert", "shard"), None),
            P(("expert", "shard"), "dp", None),
            P(("expert", "shard"), "dp", None),
            P(),
            P("shard", None),
            P("shard", None),
        ),
        check_vma=False,
    )
```

profile of v0, /device:TPU:0, one launch (start us, length us, event | category | flops | bytes accessed | tf_op | source)
XLA Modules:
  0.0 3786.9 jit_solution(161631792882108519)
XLA Ops:
  10.5 38.9 %all-gather.14.cloned.1.call-done = bf16[1536,512]{1,0:T(8,128)(2,1)} async-done(((bf16[384,512]{1,0:T(8,128)(2,1)}), bf16[1536,512]{1,0:T(8,128)(2,1)}) %all-gather.14.cloned.1.call-update) | async-done | bytes 1572880 | tf_op jit(solution)/shard_map/all_gather | solution.py:84
  49.4 3.7 convolution_convert_fusion.3
  54.8 32.2 all-gather.10.cloned.1.call-done
  99.0 4.5 all-gather
  106.8 18.1 reduce-window.6
  130.9 69.3 %all-gather.8.cloned.1.call-done = bf16[1536,1536]{1,0:T(8,128)(2,1)} async-done(((bf16[384,1536]{1,0:T(8,128)(2,1)}), bf16[1536,1536]{1,0:T(8,128)(2,1)}) %all-gather.8.cloned.1.call-update) | async-done | bytes 4718608 | tf_op jit(solution)/shard_map/all_gather | solution.py:82
  200.2 6.6 copy.67
  206.8 5.4 fusion.115
  214.6 7.4 all-gather.12.cloned.1.call-done
  222.0 83.9 %while.32 = (s32[]{:T(128)}, bf16[8,3,512,64]{2,3,1,0:T(8,128)(2,1)}, f32[8,3,512]{2,1,0:T(4,128)}, f32[8,3]{1,0:T(8,128)}, bf16[8,3,512,64]{2,3,1,0:T(8,128)(2,...) while((s32[]{:T(128)}, ...), condition=%wide.region_5.6_spmd.clone.clone, body=%wide.region_1.5_spmd.clone.sunk.clone | while | flops 419953152 | bytes 21885080 | solution.py:139
  226.9 3.6 fusion.211
  237.5 3.6 fusion.211
  248.0 3.6 fusion.211
  258.4 3.6 fusion.211
  268.9 3.6 fusion.211
  279.4 3.6 fusion.211
  289.9 3.6 fusion.211
  300.4 3.6 fusion.211
  305.9 7.0 all-gather.18.cloned.1.call-done
  312.9 6.0 multiply_reduce_fusion.3
  319.3 6.5 broadcast_bitcast_fusion
  325.9 33.9 scatter_custom_fusion
  359.8 551.4 %all_to_all.20 = bf16[16,2,256,1536]{3,2,1,0:T(8,128)(2,1)} all-to-all(bf16[16,2,256,1536]{3,2,1,0:T(8,128)(2,1)} %bitcast.334), channel_id=1, replica_groups=mesh['dp'=2,'expert'=4,'shard'=4] {'expert','shard'}, dimensions={0} | all-to-all | bytes 50331648 | tf_op jit(solution)/shard_map/all_to_all | solution.py:181
  911.2 34.5 fusion.63
  945.7 15.1 multiply_convert_fusion.1
  960.8 20.3 fusion.61
  981.1 20.8 copy.74
  1002.0 5.8 all-to-all-start.1
  1007.8 3.6 bitcast_convert_fusion.2
  1012.1 539.4 %all-to-all-done.1 = bf16[16,2,256,1536]{3,2,1,0:T(8,128)(2,1)} async-done(((bf16[16,2,256,1536]{3,2,1,0:T(8,128)(2,1)}), bf16[16,2,256,1536]{3,2,1,0:T(8,128)(2,1)}, u32[]{:S(2)}, u32[]{:S(2)}) %all-to-all-start.1) | async-done | bytes 25165856 | tf_op jit(solution)/shard_map/all_to_all | solution.py:193
  1551.5 36.8 gather_fusion
  1588.3 8.5 fusion.73
  1597.8 8.3 fusion.54
  1606.1 34.2 scatter_custom_fusion.1
  1640.3 551.4 %all_to_all.21 = bf16[16,2,256,1536]{3,2,1,0:T(8,128)(2,1)} all-to-all(bf16[16,2,256,1536]{3,2,1,0:T(8,128)(2,1)} %bitcast.333), channel_id=1, replica_groups=mesh['dp'=2,'expert'=4,'shard'=4] {'expert','shard'}, dimensions={0} | all-to-all | bytes 50331648 | tf_op jit(solution)/shard_map/all_to_all | solution.py:209
  2191.7 30.9 fusion.68
  2222.6 33.6 fusion.62
  2256.2 20.8 copy.77
  2277.1 5.7 all-to-all-start.3
  2283.6 7.5 fusion.75
  2291.1 535.5 %all-to-all-done.3 = bf16[16,2,256,1536]{3,2,1,0:T(8,128)(2,1)} async-done(((bf16[16,2,256,1536]{3,2,1,0:T(8,128)(2,1)}), bf16[16,2,256,1536]{3,2,1,0:T(8,128)(2,1)}, u32[]{:S(2)}, u32[]{:S(2)}) %all-to-all-start.3) | async-done | bytes 25165856 | tf_op jit(solution)/shard_map/all_to_all | solution.py:227
  2826.6 36.7 gather_fusion.1
  2863.3 10.7 convert_reduce_fusion
  2879.0 3.7 convolution_convert_fusion.2
  2885.2 130.4 %while.33 = (s32[]{:T(128)}, f32[8,3,512,64]{2,3,1,0:T(8,128)}, bf16[8,1024,64]{1,2,0:T(8,128)(2,1)}, bf16[8,1024,64]{1,2,0:T(8,128)(2,1)}, bf16[8,3,512,64]{2,3...) while((s32[]{:T(128)}, f32[8,3,512,64]{2,3,1,0:T(8,128)}, ...), condition=%wide.region_20.21_spmd.clone.clone, body=%wide.region_18.20_spmd.clone.sunk.clone | while | flops 1027078656 | bytes 51436672 | solution.py:281
  3018.1 20.7 bitcast_convert_fusion.1
  3038.9 33.8 bitcast_convert_fusion
  3074.1 4.0 fusion.128
  3084.7 7.3 fusion.121
  3096.4 5.4 fusion.119
  3102.6 37.4 pmax.7
  3142.6 15.5 reduce-scatter.28.cloned.1.call-done
  3159.5 43.7 %reduce-scatter.26.cloned.1.call-done = bf16[2,256,1536]{2,1,0:T(8,128)(2,1)} async-done(((bf16[2,512,1536]{2,1,0:T(8,128)(2,1)}), bf16[2,256,1536]{2,1,0:T(8,128)(2,1)}) %reduce-scatter.26.cloned.1.call-update) | async-done | bytes 1572880 | tf_op jit(solution)/shard_map/reduce_scatter | solution.py:234
  3203.2 3.5 convert_element_type.247
  3206.7 76.6 %reduce-scatter.24.cloned.1.call-done = bf16[2,768,1024]{2,1,0:T(8,128)(2,1)} async-done(((bf16[2,1536,1024]{2,1,0:T(8,128)(2,1)}), bf16[2,768,1024]{2,1,0:T(8,128)(2,1)}) %reduce-scatter.24.cloned.1.call-update) | async-done | bytes 3145744 | tf_op jit(solution)/shard_map/reduce_scatter | solution.py:231
  3283.3 5.5 convert_element_type.245
  3288.8 4.8 fusion.147
  3295.2 3.4 fusion.100
  3298.7 39.4 %all-reduce.2 = (f32[1536]{0:T(1024)S(1)}, f32[1536]{0:T(1024)S(1)}) all-reduce(f32[1536]{0:T(1024)S(1)} %get-tuple-element.176, f32[1536]{0:T(1024)S(1)} %copy-done.53), channel_id=5, replica_groups=mesh['dp'=2,'expert'=4,'shard'=4] {'dp','expert','shard'}, use_global_device_ids=true, to_apply=%region_25.26.clone | all-reduce | flops 3072 | bytes 24576
  3339.2 5.4 fusion.112
  3344.7 45.9 %reduce-scatter.20.cloned.1.call-done = f32[48,512]{1,0:T(8,128)} async-done(((f32[1536,512]{1,0:T(8,128)}), f32[48,512]{1,0:T(8,128)}) %reduce-scatter.20.cloned.1.call-update) | async-done | bytes 98320 | tf_op jit(solution)/shard_map/reduce_scatter | solution.py:332
  3390.6 106.5 %reduce-scatter.18.cloned.1.call-done = f32[48,512]{1,0:T(8,128)} async-done(((f32[1536,512]{1,0:T(8,128)}), f32[48,512]{1,0:T(8,128)}) %reduce-scatter.18.cloned.1.call-update) | async-done | bytes 98320 | tf_op jit(solution)/shard_map/reduce_scatter | solution.py:331
  3497.1 141.1 %reduce-scatter.22.cloned.1.call-done = f32[48,1536]{1,0:T(8,128)} async-done(((f32[1536,1536]{1,0:T(8,128)}), f32[48,1536]{1,0:T(8,128)}) %reduce-scatter.22.cloned.1.call-update) | async-done | bytes 294928 | tf_op jit(solution)/shard_map/reduce_scatter | solution.py:333
  3638.2 142.0 %reduce-scatter.16.cloned.1.call-done = f32[48,1536]{1,0:T(8,128)} async-done(((f32[1536,1536]{1,0:T(8,128)}), f32[48,1536]{1,0:T(8,128)}) %reduce-scatter.16.cloned.1.call-update) | async-done | bytes 294928 | tf_op jit(solution)/shard_map/reduce_scatter | solution.py:330
  (329 shorter events, 244.7 us)
Async XLA Ops:
  7.2 953.6 %copy-start = (bf16[2,512,1536]{2,1,0:T(8,128)(2,1)S(1)}, bf16[2,512,1536]{2,1,0:T(8,128)(2,1)}, u32[]{:S(2)}) copy-start(bf16[2,512,1536]{2,1,0:T(8,128)(2,1)} %param.28) | copy-start | bytes 9437188
  7.2 42.2 %all-gather.14.cloned.1.call-start = ((), (), s32[]{:S(2)}) async-start(), calls=%async_computation.16 | async-start | bytes 1966080 | tf_op jit(solution)/shard_map/all_gather | solution.py:84
  7.9 79.1 %all-gather.10.cloned.1.call-start = ((), (), s32[]{:S(2)}) async-start(), calls=%async_computation.14 | async-start | bytes 1966080 | tf_op jit(solution)/shard_map/all_gather | solution.py:83
  8.7 119.9 %all-gather.16.cloned.1.call-start = ((), (), s32[]{:S(2)}) async-start(), calls=%async_computation.17 | async-start | bytes 1572864 | tf_op jit(solution)/shard_map/all_gather | solution.py:109
  10.5 79.0 %copy-start.43 = (f32[512]{0:T(512)}, f32[512]{0:T(512)S(1)}, u32[]{:S(2)}) copy-start(f32[512]{0:T(512)S(1)} %add_rsqrt_fusion.1) | copy-start | bytes 6148
  53.1 36.4 copy-start.24
  53.2 147.1 %all-gather.8.cloned.1.call-start = ((), (), s32[]{:S(2)}) async-start(), calls=%async_computation.13 | async-start | bytes 5898240 | tf_op jit(solution)/shard_map/all_gather | solution.py:82
  53.7 168.2 %all-gather.12.cloned.1.call-start = ((), (), s32[]{:S(2)}) async-start(), calls=%async_computation.15 | async-start | bytes 1572864 | tf_op jit(solution)/shard_map/all_gather | solution.py:108
  54.8 157.4 %copy-start.17 = (f32[512,32]{0,1:T(8,128)}, f32[512,32]{0,1:T(8,128)S(1)}, u32[]{:S(2)}) copy-start(f32[512,32]{0,1:T(8,128)S(1)} %get-tuple-element.246) | copy-start | bytes 196612
  92.5 2.2 copy-start.32
  92.5 6.5 copy-start.35
  93.6 219.3 %all-gather.18.cloned.1.call-start = ((), (), s32[]{:S(2)}) async-start(), calls=%async_computation.18 | async-start | bytes 5898240 | tf_op jit(solution)/shard_map/all_gather | solution.py:85
  105.2 23.0 copy-start.48
  105.2 23.4 copy-start.49
  128.6 879.2 %copy-start.50 = (s32[4096,1]{0,1:T(1,128)}, s32[4096,1]{0,1:T(1,128)S(1)}, u32[]{:S(2)}) copy-start(s32[4096,1]{0,1:T(1,128)S(1)} %compare_select_fusion) | copy-start | bytes 49156
  200.2 6.6 copy-start.44
  212.9 9.1 copy-start.37
  305.9 13.1 copy-start.26
  312.9 6.1 copy-start.46
  318.9 6.9 copy-start.4
  319.0 6.9 copy-start.51
  319.3 6.6 copy-start.6
  1002.0 549.6 %all-to-all-start.1 = ((bf16[16,2,256,1536]{3,2,1,0:T(8,128)(2,1)}), bf16[16,2,256,1536]{3,2,1,0:T(8,128)(2,1)}, u32[]{:S(2)}, u32[]{:S(2)}) async-start(bf16[16,2,256,1536]{3,2,1,0:T(8,128)(2,1)} %copy.74), calls=%async_computation.1 | async-start | bytes 50331648 | tf_op jit(solution)/shard_map/all_to_all | solution.py:193
  1007.8 3.7 copy-start.7
  1007.8 3.7 copy-start.28
  1007.8 543.8 %copy-start.41 = (s32[4096]{0:T(1024)}, s32[4096]{0:T(1024)S(1)}, u32[]{:S(2)}) copy-start(s32[4096]{0:T(1024)S(1)} %broadcast_clamp_fusion) | copy-start | bytes 49156
  1007.8 4.2 copy-start.33
  1596.9 9.2 copy-start.39
  1597.5 8.6 copy-start.30
  2277.0 6.0 copy-start.31
  2277.1 6.0 copy-start.40
  2277.1 6.0 copy-start.54
  2277.1 6.0 copy-start.34
  2277.1 549.5 %all-to-all-start.3 = ((bf16[16,2,256,1536]{3,2,1,0:T(8,128)(2,1)}), bf16[16,2,256,1536]{3,2,1,0:T(8,128)(2,1)}, u32[]{:S(2)}, u32[]{:S(2)}) async-start(bf16[16,2,256,1536]{3,2,1,0:T(8,128)(2,1)} %copy.77), calls=%async_computation.3 | async-start | bytes 50331648 | tf_op jit(solution)/shard_map/all_to_all | solution.py:227
  2282.8 790.0 %reduce-scatter.14.cloned.1.call-start = ((), (), s32[]{:S(2)}) async-start(), calls=%async_computation.20 | async-start | bytes 1572864 | tf_op jit(solution)/shard_map/reduce_scatter | solution.py:294
  2283.5 543.0 %copy-start.42 = (s32[4096]{0:T(1024)S(1)}, s32[4096]{0:T(1024)}, u32[]{:S(2)}) copy-start(s32[4096]{0:T(1024)} %copy-done.41) | copy-start | bytes 49156
  2863.3 10.7 copy-start.5
  2863.3 10.7 copy-start.29
  2863.3 10.7 copy-start.47
  2863.3 10.7 copy-start.52
  2874.0 2.4 copy-start.12
  2874.1 4.6 slice-start
  2876.4 2.6 slice-start.1
  2878.6 4.0 copy-start.3
  2882.6 2.6 copy-start.27
  2882.6 2.6 copy-start.36
  2882.6 2.6 copy-start.38
  2885.2 131.3 %copy-start.8 = (bf16[512,1536]{1,0:T(8,128)(2,1)S(1)}, bf16[512,1536]{1,0:T(8,128)(2,1)}, u32[]{:S(2)}) copy-start(bf16[512,1536]{1,0:T(8,128)(2,1)} %copy-done.6) | copy-start | bytes 4718596
  3015.7 62.5 %reduce-scatter.12.cloned.1.call-start = ((), (), s32[]{:S(2)}) async-start(), calls=%async_computation.19 | async-start | bytes 1572864 | tf_op jit(solution)/shard_map/reduce_scatter | solution.py:291
  3016.4 141.7 %reduce-scatter.28.cloned.1.call-start = ((), (), s32[]{:S(2)}) async-start(), calls=%async_computation.27 | async-start | bytes 811008
  3018.0 185.2 %reduce-scatter.26.cloned.1.call-start = ((), (), s32[]{:S(2)}) async-start(), calls=%async_computation.26 | async-start | bytes 4718592 | tf_op jit(solution)/shard_map/reduce_scatter | solution.py:234
  3038.8 244.5 %reduce-scatter.24.cloned.1.call-start = ((), (), s32[]{:S(2)}) async-start(), calls=%async_computation.25 | async-start | bytes 9437184 | tf_op jit(solution)/shard_map/reduce_scatter | solution.py:231
  3072.7 317.9 %reduce-scatter.20.cloned.1.call-start = ((), (), s32[]{:S(2)}) async-start(), calls=%async_computation.23 | async-start | bytes 3244032 | tf_op jit(solution)/shard_map/reduce_scatter | solution.py:332
  3078.1 419.0 %reduce-scatter.18.cloned.1.call-start = ((), (), s32[]{:S(2)}) async-start(), calls=%async_computation.22 | async-start | bytes 3244032 | tf_op jit(solution)/shard_map/reduce_scatter | solution.py:331
  3083.3 554.9 %reduce-scatter.22.cloned.1.call-start = ((), (), s32[]{:S(2)}) async-start(), calls=%async_computation.24 | async-start | bytes 9732096 | tf_op jit(solution)/shard_map/reduce_scatter | solution.py:333
  3092.1 688.1 %reduce-scatter.16.cloned.1.call-start = ((), (), s32[]{:S(2)}) async-start(), calls=%async_computation.21 | async-start | bytes 9732096 | tf_op jit(solution)/shard_map/reduce_scatter | solution.py:330
  3101.8 38.8 %copy-start.20 = (bf16[384,512]{1,0:T(8,128)(2,1)S(1)}, bf16[384,512]{1,0:T(8,128)(2,1)}, u32[]{:S(2)}) copy-start(bf16[384,512]{1,0:T(8,128)(2,1)} %param.22) | copy-start | bytes 1179652
  3101.8 39.7 %copy-start.15 = (bf16[384,1536]{1,0:T(8,128)(2,1)S(1)}, bf16[384,1536]{1,0:T(8,128)(2,1)}, u32[]{:S(2)}) copy-start(bf16[384,1536]{1,0:T(8,128)(2,1)} %param.21) | copy-start | bytes 3538948
  3140.1 66.6 %copy-start.56 = (f32[24]{0:T(128)}, f32[24]{0:T(128)S(1)}, u32[]{:S(2)}) copy-start(f32[24]{0:T(128)S(1)} %pmax.7) | copy-start | bytes 292
  3283.3 5.5 copy-start.22
  3288.8 4.8 copy-start.10
  3288.8 4.8 copy-start.14
  3295.2 3.5 copy-start.53
  3339.2 441.0 %copy-start.1 = (bf16[2,512,1536]{2,1,0:T(8,128)(2,1)S(1)}, bf16[2,512,1536]{2,1,0:T(8,128)(2,1)}, u32[]{:S(2)}) copy-start(bf16[2,512,1536]{2,1,0:T(8,128)(2,1)} %param.28) | copy-start | bytes 9437188
  (12 other events, 15.6 us)
Sparse Core Ops, SparseCore 0:
  9.6 39.7 all-gather.13
  51.0 35.9 all-gather.9
  89.1 20.1 all-gather.15
  110.8 89.4 all-gather.7
  202.2 19.7 all-gather.11
  223.4 89.4 all-gather.17
  3015.8 18.9 reduce-scatter.13
  3037.1 20.2 reduce-scatter.11
  3062.6 95.5 reduce-scatter.27
  3160.8 42.3 reduce-scatter.25
  3206.2 77.0 reduce-scatter.23
  3289.2 101.4 reduce-scatter.19
  3396.6 100.4 reduce-scatter.17
  3503.5 134.6 reduce-scatter.21
  3645.5 134.5 reduce-scatter.15
where the time goes:
time: 3800 us; the launch traced here: 3790 us
  waiting for transfers between devices  1800 us (47%)
  blocking collectives  1180 us (31%)
  matrix products  397 us (10%)
  local copies, waits for them, and re-layouts  236 us (6%)
  other arithmetic  137 us (4%)
    all_to_all x1, blocking collectives, on_device(): lax.all_to_all(outgoing, ('expert', 'shard'), split_axis=0, concat_axis=0...  551 us
    all_to_all x1, blocking collectives, on_device(): lax.all_to_all(outgoing_grads, ('expert', 'shard'), split_axis=0, concat_...  551 us
    all_to_all x1, waiting for transfers between devices, on_device(): lax.all_to_all(results, ('expert', 'shard'), split_axis=0, concat_axis=0,...  539 us
    all_to_all x1, waiting for transfers between devices, on_device(): lax.all_to_all(grad_received, ('expert', 'shard'), split_axis=0, concat_a...  535 us
    reduce_scatter x1, waiting for transfers between devices, on_device(): lax.psum_scatter(query_grad, ('dp', 'expert', 'shard'), scatter_dimension...  142 us
    reduce_scatter x1, waiting for transfers between devices, on_device(): lax.psum_scatter(output_grad, ('dp', 'expert', 'shard'), scatter_dimensio...  141 us
    reduce_scatter x1, waiting for transfers between devices, on_device(): lax.psum_scatter(key_grad, ('dp', 'expert', 'shard'), scatter_dimension=0...  107 us
    reduce_scatter x1, waiting for transfers between devices, on_device(): lax.psum_scatter(weight_in_grad.astype(jnp.bfloat16), 'dp', scatter_dimen...  76.6 us
  transfers between devices with their start and end apart: 17, of which 14 were waited for; matrix products, arithmetic and copies ran while one was open for 7% of the time, Pallas kernels for 0%

commit v1 on v0

--- a/solution.py
+++ b/solution.py
@@ -3,13 +3,16 @@
 import jax
 import jax.numpy as jnp
 from jax import lax
+from jax.experimental import pallas as pl
+from jax.experimental.pallas import tpu as pltpu
 from jax.sharding import PartitionSpec as P
 
 QUERY_HEADS = 24
 KEY_VALUE_HEADS = 8
 HEAD_DIM = 64
 TOP = 8
-
+GROUP = ("expert", "shard")
+EVERY = ("dp", "expert", "shard")
 
 EPSILON = 1e-06
 EXCLUDED = -1e30
@@ -54,6 +57,111 @@
     return lax.dot_general(
         left_side, right_side, (((1,), (1,)), ((), ())), preferred_element_type=jnp.float32
     )
+
+
+def as_column(vector, before=0):
+    return jnp.pad(vector[:, None], ((0, 0), (0, 127 - before)))
+
+
+def masked_softmax(logits, picked):
+    kept = jnp.where(picked, logits, EXCLUDED)
+    exponent = jnp.exp(kept - jnp.max(kept, axis=-1, keepdims=True))
+    return exponent / jnp.sum(exponent, axis=-1, keepdims=True)
+
+
+def experts_kernel(
+    at_ref, routes_ref, router_ref, rows_ref, cot_ref, win_ref, wout_ref,
+    out_ref, grad_ref, gates_ref, dwin_ref, dwout_ref, acc_in, acc_out,
+):
+    step, steps = pl.program_id(0), pl.num_programs(0)
+    own_count, width = wout_ref.shape[0], wout_ref.shape[1]
+
+    @pl.when(step == 0)
+    def _():
+        acc_in[...] = jnp.zeros_like(acc_in)
+        acc_out[...] = jnp.zeros_like(acc_out)
+
+    rows, cot = rows_ref[...], cot_ref[...]
+    logits = jnp.dot(rows, router_ref[...], preferred_element_type=jnp.float32)
+    lanes = lax.broadcasted_iota(jnp.int32, logits.shape, 1)
+    picked = lanes == routes_ref[:, 0:1]
+    for k in range(1, TOP):
+        picked = picked | (lanes == routes_ref[:, k : k + 1])
+    gates = masked_softmax(logits, picked)
+    first = at_ref[0] * own_count
+    out_sum = grad_sum = None
+    gate_lanes = lax.broadcasted_iota(jnp.int32, gates_ref.shape, 1)
+    gate_grads = jnp.zeros(gates_ref.shape, jnp.float32)
+    for e in range(own_count):
+        gate = jnp.sum(jnp.where(lanes == first + e, gates, 0.0), axis=1, keepdims=True)
+        both = jnp.dot(rows, win_ref[e], preferred_element_type=jnp.float32)
+        gate_part, up_part = both[:, :width], both[:, width:]
+        sig = jax.nn.sigmoid(gate_part)
+        activated = gate_part * sig
+        hidden = (activated * up_part).astype(jnp.bfloat16).astype(jnp.float32)
+        gated = (gate * hidden).astype(jnp.bfloat16)
+        term = jnp.dot(gated, wout_ref[e], preferred_element_type=jnp.float32)
+        out_sum = term if out_sum is None else out_sum + term
+        plain = contract_cols(cot, wout_ref[e])
+        own_grad = jnp.sum(plain * hidden, axis=1, keepdims=True)
+        gate_grads = jnp.where(gate_lanes == e, own_grad, gate_grads)
+        back = gate * plain
+        d_gate = back * up_part * sig * (1.0 + gate_part * (1.0 - sig))
+        d_up = back * activated
+        d_both = jnp.concatenate([d_gate, d_up], axis=1).astype(jnp.bfloat16)
+        term = contract_cols(d_both, win_ref[e])
+        grad_sum = term if grad_sum is None else grad_sum + term
+        acc_in[e] += contract_rows(rows, d_both)
+        acc_out[e] += contract_rows(gated, cot)
+    out_ref[...] = out_sum.astype(jnp.bfloat16)
+    grad_ref[...] = grad_sum.astype(jnp.bfloat16)
+    gates_ref[...] = gate_grads
+
+    @pl.when(step == steps - 1)
+    def _():
+        dwin_ref[...] = acc_in[...].astype(jnp.bfloat16)
+        dwout_ref[...] = acc_out[...].astype(jnp.bfloat16)
+
+
+def experts_pass(group_at, routes, w_router, rows, cotangent, expert_in, expert_out):
+    total, model = rows.shape
+    tile = 256
+    by_row = lambda width: pl.BlockSpec((tile, width), lambda i: (i, 0))
+    whole = lambda shape: pl.BlockSpec(
+        shape, lambda i: (0,) * len(shape), pipeline_mode=pl.Buffered(1)
+    )
+    return pl.pallas_call(
+        experts_kernel,
+        grid=(total // tile,),
+        out_shape=(
+            jax.ShapeDtypeStruct((total, model), jnp.bfloat16),
+            jax.ShapeDtypeStruct((total, model), jnp.bfloat16),
+            jax.ShapeDtypeStruct((total, expert_in.shape[0]), jnp.float32),
+            jax.ShapeDtypeStruct(expert_in.shape, jnp.bfloat16),
+            jax.ShapeDtypeStruct(expert_out.shape, jnp.bfloat16),
+        ),
+        in_specs=[
+            pl.BlockSpec(memory_space=pltpu.SMEM),
+            by_row(routes.shape[1]),
+            whole(w_router.shape),
+            by_row(model),
+            by_row(model),
+            whole(expert_in.shape),
+            whole(expert_out.shape),
+        ],
+        out_specs=(
+            by_row(model),
+            by_row(model),
+            by_row(expert_in.shape[0]),
+            whole(expert_in.shape),
+            whole(expert_out.shape),
+        ),
+        scratch_shapes=[
+            pltpu.VMEM(expert_in.shape, jnp.float32),
+            pltpu.VMEM(expert_out.shape, jnp.float32),
+        ],
+        compiler_params=pltpu.CompilerParams(vmem_limit_bytes=60 * 2**20),
+    )(group_at[None].astype(jnp.int32), routes, w_router, rows, cotangent, expert_in, expert_out)
 
 
 def on_device(
@@ -75,6 +183,9 @@
     inputs = tokens[0].astype(jnp.float32)
     token_matrix, model_width = inputs.shape
     query_per_key = QUERY_HEADS // KEY_VALUE_HEADS
+    query_width, key_width = w_query.shape[1], key_weight.shape[1]
+    all_cotangent = lax.all_gather(cotangent[0], GROUP, axis=0, tiled=True)
+    all_routes = lax.all_gather(routes[0], GROUP, axis=0, tiled=True)
     scale_attn = rms_scale(inputs)
     normed_attn = inputs * scale_attn
     hidden_attn = (normed_attn * gain_attn).astype(jnp.bfloat16)
@@ -149,103 +260,52 @@
     normed_ffn = residual * scale_ffn
     hidden_ffn = (normed_ffn * gain_ffn).astype(jnp.bfloat16)
     expert_count = w_router.shape[1]
-    local_experts = expert_in.shape[0]
-    groups = expert_count // local_experts
-    capacity = 2 * token_matrix * TOP // expert_count
-    expert_width = expert_out.shape[1]
     router_logits = jnp.dot(hidden_ffn, w_router, preferred_element_type=jnp.float32)
     route_ids = routes[0]
-    picked = (route_ids[:, :, None] == jnp.arange(expert_count)[None, None, :]).astype(jnp.float32)
-    chosen = jnp.sum(picked * router_logits[:, None, :], axis=-1)
-    chosen_exp = jnp.exp(chosen - jnp.max(chosen, axis=-1, keepdims=True))
-    gate_weights = chosen_exp / jnp.sum(chosen_exp, axis=-1, keepdims=True)
-    flat_experts = route_ids.reshape(-1)
-    one_hot = (flat_experts[:, None] == jnp.arange(expert_count)[None, :]).astype(jnp.int32)
-    slot_place = jnp.sum((jnp.cumsum(one_hot, axis=0) - one_hot) * one_hot, axis=1)
-    slot_index = flat_experts * capacity + slot_place
-
-    def pack_rows(row_values):
-        filled = (
-            jnp.zeros((expert_count * capacity, model_width), jnp.bfloat16)
-            .at[slot_index]
-            .set(row_values)
-        )
-        return filled.reshape(groups, local_experts, capacity, model_width)
-
-    def unpack_rows(buffer):
-        return buffer.reshape(expert_count * capacity, model_width)[slot_index].reshape(
-            token_matrix, TOP, model_width
-        )
-
-    outgoing = pack_rows(jnp.repeat(hidden_ffn, TOP, axis=0))
-    received = lax.all_to_all(
-        outgoing, ("expert", "shard"), split_axis=0, concat_axis=0, tiled=True
-    )
-    gate_up = jnp.einsum("secd,edf->secf", received, expert_in, preferred_element_type=jnp.float32)
-    gate_part = gate_up[..., :expert_width]
-    up_part = gate_up[..., expert_width:]
-    sigmoid_gate = jax.nn.sigmoid(gate_part)
-    activated = gate_part * sigmoid_gate
-    hidden_low = (activated * up_part).astype(jnp.bfloat16)
-    results = jnp.einsum(
-        "secf,efd->secd", hidden_low, expert_out, preferred_element_type=jnp.float32
+    picked = (route_ids[:, :, None] == jnp.arange(expert_count)[None, None, :]).any(axis=1)
+    gate_weights = masked_softmax(router_logits, picked)
+    grad_out = cotangent[0].astype(jnp.float32)
+    all_hidden = lax.all_gather(hidden_ffn, GROUP, axis=0, tiled=True)
+    group_at = lax.axis_index("expert") * lax.axis_size("shard") + lax.axis_index("shard")
+    partial_out, partial_grad, grad_gates_own, weight_in_grad, weight_out_grad = experts_pass(
+        group_at, all_routes, w_router, all_hidden, all_cotangent, expert_in, expert_out
+    )
+    grad_gates = (
+        lax.all_to_all(
+            grad_gates_own.reshape(-1, token_matrix, expert_in.shape[0]), GROUP, 0, 0, tiled=True
+        )
+        .transpose(1, 0, 2)
+        .reshape(token_matrix, expert_count)
+    )
+    grad_hidden_ffn = lax.psum_scatter(
+        partial_grad, GROUP, scatter_dimension=0, tiled=True
+    ).astype(jnp.float32)
+    branch_ffn = lax.psum_scatter(partial_out, GROUP, scatter_dimension=0, tiled=True)
+    out = (residual + branch_ffn.astype(jnp.float32)).astype(jnp.bfloat16)
+    grad_in_shard, grad_out_shard = (
+        lax.psum_scatter(weight_in_grad, "dp", scatter_dimension=1, tiled=True).astype(jnp.float32),
+        lax.psum_scatter(weight_out_grad, "dp", scatter_dimension=1, tiled=True).astype(
+            jnp.float32
+        ),
+    )
+    weighted = gate_weights * jnp.where(picked, grad_gates, 0.0)
+    grad_logits = (
+        weighted - gate_weights * jnp.sum(weighted, axis=-1, keepdims=True)
     ).astype(jnp.bfloat16)
-    returned = lax.all_to_all(results, ("expert", "shard"), split_axis=0, concat_axis=0, tiled=True)
-    gathered_rows = unpack_rows(returned)
-    branch_ffn = jnp.einsum(
-        "tk,tkd->td", gate_weights, gathered_rows, preferred_element_type=jnp.float32
-    )
-    out = (residual + branch_ffn).astype(jnp.bfloat16)
-    grad_out = cotangent[0].astype(jnp.float32)
-    grad_gates = jnp.einsum(
-        "tkd,td->tk", gathered_rows, grad_out, preferred_element_type=jnp.float32
-    )
-    grad_rows = (
-        (gate_weights[:, :, None] * grad_out[:, None, :])
-        .astype(jnp.bfloat16)
-        .reshape(token_matrix * TOP, model_width)
-    )
-    outgoing_grads = pack_rows(grad_rows)
-    grad_results = lax.all_to_all(
-        outgoing_grads, ("expert", "shard"), split_axis=0, concat_axis=0, tiled=True
-    )
-    weight_out_grad = jnp.einsum(
-        "secf,secd->efd", hidden_low, grad_results, preferred_element_type=jnp.float32
-    )
-    grad_hidden = jnp.einsum(
-        "secd,efd->secf", grad_results, expert_out, preferred_element_type=jnp.float32
-    )
-    grad_gate = grad_hidden * up_part * sigmoid_gate * (1.0 + gate_part * (1.0 - sigmoid_gate))
-    grad_up = grad_hidden * activated
-    grad_gate_up = jnp.concatenate([grad_gate, grad_up], axis=-1).astype(jnp.bfloat16)
-    weight_in_grad = jnp.einsum(
-        "secd,secf->edf", received, grad_gate_up, preferred_element_type=jnp.float32
-    )
-    grad_received = jnp.einsum(
-        "secf,edf->secd", grad_gate_up, expert_in, preferred_element_type=jnp.float32
-    ).astype(jnp.bfloat16)
-    grad_sent = lax.all_to_all(
-        grad_received, ("expert", "shard"), split_axis=0, concat_axis=0, tiled=True
-    )
-    grad_in_shard, grad_out_shard = (
-        lax.psum_scatter(
-            weight_in_grad.astype(jnp.bfloat16), "dp", scatter_dimension=1, tiled=True
-        ).astype(jnp.float32),
-        lax.psum_scatter(
-            weight_out_grad.astype(jnp.bfloat16), "dp", scatter_dimension=1, tiled=True
-        ).astype(jnp.float32),
-    )
-    grad_hidden_ffn = jnp.sum(unpack_rows(grad_sent), axis=1, dtype=jnp.float32)
-    grad_chosen = gate_weights * (
-        grad_gates - jnp.sum(gate_weights * grad_gates, axis=-1, keepdims=True)
-    )
-    grad_logits = jnp.einsum("tk,tke->te", grad_chosen, picked).astype(jnp.bfloat16)
     router_grad = contract_rows(hidden_ffn, grad_logits)
     grad_hidden_ffn = grad_hidden_ffn + contract_cols(grad_logits, w_router)
     gain_ffn_grad = jnp.sum(grad_hidden_ffn * normed_ffn, axis=0)
     grad_residual = grad_out + norm_back(grad_hidden_ffn, normed_ffn, scale_ffn, gain_ffn)
     grad_branch = grad_residual.astype(jnp.bfloat16)
     output_grad = contract_rows(grad_branch, attn_low)
+    late_sums = lax.psum_scatter(
+        jnp.concatenate(
+            [output_grad, router_grad, as_column(gain_ffn_grad, expert_count)], axis=1
+        ).astype(jnp.bfloat16),
+        EVERY,
+        scatter_dimension=0,
+        tiled=True,
+    ).astype(jnp.float32)
     attention_gradient = jnp.dot(
         grad_branch, full_output, preferred_element_type=jnp.float32
     ).astype(jnp.bfloat16)
@@ -323,17 +383,14 @@
     )
     gain_attn_grad = jnp.sum(grad_hidden_attn * normed_attn, axis=0)
     grad_inputs = grad_residual + norm_back(grad_hidden_attn, normed_attn, scale_attn, gain_attn)
-    summed = (
-        lax.psum_scatter(
-            gain_attn_grad, ("dp", "expert", "shard"), scatter_dimension=0, tiled=True
-        ),
-        lax.psum_scatter(query_grad, ("dp", "expert", "shard"), scatter_dimension=0, tiled=True),
-        lax.psum_scatter(key_grad, ("dp", "expert", "shard"), scatter_dimension=0, tiled=True),
-        lax.psum_scatter(value_grad, ("dp", "expert", "shard"), scatter_dimension=0, tiled=True),
-        lax.psum_scatter(output_grad, ("dp", "expert", "shard"), scatter_dimension=0, tiled=True),
-        lax.psum_scatter(gain_ffn_grad, ("dp", "expert", "shard"), scatter_dimension=0, tiled=True),
-        lax.psum_scatter(router_grad, ("dp", "expert", "shard"), scatter_dimension=0, tiled=True),
-    )
+    attn_sums = lax.psum_scatter(
+        jnp.concatenate(
+            [query_grad, key_grad, value_grad, as_column(gain_attn_grad)], axis=1
+        ).astype(jnp.bfloat16),
+        EVERY,
+        scatter_dimension=0,
+        tiled=True,
+    ).astype(jnp.float32)
     clip_limit = threshold[0].astype(jnp.float32)
     shrink_factor = clip_limit / jnp.maximum(largest, clip_limit)
     query_scale = jnp.repeat(jnp.sqrt(shrink_factor), HEAD_DIM)
@@ -345,13 +402,13 @@
     return (
         out[None],
         grad_inputs.astype(jnp.bfloat16)[None],
-        summed[0],
-        summed[1],
-        summed[2],
-        summed[3],
-        summed[4],
-        summed[5],
-        summed[6],
+        attn_sums[:, query_width + 2 * key_width],
+        attn_sums[:, :query_width],
+        attn_sums[:, query_width : query_width + key_width],
+        attn_sums[:, query_width + key_width : query_width + 2 * key_width],
+        late_sums[:, :query_width],
+        late_sums[:, query_width + expert_count],
+        late_sums[:, query_width : query_width + expert_count],
         grad_in_shard,
         grad_out_shard,
         largest,

time: 3800 us -> 2010 us (0.53)
  blocking collectives: 1180 us -> 185 us
  waiting for transfers between devices: 1800 us -> 1180 us
  Pallas kernels: 0 us -> 280 us
  matrix products: 397 us -> 191 us
  local copies, waits for them, and re-layouts: 236 us -> 65.3 us
  other arithmetic: 137 us -> 80.2 us
    all_to_all x2 -> x0, blocking collectives: 1100 us -> none  [the longest x1 551 us: on_device(): lax.all_to_all(outgoing, ('expert', 'shard'), split_axis=0, concat_axis=0...]
    all_to_all x2 -> x1, waiting for transfers between devices: 1070 us -> 3.98 us  [on_device(): lax.all_to_all(grad_gates_own.reshape(-1, token_matrix, expert_in.shape[0...]
    pallas_call x0 -> x1, Pallas kernels: none -> 280 us  [experts_pass(): pl.pallas_call(experts_kernel, grid=(total // tile,), out_shape=(jax.Shap...]
    unnamed x16 -> x18, waiting for transfers between devices: 18.8 us -> 245 us
    all_gather x0 -> x2, waiting for transfers between devices: none -> 208 us  [the longest x1 137 us: on_device(): all_hidden = lax.all_gather(hidden_ffn, GROUP, axis=0, tiled=True)]
    dot_general x8 -> x0, matrix products: 190 us -> none  [the longest x1 34.5 us: on_device(): jnp.einsum('secd,edf->secf', received, expert_in, preferred_element_type=...]
    all_gather x0 -> x1, blocking collectives: none -> 140 us  [on_device(): all_routes = lax.all_gather(routes[0], GROUP, axis=0, tiled=True)]
    gather x2 -> x0, local copies, waits for them, and re-layouts: 73.5 us -> none  [unpack_rows(): buffer.reshape(expert_count * capacity, model_width)[slot_index]]
  transfers between devices with their start and end apart: 17 -> 17, of which waited for: 14 -> 15; matrix products, arithmetic and copies ran while one was open for 7% -> 10% of each run, Pallas kernels for 0% -> 0%
where the time goes in v1:
time: 2010 us; the launch traced here: 2000 us
  waiting for transfers between devices  1180 us (59%)
  Pallas kernels  280 us (14%)
  matrix products  191 us (10%)
  blocking collectives  185 us (9%)
  other arithmetic  80.2 us (4%)
  local copies, waits for them, and re-layouts  65.3 us (3%)
    pallas_call x1, Pallas kernels, experts_pass(): pl.pallas_call(experts_kernel, grid=(total // tile,), out_shape=(jax.Shap...  280 us
    unnamed x18, waiting for transfers between devices  245 us
    reduce_scatter x1, waiting for transfers between devices, on_device(): lax.psum_scatter(partial_out, GROUP, scatter_dimension=0, tiled=True)  243 us
    reduce_scatter x1, waiting for transfers between devices, on_device(): lax.psum_scatter(partial_grad, GROUP, scatter_dimension=0, tiled=True)  228 us
    all_gather x1, blocking collectives, on_device(): all_routes = lax.all_gather(routes[0], GROUP, axis=0, tiled=True)  140 us
    all_gather x1, waiting for transfers between devices, on_device(): all_hidden = lax.all_gather(hidden_ffn, GROUP, axis=0, tiled=True)  137 us
    all_gather x1, waiting for transfers between devices, on_device(): lax.all_gather(w_query, 'shard', axis=0, tiled=True)  89.4 us
    all_gather x1, waiting for transfers between devices, on_device(): all_cotangent = lax.all_gather(cotangent[0], GROUP, axis=0, tiled=True)  71.1 us
  transfers between devices with their start and end apart: 17, of which 15 were waited for; matrix products, arithmetic and copies ran while one was open for 10% of the time, Pallas kernels for 0%

profile of v1, /device:TPU:0, one launch (start us, length us, event | category | flops | bytes accessed | tf_op | source)
XLA Modules:
  0.0 2004.6 jit_solution(12047585521437207049)
XLA Ops:
  10.5 38.9 %all-gather.18.cloned.1.call-done = bf16[1536,512]{1,0:T(8,128)(2,1)} async-done(((bf16[384,512]{1,0:T(8,128)(2,1)}), bf16[1536,512]{1,0:T(8,128)(2,1)}) %all-gather.18.cloned.1.call-update) | async-done | bytes 1572880 | tf_op jit(solution)/shard_map/all_gather | solution.py:195
  49.4 3.7 convolution_convert_fusion.6
  54.8 32.2 %all-gather.14.cloned.1.call-done = bf16[1536,512]{1,0:T(8,128)(2,1)} async-done(((bf16[384,512]{1,0:T(8,128)(2,1)}), bf16[1536,512]{1,0:T(8,128)(2,1)}) %all-gather.14.cloned.1.call-update) | async-done | bytes 1572880 | tf_op jit(solution)/shard_map/all_gather | solution.py:194
  94.5 4.6 all-gather
  100.4 8.9 all-gather.20.cloned.1.call-done
  110.8 89.4 %all-gather.12.cloned.1.call-done = bf16[1536,1536]{1,0:T(8,128)(2,1)} async-done(((bf16[384,1536]{1,0:T(8,128)(2,1)}), bf16[1536,1536]{1,0:T(8,128)(2,1)}) %all-gather.12.cloned.1.call-update) | async-done | bytes 4718608 | tf_op jit(solution)/shard_map/all_gather | solution.py:193
  200.2 6.6 copy.64
  206.8 4.8 fusion.82
  212.8 9.1 all-gather.16.cloned.1.call-done
  221.9 76.1 %while.32 = (s32[]{:T(128)}, bf16[8,3,512,64]{2,3,1,0:T(8,128)(2,1)}, f32[8,3,512]{2,1,0:T(4,128)}, f32[8,3]{1,0:T(8,128)}, bf16[8,3,512,64]{2,3,1,0:T(8,128)(2,...) while((s32[]{:T(128)}, ...), condition=%wide.region_5.6_spmd.clone.clone, body=%wide.region_1.5_spmd.clone.sunk.clone | while | flops 419953152 | bytes 21889676 | solution.py:250
  227.4 2.7 fusion.162
  237.0 2.7 fusion.162
  256.0 2.7 fusion.162
  265.5 2.7 fusion.162
  275.0 2.7 fusion.162
  284.5 2.7 fusion.162
  294.1 2.7 fusion.162
  298.1 14.7 all-gather.22.cloned.1.call-done
  312.8 6.0 multiply_reduce_fusion.3
  321.5 140.3 %all-gather.1 = s32[1,8192,8]{2,1,0:T(8,128)} all-gather(s32[1,512,8]{2,1,0:T(8,128)S(1)} %copy.67), channel_id=3, replica_groups=mesh['dp'=2,'expert'=4,'shard'=4] {'expert','shard'}, dimensions={1}, use_global_device_ids=true | all-gather | bytes 278528 | tf_op jit(solution)/shard_map/all_gather | solution.py:188
  461.8 71.1 %all-gather.26.cloned.1.call-done = bf16[1,8192,1536]{2,1,0:T(8,128)(2,1)} async-done(((bf16[1,512,1536]{2,1,0:T(8,128)(2,1)}), bf16[1,8192,1536]{2,1,0:T(8,128)(2,1)}) %all-gather.26.cloned.1.call-update) | async-done | bytes 25165840 | tf_op jit(solution)/shard_map/all_gather | solution.py:187
  532.9 137.4 %all-gather.24.cloned.1.call-done.rows_ref = bf16[8192,1536]{1,0:T(8,128)(2,1)} async-done(((bf16[512,1536]{1,0:T(8,128)(2,1)}), bf16[8192,1536]{1,0:T(8,128)(2,1)}) %all-gather.24.cloned.1.call-update) | async-done | bytes 25165840 | tf_op jit(solution)/shard_map/all_gather | solution.py:268
  670.3 279.8 %shard_map.245 = (bf16[8192,1536]{1,0:T(8,128)(2,1)}, bf16[8192,1536]{1,0:T(8,128)(2,1)}, f32[8192,2]{1,0:T(8,128)}, bf16[2,1536,1024]{2,1,0:T(8,128)(2,1)}, bf16[2,512,1536]{2,1,0:T(8,128)(2,1)}) custom-call(s32[1]{0:T(128)} %bitcast.19.at_ref, s32[8192,8]{1,0:T(8,128)} %bitcast.248, bf16[1536,32]{1,0:T(8,128)(2,1)} %copy.68.router_ref, ...), custom_call_target="tpu_custom_call" | custom-call | tf_op jit(solution)/shard_map/pallas_call | solution.py:133
  950.8 3.5 copy.69
  954.2 4.7 all-to-all-start
  961.6 4.0 all-to-all-done
  965.7 228.3 %reduce-scatter.15.cloned.1.call-done = bf16[512,1536]{1,0:T(8,128)(2,1)} async-done(((bf16[8192,1536]{1,0:T(8,128)(2,1)}), bf16[512,1536]{1,0:T(8,128)(2,1)}) %reduce-scatter.15.cloned.1.call-update) | async-done | bytes 1572880 | tf_op jit(solution)/shard_map/reduce_scatter | solution.py:280
  1194.0 4.1 multiply_reduce_fusion.1
  1198.1 242.8 %reduce-scatter.13.cloned.1.call-done = bf16[512,1536]{1,0:T(8,128)(2,1)} async-done(((bf16[8192,1536]{1,0:T(8,128)(2,1)}), bf16[512,1536]{1,0:T(8,128)(2,1)}) %reduce-scatter.13.cloned.1.call-update) | async-done | bytes 1572880 | tf_op jit(solution)/shard_map/reduce_scatter | solution.py:283
  1440.9 5.0 convert_add_fusion
  1447.6 4.9 convolution_convert_fusion.4
  1453.3 119.9 %while.33 = (s32[]{:T(128)}, f32[8,3,512,64]{2,3,1,0:T(8,128)}, bf16[8,1024,64]{1,2,0:T(8,128)(2,1)}, bf16[8,1024,64]{1,2,0:T(8,128)(2,1)}, bf16[8,3,512,64]{2,3...) while((s32[]{:T(128)}, f32[8,3,512,64]{2,3,1,0:T(8,128)}, ...), condition=%wide.region_16.17_spmd.clone.clone, body=%wide.region_14.16_spmd.clone.sunk.clone | while | flops 1027078656 | bytes 51440760 | solution.py:341
  1456.5 3.0 multiply_reduce_fusion.6
  1461.2 2.7 fusion.173
  1471.5 3.0 multiply_reduce_fusion.6
  1476.2 2.7 fusion.173
  1486.4 3.0 multiply_reduce_fusion.6
  1491.1 2.7 fusion.173
  1501.4 3.0 multiply_reduce_fusion.6
  1506.1 2.8 fusion.173
  1516.4 3.0 multiply_reduce_fusion.6
  1521.1 2.7 fusion.173
  1531.4 3.0 multiply_reduce_fusion.6
  1536.1 2.7 fusion.173
  1546.4 3.0 multiply_reduce_fusion.6
  1551.1 2.8 fusion.173
  1561.4 3.0 multiply_reduce_fusion.6
  1566.1 2.7 fusion.173
  1576.4 4.7 convolution_convert_fusion
  1581.1 2.8 fusion.57
  1583.9 7.8 copy.77
  1595.8 4.6 convolution_convert_fusion.1
  1600.4 4.4 fusion.103
  1607.1 4.7 convolution_add_fusion.2
  1611.8 3.5 reduce-scatter.19.cloned.1.call-done
  1615.3 6.1 fusion.71
  1623.7 4.0 fusion.56
  1627.6 11.2 copy.75
  1639.7 40.0 %pmax.7 = f32[24]{0:T(128)S(1)} all-reduce(f32[24]{0:T(128)S(1)} %reshape.304), channel_id=1, replica_groups=mesh['dp'=2,'expert'=4,'shard'=4] {'dp','expert','shard'}, use_global_device_ids=true, to_apply=%region_26.27 | all-reduce | flops 24 | bytes 192 | tf_op jit(solution)/shard_map/pmax | solution.py:251
  1682.3 3.5 convert_element_type.213
  1685.8 56.9 %reduce-scatter.21.cloned.1.call-done = bf16[2,768,1024]{2,1,0:T(8,128)(2,1)} async-done(((bf16[2,1536,1024]{2,1,0:T(8,128)(2,1)}), bf16[2,768,1024]{2,1,0:T(8,128)(2,1)}) %reduce-scatter.21.cloned.1.call-update) | async-done | bytes 3145744 | tf_op jit(solution)/shard_map/reduce_scatter | solution.py:286
  1742.7 5.5 convert_element_type.212
  1750.3 106.8 %reduce-scatter.27.cloned.1.call-done = bf16[48,1664]{1,0:T(8,128)(2,1)} async-done(((bf16[1536,1664]{1,0:T(8,128)(2,1)}), bf16[48,1664]{1,0:T(8,128)(2,1)}) %reduce-scatter.27.cloned.1.call-update) | async-done | bytes 159760
  1860.5 132.7 %reduce-scatter.25.cloned.1.call-done = bf16[48,2688]{1,0:T(8,128)(2,1)} async-done(((bf16[1536,2688]{1,0:T(8,128)(2,1)}), bf16[48,2688]{1,0:T(8,128)(2,1)}) %reduce-scatter.25.cloned.1.call-update) | async-done | bytes 258064
  (259 shorter events, 179.9 us)
Async XLA Ops:
  7.2 42.2 %all-gather.18.cloned.1.call-start = ((), (), s32[]{:S(2)}) async-start(), calls=%async_computation.12 | async-start | bytes 1966080 | tf_op jit(solution)/shard_map/all_gather | solution.py:195
  7.9 79.1 %all-gather.14.cloned.1.call-start = ((), (), s32[]{:S(2)}) async-start(), calls=%async_computation.10 | async-start | bytes 1966080 | tf_op jit(solution)/shard_map/all_gather | solution.py:194
  8.7 100.6 %all-gather.20.cloned.1.call-start = ((), (), s32[]{:S(2)}) async-start(), calls=%async_computation.13 | async-start | bytes 1572864 | tf_op jit(solution)/shard_map/all_gather | solution.py:220
  10.5 196.3 %copy-start.25 = (f32[512]{0:T(512)}, f32[512]{0:T(512)S(1)}, u32[]{:S(2)}) copy-start(f32[512]{0:T(512)S(1)} %add_rsqrt_fusion.1) | copy-start | bytes 6148
  53.1 36.4 %copy-start.1 = (bf16[1,512,1536]{2,1,0:T(8,128)(2,1)S(1)}, bf16[1,512,1536]{2,1,0:T(8,128)(2,1)}, u32[]{:S(2)}) copy-start(bf16[1,512,1536]{2,1,0:T(8,128)(2,1)} %param.18) | copy-start | bytes 4718596
  53.1 36.4 %copy-start.23 = (f32[1536]{0:T(1024)S(1)}, f32[1536]{0:T(1024)}, u32[]{:S(2)}) copy-start(f32[1536]{0:T(1024)} %param.20) | copy-start | bytes 18436
  53.2 147.0 %all-gather.12.cloned.1.call-start = ((), (), s32[]{:S(2)}) async-start(), calls=%async_computation.9 | async-start | bytes 5898240 | tf_op jit(solution)/shard_map/all_gather | solution.py:193
  53.7 168.2 %all-gather.16.cloned.1.call-start = ((), (), s32[]{:S(2)}) async-start(), calls=%async_computation.11 | async-start | bytes 1572864 | tf_op jit(solution)/shard_map/all_gather | solution.py:219
  54.8 156.9 %copy-start.13 = (f32[512,32]{0,1:T(8,128)}, f32[512,32]{0,1:T(8,128)S(1)}, u32[]{:S(2)}) copy-start(f32[512,32]{0,1:T(8,128)S(1)} %get-tuple-element.308) | copy-start | bytes 196612
  92.0 2.4 copy-start.20
  93.1 219.7 %all-gather.22.cloned.1.call-start = ((), (), s32[]{:S(2)}) async-start(), calls=%async_computation.14 | async-start | bytes 5898240 | tf_op jit(solution)/shard_map/all_gather | solution.py:196
  93.7 439.3 %all-gather.26.cloned.1.call-start = ((), (), s32[]{:S(2)}) async-start(), calls=%async_computation.22 | async-start | bytes 26738688 | tf_op jit(solution)/shard_map/all_gather | solution.py:187
  94.4 575.9 %all-gather.24.cloned.1.call-start = ((), (), s32[]{:S(2)}) async-start(), calls=%async_computation.15 | async-start | bytes 26738688 | tf_op jit(solution)/shard_map/all_gather | solution.py:268
  298.1 14.7 copy-start.3
  298.1 14.7 copy-start.10
  312.8 6.1 copy-start.21
  318.9 1.6 copy-start.22
  318.9 1.7 copy-start.17
  320.4 873.6 %reduce-scatter.15.cloned.1.call-start = ((), (), s32[]{:S(2)}) async-start(), calls=%async_computation.17 | async-start | bytes 26738688 | tf_op jit(solution)/shard_map/reduce_scatter | solution.py:280
  950.1 490.8 %reduce-scatter.13.cloned.1.call-start = ((), (), s32[]{:S(2)}) async-start(), calls=%async_computation.16 | async-start | bytes 26738688 | tf_op jit(solution)/shard_map/reduce_scatter | solution.py:283
  954.2 11.3 all-to-all-start
  958.9 645.8 %reduce-scatter.17.cloned.1.call-start = ((), (), s32[]{:S(2)}) async-start(), calls=%async_computation.18 | async-start | bytes 1572864 | tf_op jit(solution)/shard_map/reduce_scatter | solution.py:351
  1446.0 1.7 copy-start.4
  1573.2 42.1 %reduce-scatter.19.cloned.1.call-start = ((), (), s32[]{:S(2)}) async-start(), calls=%async_computation.19 | async-start | bytes 1572864 | tf_op jit(solution)/shard_map/reduce_scatter | solution.py:354
  1573.8 108.6 %reduce-scatter.23.cloned.1.call-start = ((), (), s32[]{:S(2)}) async-start(), calls=%async_computation.21 | async-start | bytes 4718592 | tf_op jit(solution)/shard_map/reduce_scatter | solution.py:287
  1574.5 168.2 %reduce-scatter.21.cloned.1.call-start = ((), (), s32[]{:S(2)}) async-start(), calls=%async_computation.20 | async-start | bytes 9437184 | tf_op jit(solution)/shard_map/reduce_scatter | solution.py:286
  1574.5 1.4 copy-start
  1574.6 1.9 copy-start.15
  1575.1 282.0 %reduce-scatter.27.cloned.1.call-start = ((), (), s32[]{:S(2)}) async-start(), calls=%async_computation.24 | async-start | bytes 5271552
  1591.7 1.9 copy-start.9
  1591.7 1.9 copy-start.14
  1591.7 1.9 copy-start.18
  1591.7 401.5 %reduce-scatter.25.cloned.1.call-start = ((), (), s32[]{:S(2)}) async-start(), calls=%async_computation.23 | async-start | bytes 8515584
  1593.6 6.7 slice-start.2
  1594.1 1.6 copy-start.2
  1594.1 1.6 copy-start.24
  1594.1 1.6 copy-start.26
  1595.8 4.6 slice-start.3
  1604.8 2.3 copy-start.7
  1606.3 0.8 copy-start.11
  1611.8 9.6 copy-start.12
  1615.3 8.3 slice-start
  1621.4 1.1 copy-start.19
  1621.4 2.3 slice-start.1
  1638.8 0.8 copy-start.27
  1638.8 41.4 %copy-start.16 = (bf16[384,512]{1,0:T(8,128)(2,1)S(1)}, bf16[384,512]{1,0:T(8,128)(2,1)}, u32[]{:S(2)}) copy-start(bf16[384,512]{1,0:T(8,128)(2,1)} %param.22) | copy-start | bytes 1179652
  1638.8 42.3 %copy-start.8 = (bf16[384,1536]{1,0:T(8,128)(2,1)S(1)}, bf16[384,1536]{1,0:T(8,128)(2,1)}, u32[]{:S(2)}) copy-start(bf16[384,1536]{1,0:T(8,128)(2,1)} %param.21) | copy-start | bytes 3538948
  1679.8 6.1 copy-start.28
  1742.7 5.5 copy-start.5
  1742.7 5.5 copy-start.6
Sparse Core Ops, SparseCore 0:
  9.6 39.7 all-gather.17
  51.0 35.9 all-gather.13
  89.1 20.1 all-gather.19
  110.7 89.4 all-gather.11
  202.1 19.7 all-gather.15
  223.4 89.4 all-gather.21
  314.4 218.5 all-gather.25
  534.5 135.7 all-gather.23
  950.2 243.7 reduce-scatter.14
  1198.0 242.9 reduce-scatter.12
  1573.3 19.3 reduce-scatter.16
  1594.9 20.3 reduce-scatter.18
  1618.1 44.0 reduce-scatter.22
  1665.0 77.6 reduce-scatter.20
  1748.1 108.9 reduce-scatter.26
  1863.9 129.3 reduce-scatter.24

commit v2 on v1

--- a/solution.py
+++ b/solution.py
@@ -70,98 +70,385 @@
 
 
 def experts_kernel(
-    at_ref, routes_ref, router_ref, rows_ref, cot_ref, win_ref, wout_ref,
-    out_ref, grad_ref, gates_ref, dwin_ref, dwout_ref, acc_in, acc_out,
+    hidden_ref, cot_ref, routes_ref, router_ref, win_ref, wout_ref,
+    rows_ref, kept_ref, core_ref, across_ref, line_ref, stage_ref, dwin_ref, dwout_ref,
+    acc_in, acc_out, win, wout, router, row_tile, cot_tile, route_tile, made, parts,
+    load_sem, tile_sem, row_recv, core_send, across_send, line_send,
+    made_sem, part_sem, core_recv, across_recv, line_recv, stage_sem, stage_send, store_sem,
 ):
-    step, steps = pl.program_id(0), pl.num_programs(0)
     own_count, width = wout_ref.shape[0], wout_ref.shape[1]
-
-    @pl.when(step == 0)
-    def _():
-        acc_in[...] = jnp.zeros_like(acc_in)
-        acc_out[...] = jnp.zeros_like(acc_out)
-
-    rows, cot = rows_ref[...], cot_ref[...]
-    logits = jnp.dot(rows, router_ref[...], preferred_element_type=jnp.float32)
-    lanes = lax.broadcasted_iota(jnp.int32, logits.shape, 1)
-    picked = lanes == routes_ref[:, 0:1]
-    for k in range(1, TOP):
-        picked = picked | (lanes == routes_ref[:, k : k + 1])
-    gates = masked_softmax(logits, picked)
-    first = at_ref[0] * own_count
-    out_sum = grad_sum = None
-    gate_lanes = lax.broadcasted_iota(jnp.int32, gates_ref.shape, 1)
-    gate_grads = jnp.zeros(gates_ref.shape, jnp.float32)
-    for e in range(own_count):
-        gate = jnp.sum(jnp.where(lanes == first + e, gates, 0.0), axis=1, keepdims=True)
-        both = jnp.dot(rows, win_ref[e], preferred_element_type=jnp.float32)
-        gate_part, up_part = both[:, :width], both[:, width:]
-        sig = jax.nn.sigmoid(gate_part)
-        activated = gate_part * sig
-        hidden = (activated * up_part).astype(jnp.bfloat16).astype(jnp.float32)
-        gated = (gate * hidden).astype(jnp.bfloat16)
-        term = jnp.dot(gated, wout_ref[e], preferred_element_type=jnp.float32)
-        out_sum = term if out_sum is None else out_sum + term
-        plain = contract_cols(cot, wout_ref[e])
-        own_grad = jnp.sum(plain * hidden, axis=1, keepdims=True)
-        gate_grads = jnp.where(gate_lanes == e, own_grad, gate_grads)
-        back = gate * plain
-        d_gate = back * up_part * sig * (1.0 + gate_part * (1.0 - sig))
-        d_up = back * activated
-        d_both = jnp.concatenate([d_gate, d_up], axis=1).astype(jnp.bfloat16)
-        term = contract_cols(d_both, win_ref[e])
-        grad_sum = term if grad_sum is None else grad_sum + term
-        acc_in[e] += contract_rows(rows, d_both)
-        acc_out[e] += contract_rows(gated, cot)
-    out_ref[...] = out_sum.astype(jnp.bfloat16)
-    grad_ref[...] = grad_sum.astype(jnp.bfloat16)
-    gates_ref[...] = gate_grads
-
-    @pl.when(step == steps - 1)
-    def _():
-        dwin_ref[...] = acc_in[...].astype(jnp.bfloat16)
-        dwout_ref[...] = acc_out[...].astype(jnp.bfloat16)
-
-
-def experts_pass(group_at, routes, w_router, rows, cotangent, expert_in, expert_out):
-    total, model = rows.shape
-    tile = 256
-    by_row = lambda width: pl.BlockSpec((tile, width), lambda i: (i, 0))
-    whole = lambda shape: pl.BlockSpec(
-        shape, lambda i: (0,) * len(shape), pipeline_mode=pl.Buffered(1)
-    )
-    return pl.pallas_call(
+    rows_own, model = hidden_ref.shape
+    tile = rows_own // 2
+    expert, depth = lax.axis_index("expert"), lax.axis_index("shard")
+    side, core = expert // 2, expert % 2
+    sibling = {"expert": 2 * side + (core + 1) % 2}
+    opposite = {"expert": 2 * ((side + 1) % 2) + core}
+
+    def along(distance):
+        return {"shard": (depth + distance) % 4}
+
+    def remote(src, dst, send, recv, to):
+        return pltpu.make_async_remote_copy(
+            src_ref=src, dst_ref=dst, send_sem=send, recv_sem=recv, device_id=to,
+            device_id_type=pl.DeviceIdType.MESH,
+        )
+
+    barrier = pltpu.get_barrier_semaphore()
+    for peer in (sibling, opposite, along(1), along(2), along(3)):
+        pl.semaphore_signal(barrier, inc=1, device_id=peer, device_id_type=pl.DeviceIdType.MESH)
+    pl.semaphore_wait(barrier, 5)
+
+    loads = [
+        pltpu.make_async_copy(win_ref, win, load_sem.at[0]),
+        pltpu.make_async_copy(wout_ref, wout, load_sem.at[1]),
+        pltpu.make_async_copy(router_ref, router, load_sem.at[2]),
+    ]
+
+    def to_sibling(src, r):
+        return remote(src, rows_ref.at[r + 1], core_send.at[r // 2], row_recv.at[r + 1], sibling)
+
+    def to_opposite(src, r):
+        return remote(src, rows_ref.at[r + 2], across_send.at[r // 4], row_recv.at[r + 2], opposite)
+
+    def to_line(zi):
+        return remote(
+            hidden_ref, rows_ref.at[4 * zi], line_send.at[zi], row_recv.at[4 * zi], along(4 - zi)
+        )
+
+    def own_rows():
+        return pltpu.make_async_copy(hidden_ref, rows_ref.at[0], row_recv.at[0])
+
+    to_sibling(hidden_ref, 0).start()
+    to_opposite(hidden_ref, 0).start()
+    for zi in range(1, 4):
+        to_line(zi).start()
+    own_rows().start()
+    for load in loads:
+        load.start()
+
+    def arrive(r):
+        @pl.when(r == 0)
+        def _():
+            own_rows().wait()
+
+        @pl.when(r > 0)
+        def _():
+            remote(
+                rows_ref.at[r], rows_ref.at[r], core_send.at[0], row_recv.at[r], sibling
+            ).wait_recv()
+
+            @pl.when(r % 2 == 0)
+            def _():
+                to_sibling(rows_ref.at[r], r).start()
+
+            @pl.when(r % 4 == 0)
+            def _():
+                to_opposite(rows_ref.at[r], r).start()
+
+    def block_at(step):
+        turn = (step // 2 + 1) // 2
+        place = (turn + 7) % 8
+        return 4 * ((place + place // 4) % 4) + 2 * (1 - place // 4) + (step // 2 + 1) % 2
+
+    def tiles(step):
+        r, sub, slot = block_at(step), step % 2, step % 2
+        other = 2 * ((side + (r % 4) // 2) % 2) + (core + r) % 2
+        start = (other * 4 + (depth + r // 4) % 4) * rows_own + sub * tile
+        start = pl.multiple_of(start, tile)
+        return (
+            pltpu.make_async_copy(
+                rows_ref.at[r, pl.ds(pl.multiple_of(sub * tile, tile), tile)],
+                row_tile.at[slot], tile_sem.at[0, slot],
+            ),
+            pltpu.make_async_copy(
+                cot_ref.at[pl.ds(start, tile)], cot_tile.at[slot], tile_sem.at[1, slot]
+            ),
+            pltpu.make_async_copy(
+                routes_ref.at[pl.ds(start, tile)], route_tile.at[slot], tile_sem.at[2, slot]
+            ),
+        )
+
+    acc_in[...] = jnp.zeros_like(acc_in)
+    acc_out[...] = jnp.zeros_like(acc_out)
+    arrive(1)
+    for copy in tiles(0):
+        copy.start()
+    for load in loads:
+        load.wait()
+
+    def send_made(step):
+        r, sub, slot = block_at(step), step % 2, step % 2
+        return remote(
+            made.at[slot], core_ref.at[r // 2, sub], made_sem.at[slot],
+            core_recv.at[r // 2, sub], sibling,
+        )
+
+    def keep_made(step):
+        r, sub, slot = block_at(step), step % 2, step % 2
+        return pltpu.make_async_copy(made.at[slot], kept_ref.at[r // 2, sub], made_sem.at[slot])
+
+    def made_done(step):
+        away = (step // 2 + 1) % 2
+
+        @pl.when(away == 1)
+        def _():
+            send_made(step).wait_send()
+
+        @pl.when(away == 0)
+        def _():
+            keep_made(step).wait()
+
+    def send_y(zi, sub):
+        return remote(
+            stage_ref.at[zi, sub], across_ref.at[zi, sub], stage_send.at[zi, sub],
+            across_recv.at[zi, sub], opposite,
+        )
+
+    def send_z(zi, sub):
+        return remote(
+            stage_ref.at[3 + zi, sub], line_ref.at[zi, sub], stage_send.at[3 + zi, sub],
+            line_recv.at[zi, sub], along(zi),
+        )
+
+    def staged(place, sub):
+        return pltpu.make_async_copy(parts.at[0], stage_ref.at[place, sub], stage_sem.at[0])
+
+    def load_kept(pair, sub):
+        return pltpu.make_async_copy(kept_ref.at[pair, sub], parts.at[0], part_sem.at[0])
+
+    def load_core(pair, sub):
+        return pltpu.make_async_copy(core_ref.at[pair, sub], parts.at[1], part_sem.at[1])
+
+    def load_across(zi, sub):
+        return pltpu.make_async_copy(across_ref.at[zi, sub], parts.at[2], part_sem.at[2])
+
+    def core_arrived(pair, sub):
+        remote(
+            made.at[0], core_ref.at[pair, sub], made_sem.at[0], core_recv.at[pair, sub], sibling
+        ).wait_recv()
+
+    def begin_y(zi, sub):
+        core_arrived(2 * zi + 1, sub)
+        load_kept(2 * zi + 1, sub).start()
+        load_core(2 * zi + 1, sub).start()
+
+    def end_y(zi, sub):
+        load_kept(2 * zi + 1, sub).wait()
+        load_core(2 * zi + 1, sub).wait()
+        parts[0] = (parts[0].astype(jnp.float32) + parts[1].astype(jnp.float32)).astype(
+            jnp.bfloat16
+        )
+        staged(zi, sub).start()
+
+    def begin_z(zi, sub):
+        core_arrived(2 * zi, sub)
+        send_y(zi, sub).wait_recv()
+        load_kept(2 * zi, sub).start()
+        load_core(2 * zi, sub).start()
+        load_across(zi, sub).start()
+
+    def end_z(zi, sub):
+        load_kept(2 * zi, sub).wait()
+        load_core(2 * zi, sub).wait()
+        load_across(zi, sub).wait()
+        parts[0] = (
+            parts[0].astype(jnp.float32) + parts[1].astype(jnp.float32) + parts[2].astype(jnp.float32)
+        ).astype(jnp.bfloat16)
+        staged(3 + zi, sub).start()
+
+    first = (expert * 4 + depth) * own_count
+
+    def body(step, carry):
+        slot, sub = step % 2, step % 2
+        stage_y = (step >= 10) & (step < 24) & (step % 4 >= 2)
+        zi_y = (step // 4 - 1) % 4
+        stage_z = (step == 24) | (step == 25) | (step >= 30)
+        zi_z = 1 + (step - 24) // 6
+        for copy in tiles(step):
+            copy.wait()
+
+        @pl.when(step < 31)
+        def _():
+            after = block_at(step + 1)
+
+            @pl.when((step % 2 == 1) & ((after % 4 != 0) | (after == 0)))
+            def _():
+                arrive(after)
+
+            for early, r in ((2, 4), (6, 8), (10, 12)):
+                @pl.when(step == early)
+                def _():
+                    arrive(jnp.int32(r))
+
+            for copy in tiles(step + 1):
+                copy.start()
+
+        before_y = (step >= 11) & (step < 25) & ((step - 1) % 4 >= 2)
+        before_z = (step == 25) | (step == 26) | (step == 31)
+
+        @pl.when(before_y)
+        def _():
+            zi = ((step - 1) // 4 - 1) % 4
+            staged(zi, 1 - sub).wait()
+            send_y(zi, 1 - sub).start()
+
+        @pl.when(before_z)
+        def _():
+            zi = 1 + (step - 25) // 6
+            staged(3 + zi, 1 - sub).wait()
+            send_z(zi, 1 - sub).start()
+
+        @pl.when(stage_y)
+        def _():
+            begin_y(zi_y, sub)
+
+        @pl.when(stage_z)
+        def _():
+            begin_z(zi_z, sub)
+
+        @pl.when(step >= 2)
+        def _():
+            made_done(step - 2)
+
+        rows, cot = row_tile[slot], cot_tile[slot]
+        logits = jnp.dot(rows, router[...], preferred_element_type=jnp.float32)
+        lanes = lax.broadcasted_iota(jnp.int32, logits.shape, 1)
+        routes = route_tile[slot]
+        picked = lanes == routes[:, 0:1]
+        for k in range(1, TOP):
+            picked = picked | (lanes == routes[:, k : k + 1])
+        gates = masked_softmax(logits, picked)
+        out_sum = grad_sum = None
+        gate_lanes = lax.broadcasted_iota(jnp.int32, (tile, 128), 1)
+        gate_grads = jnp.zeros((tile, 128), jnp.float32)
+        for e in range(own_count):
+            gate = jnp.sum(jnp.where(lanes == first + e, gates, 0.0), axis=1, keepdims=True)
+            both = jnp.dot(rows, win[e], preferred_element_type=jnp.float32)
+            gate_part, up_part = both[:, :width], both[:, width:]
+            sig = jax.nn.sigmoid(gate_part)
+            activated = gate_part * sig
+            hidden = (activated * up_part).astype(jnp.bfloat16).astype(jnp.float32)
+            gated = (gate * hidden).astype(jnp.bfloat16)
+            term = jnp.dot(gated, wout[e], preferred_element_type=jnp.float32)
+            out_sum = term if out_sum is None else out_sum + term
+            plain = contract_cols(cot, wout[e])
+            own_grad = jnp.sum(plain * hidden, axis=1, keepdims=True)
+            high = own_grad.astype(jnp.bfloat16).astype(jnp.float32)
+            gate_grads = jnp.where(gate_lanes == first + e, high, gate_grads)
+            gate_grads = jnp.where(gate_lanes == 64 + first + e, own_grad - high, gate_grads)
+            back = gate * plain
+            d_gate = back * up_part * sig * (1.0 + gate_part * (1.0 - sig))
+            d_up = back * activated
+            d_both = jnp.concatenate([d_gate, d_up], axis=1).astype(jnp.bfloat16)
+            term = contract_cols(d_both, win[e])
+            grad_sum = term if grad_sum is None else grad_sum + term
+            acc_in[e] += contract_rows(rows, d_both)
+            acc_out[e] += contract_rows(gated, cot)
+        made[slot, :, :model] = grad_sum.astype(jnp.bfloat16)
+        made[slot, :, model : 2 * model] = out_sum.astype(jnp.bfloat16)
+        made[slot, :, 2 * model :] = gate_grads.astype(jnp.bfloat16)
+
+        away = (step // 2 + 1) % 2
+
+        @pl.when(away == 1)
+        def _():
+            send_made(step).start()
+
+        @pl.when(away == 0)
+        def _():
+            keep_made(step).start()
+
+        @pl.when(stage_y)
+        def _():
+            end_y(zi_y, sub)
+
+        @pl.when(stage_z)
+        def _():
+            end_z(zi_z, sub)
+
+        return carry
+
+    lax.fori_loop(0, 32, body, 0)
+    stores = [
+        pltpu.make_async_copy(acc_in, dwin_ref, store_sem.at[0]),
+        pltpu.make_async_copy(acc_out, dwout_ref, store_sem.at[1]),
+    ]
+    for store in stores:
+        store.start()
+    staged(5, 1).wait()
+    send_z(2, 1).start()
+    for sub in range(2):
+        begin_z(3, sub)
+        end_z(3, sub)
+        staged(6, sub).wait()
+        send_z(3, sub).start()
+    made_done(30)
+    made_done(31)
+    for sub in range(2):
+        core_arrived(0, sub)
+        send_y(0, sub).wait_recv()
+        for zi in range(4):
+            send_y(zi, sub).wait_send()
+        for zi in range(1, 4):
+            send_z(zi, sub).wait_send()
+            send_z(zi, sub).wait_recv()
+    for r in range(0, 16, 2):
+        to_sibling(hidden_ref, r).wait_send()
+    for r in range(0, 16, 4):
+        to_opposite(hidden_ref, r).wait_send()
+    for zi in range(1, 4):
+        to_line(zi).wait_send()
+    for store in stores:
+        store.wait()
+
+
+def experts_pass(hidden, cotangent, routes, w_router, expert_in, expert_out):
+    rows_own, model = hidden.shape
+    tile = rows_own // 2
+    wide = 2 * model + 128
+    anywhere = pl.BlockSpec(memory_space=pl.ANY)
+    low = jnp.bfloat16
+    kept = jax.ShapeDtypeStruct((8, 2, tile, wide), low)
+    quarter = jax.ShapeDtypeStruct((4, 2, tile, wide), low)
+    dma = pltpu.SemaphoreType.DMA
+    results = pl.pallas_call(
         experts_kernel,
-        grid=(total // tile,),
         out_shape=(
-            jax.ShapeDtypeStruct((total, model), jnp.bfloat16),
-            jax.ShapeDtypeStruct((total, model), jnp.bfloat16),
-            jax.ShapeDtypeStruct((total, expert_in.shape[0]), jnp.float32),
-            jax.ShapeDtypeStruct(expert_in.shape, jnp.bfloat16),
-            jax.ShapeDtypeStruct(expert_out.shape, jnp.bfloat16),
+            jax.ShapeDtypeStruct((16, rows_own, model), low),
+            kept,
+            kept,
+            quarter,
+            quarter,
+            jax.ShapeDtypeStruct((7, 2, tile, wide), low),
+            jax.ShapeDtypeStruct(expert_in.shape, jnp.float32),
+            jax.ShapeDtypeStruct(expert_out.shape, jnp.float32),
         ),
-        in_specs=[
-            pl.BlockSpec(memory_space=pltpu.SMEM),
-            by_row(routes.shape[1]),
-            whole(w_router.shape),
-            by_row(model),
-            by_row(model),
-            whole(expert_in.shape),
-            whole(expert_out.shape),
-        ],
-        out_specs=(
-            by_row(model),
-            by_row(model),
-            by_row(expert_in.shape[0]),
-            whole(expert_in.shape),
-            whole(expert_out.shape),
-        ),
+        in_specs=[anywhere] * 6,
+        out_specs=(anywhere,) * 8,
         scratch_shapes=[
             pltpu.VMEM(expert_in.shape, jnp.float32),
             pltpu.VMEM(expert_out.shape, jnp.float32),
+            pltpu.VMEM(expert_in.shape, low),
+            pltpu.VMEM(expert_out.shape, low),
+            pltpu.VMEM(w_router.shape, low),
+            pltpu.VMEM((2, tile, model), low),
+            pltpu.VMEM((2, tile, model), low),
+            pltpu.VMEM((2, tile, routes.shape[1]), jnp.int32),
+            pltpu.VMEM((2, tile, wide), low),
+            pltpu.VMEM((3, tile, wide), low),
+            dma((3,)), dma((3, 2)), dma((16,)), dma((8,)), dma((4,)), dma((4,)),
+            dma((2,)), dma((3,)), dma((8, 2)), dma((4, 2)), dma((4, 2)), dma((1,)), dma((7, 2)), dma((2,)),
         ],
-        compiler_params=pltpu.CompilerParams(vmem_limit_bytes=60 * 2**20),
-    )(group_at[None].astype(jnp.int32), routes, w_router, rows, cotangent, expert_in, expert_out)
+        compiler_params=pltpu.CompilerParams(
+            collective_id=0, has_side_effects=True, vmem_limit_bytes=60 * 2**20
+        ),
+    )(hidden, cotangent, routes, w_router, expert_in, expert_out)
+    _, kept, core, across, line, _, weight_in_grad, weight_out_grad = results
+    total = kept[0].astype(jnp.float32) + core[0].astype(jnp.float32)
+    total = total + across[0].astype(jnp.float32)
+    for zi in range(1, 4):
+        total = total + line[zi].astype(jnp.float32)
+    return total.reshape(rows_own, wide), weight_in_grad, weight_out_grad
 
 
 def on_device(
@@ -265,28 +552,21 @@
     picked = (route_ids[:, :, None] == jnp.arange(expert_count)[None, None, :]).any(axis=1)
     gate_weights = masked_softmax(router_logits, picked)
     grad_out = cotangent[0].astype(jnp.float32)
-    all_hidden = lax.all_gather(hidden_ffn, GROUP, axis=0, tiled=True)
-    group_at = lax.axis_index("expert") * lax.axis_size("shard") + lax.axis_index("shard")
-    partial_out, partial_grad, grad_gates_own, weight_in_grad, weight_out_grad = experts_pass(
-        group_at, all_routes, w_router, all_hidden, all_cotangent, expert_in, expert_out
-    )
-    grad_gates = (
-        lax.all_to_all(
-            grad_gates_own.reshape(-1, token_matrix, expert_in.shape[0]), GROUP, 0, 0, tiled=True
-        )
-        .transpose(1, 0, 2)
-        .reshape(token_matrix, expert_count)
-    )
-    grad_hidden_ffn = lax.psum_scatter(
-        partial_grad, GROUP, scatter_dimension=0, tiled=True
-    ).astype(jnp.float32)
-    branch_ffn = lax.psum_scatter(partial_out, GROUP, scatter_dimension=0, tiled=True)
-    out = (residual + branch_ffn.astype(jnp.float32)).astype(jnp.bfloat16)
+    summed, weight_in_grad, weight_out_grad = experts_pass(
+        hidden_ffn, all_cotangent, all_routes, w_router, expert_in, expert_out
+    )
+    model = hidden_ffn.shape[1]
+    grad_hidden_ffn = summed[:, :model]
+    out = (residual + summed[:, model : 2 * model]).astype(jnp.bfloat16)
+    gate_cols = summed[:, 2 * model :]
+    grad_gates = gate_cols[:, :expert_count] + gate_cols[:, 64 : 64 + expert_count]
     grad_in_shard, grad_out_shard = (
-        lax.psum_scatter(weight_in_grad, "dp", scatter_dimension=1, tiled=True).astype(jnp.float32),
-        lax.psum_scatter(weight_out_grad, "dp", scatter_dimension=1, tiled=True).astype(
-            jnp.float32
-        ),
+        lax.psum_scatter(
+            weight_in_grad.astype(jnp.bfloat16), "dp", scatter_dimension=1, tiled=True
+        ).astype(jnp.float32),
+        lax.psum_scatter(
+            weight_out_grad.astype(jnp.bfloat16), "dp", scatter_dimension=1, tiled=True
+        ).astype(jnp.float32),
     )
     weighted = gate_weights * jnp.where(picked, grad_gates, 0.0)
     grad_logits = (

time: 2010 us -> 1690 us (0.84)
  waiting for transfers between devices: 1180 us -> 558 us
  Pallas kernels: 280 us -> 543 us
  blocking collectives: 185 us -> 220 us
  other arithmetic: 80.2 us -> 101 us
    reduce_scatter x4 -> x2, waiting for transfers between devices: 528 us -> 75.6 us  [the longest x1 75.6 us: on_device(): lax.psum_scatter(weight_in_grad.astype(jnp.bfloat16), 'dp', scatter_dimen...]
    pallas_call x1, Pallas kernels: 280 us -> 543 us  [experts_pass(): pl.pallas_call(experts_kernel, out_shape=(jax.ShapeDtypeStruct((16, rows_...]
    all_gather x1 -> x0, waiting for transfers between devices: 137 us -> none  [on_device(): all_hidden = lax.all_gather(hidden_ffn, GROUP, axis=0, tiled=True)]
    all_gather x1, waiting for transfers between devices: 89.4 us -> 0.02 us  [on_device(): lax.all_gather(w_query, 'shard', axis=0, tiled=True)]
    all_gather x1, waiting for transfers between devices: 71.1 us -> 127 us  [on_device(): all_cotangent = lax.all_gather(cotangent[0], GROUP, axis=0, tiled=True)]
    reduce_scatter x1, waiting for transfers between devices: 0.01 us -> 37.5 us  [on_device(): lax.psum_scatter(complete_key_gradient.astype(jnp.bfloat16), 'dp', scatte...]
    unnamed x18 -> x15, waiting for transfers between devices: 245 us -> 214 us
    all_gather x1, blocking collectives: 140 us -> 168 us  [on_device(): all_routes = lax.all_gather(routes[0], GROUP, axis=0, tiled=True)]
  transfers between devices with their start and end apart: 17 -> 13, of which waited for: 15 -> 10; matrix products, arithmetic and copies ran while one was open for 10% -> 12% of each run, Pallas kernels for 0% -> 0%
where the time goes in v2:
time: 1690 us
  waiting for transfers between devices  558 us (33%)
  Pallas kernels  543 us (32%)
  blocking collectives  220 us (13%)
  matrix products  184 us (11%)
  other arithmetic  101 us (6%)
  local copies, waits for them, and re-layouts  64.6 us (4%)
    pallas_call x1, Pallas kernels, experts_pass(): pl.pallas_call(experts_kernel, out_shape=(jax.ShapeDtypeStruct((16, rows_...  543 us
    unnamed x15, waiting for transfers between devices  214 us
    all_gather x1, blocking collectives, on_device(): all_routes = lax.all_gather(routes[0], GROUP, axis=0, tiled=True)  168 us
    all_gather x1, waiting for transfers between devices, on_device(): all_cotangent = lax.all_gather(cotangent[0], GROUP, axis=0, tiled=True)  127 us
    reduce_scatter x1, waiting for transfers between devices, on_device(): lax.psum_scatter(weight_in_grad.astype(jnp.bfloat16), 'dp', scatter_dimen...  75.6 us
    pmax x1, blocking collectives, on_device(): largest = lax.pmax(head_max.reshape(QUERY_HEADS), ('dp', 'expert', 'shard'))  47.8 us
    all_gather x1, waiting for transfers between devices, on_device(): lax.all_gather(value_weight, 'shard', axis=0, tiled=True)  38.9 us
    reduce_scatter x1, waiting for transfers between devices, on_device(): lax.psum_scatter(complete_key_gradient.astype(jnp.bfloat16), 'dp', scatte...  37.5 us
  transfers between devices with their start and end apart: 13, of which 10 were waited for; matrix products, arithmetic and copies ran while one was open for 12% of the time, Pallas kernels for 0%

profile of v2, /device:TPU:0, one launch (start us, length us, event | category | flops | bytes accessed | tf_op | source)
XLA Modules:
  0.0 1685.7 jit_solution(3456894109510307171)
XLA Ops:
  10.5 38.9 %all-gather.17.cloned.1.call-done = bf16[1536,512]{1,0:T(8,128)(2,1)} async-done(((bf16[384,512]{1,0:T(8,128)(2,1)}), bf16[1536,512]{1,0:T(8,128)(2,1)}) %all-gather.17.cloned.1.call-update) | async-done | bytes 1572880 | tf_op jit(solution)/shard_map/all_gather | solution.py:482
  49.4 3.7 convolution_convert_fusion.6
  54.8 32.2 %all-gather.13.cloned.1.call-done = bf16[1536,512]{1,0:T(8,128)(2,1)} async-done(((bf16[384,512]{1,0:T(8,128)(2,1)}), bf16[1536,512]{1,0:T(8,128)(2,1)}) %all-gather.13.cloned.1.call-update) | async-done | bytes 1572880 | tf_op jit(solution)/shard_map/all_gather | solution.py:481
  87.0 2.6 copy.65
  89.5 2.5 fusion.81
  95.8 4.4 all-gather
  100.2 167.7 %all-gather.2 = s32[1,8192,8]{2,1,0:T(8,128)} all-gather(s32[1,512,8]{2,1,0:T(8,128)S(1)} %copy.67), channel_id=4, replica_groups=mesh['dp'=2,'expert'=4,'shard'=4] {'expert','shard'}, dimensions={1}, use_global_device_ids=true | all-gather | bytes 278528 | tf_op jit(solution)/shard_map/all_gather | solution.py:475
  270.8 6.7 copy.64
  277.5 4.7 fusion.83
  284.5 76.1 %while.32 = (s32[]{:T(128)}, bf16[8,3,512,64]{2,3,1,0:T(8,128)(2,1)}, f32[8,3,512]{2,1,0:T(4,128)}, f32[8,3]{1,0:T(8,128)}, bf16[8,3,512,64]{2,3,1,0:T(8,128)(2,...) while((s32[]{:T(128)}, ...), condition=%wide.region_5.6_spmd.clone.clone, body=%wide.region_1.5_spmd.clone.sunk.clone | while | flops 419953152 | bytes 21889676 | solution.py:537
  287.1 2.3 select_reduce_fusion.7
  290.0 2.7 fusion.165
  296.6 2.3 select_reduce_fusion.7
  299.5 2.7 fusion.165
  309.1 2.7 fusion.165
  318.6 2.7 fusion.165
  328.1 2.7 fusion.165
  337.6 2.7 fusion.165
  347.1 2.7 fusion.165
  356.6 2.7 fusion.165
  360.6 14.7 all-gather.21.cloned.1.call-done
  375.4 6.0 multiply_reduce_fusion.3
  383.8 127.4 %all-gather.23.cloned.1.call-done = bf16[1,8192,1536]{2,1,0:T(8,128)(2,1)} async-done(((bf16[1,512,1536]{2,1,0:T(8,128)(2,1)}), bf16[1,8192,1536]{2,1,0:T(8,128)(2,1)}) %all-gather.23.cloned.1.call-update) | async-done | bytes 25165840 | tf_op jit(solution)/shard_map/all_gather | solution.py:474
  511.2 542.8 %shard_map.245 = (bf16[16,512,1536]{2,1,0:T(8,128)(2,1)}, bf16[8,2,256,3200]{3,2,1,0:T(8,128)(2,1)}, bf16[8,2,256,3200]{3,2,1,0:T(8,128)(2,1)}, bf16[4,2,256,320...) custom-call(bf16[512,1536]{1,0:T(8,128)(2,1)} %copy-done, ...), custom_call_target="tpu_custom_call" | custom-call | tf_op jit(solution)/shard_map/pallas_call | solution.py:414
  1054.0 8.3 add_add_fusion
  1065.3 2.3 convert_add_fusion
  1069.3 2.6 convolution_convert_fusion.4
  1072.6 119.9 %while.33 = (s32[]{:T(128)}, f32[8,3,512,64]{2,3,1,0:T(8,128)}, bf16[8,1024,64]{1,2,0:T(8,128)(2,1)}, bf16[8,1024,64]{1,2,0:T(8,128)(2,1)}, bf16[8,3,512,64]{2,3...) while((s32[]{:T(128)}, f32[8,3,512,64]{2,3,1,0:T(8,128)}, ...), condition=%wide.region_14.15_spmd.clone.clone, body=%wide.region_12.14_spmd.clone.sunk.clone | while | flops 1027078656 | bytes 51440760 | solution.py:621
  1075.9 3.0 multiply_reduce_fusion.6
  1080.6 2.7 fusion.176
  1090.9 3.0 multiply_reduce_fusion.6
  1095.5 2.7 fusion.176
  1105.8 3.0 multiply_reduce_fusion.6
  1110.5 2.8 fusion.176
  1120.8 3.0 multiply_reduce_fusion.6
  1125.5 2.7 fusion.176
  1135.8 3.0 multiply_reduce_fusion.6
  1140.5 2.8 fusion.176
  1150.8 3.0 multiply_reduce_fusion.6
  1155.5 2.8 fusion.176
  1165.8 3.0 multiply_reduce_fusion.6
  1170.5 2.7 fusion.176
  1180.8 3.0 multiply_reduce_fusion.6
  1185.5 2.7 fusion.176
  1193.4 4.8 convert_element_type.254
  1200.1 4.9 convolution_convert_fusion
  1205.0 2.6 fusion.57
  1207.6 7.6 copy.80
  1215.2 8.3 convert_element_type.252
  1227.6 4.6 convolution_convert_fusion.1
  1232.2 4.4 fusion.106
  1236.6 37.5 %reduce-scatter.11.cloned.1.call-done = bf16[512,512]{0,1:T(8,128)(2,1)} async-done(((bf16[1024,512]{0,1:T(8,128)(2,1)}), bf16[512,512]{0,1:T(8,128)(2,1)}) %reduce-scatter.11.cloned.1.call-update) | async-done | bytes 524304 | tf_op jit(solution)/shard_map/reduce_scatter | solution.py:631
  1276.2 4.7 convolution_add_fusion.2
  1280.9 15.8 reduce-scatter.13.cloned.1.call-done
  1296.7 6.1 fusion.71
  1305.1 4.0 fusion.56
  1309.1 11.3 copy.78
  1321.3 47.8 %pmax.7 = f32[24]{0:T(128)S(1)} all-reduce(f32[24]{0:T(128)S(1)} %reshape.314), channel_id=1, replica_groups=mesh['dp'=2,'expert'=4,'shard'=4] {'dp','expert','shard'}, use_global_device_ids=true, to_apply=%region_24.25 | all-reduce | flops 24 | bytes 192 | tf_op jit(solution)/shard_map/pmax | solution.py:538
  1372.1 4.1 fusion.80
  1376.2 3.5 convert_element_type.255
  1379.7 78.6 %reduce-scatter.21.cloned.1.call-done = bf16[48,1664]{1,0:T(8,128)(2,1)} async-done(((bf16[1536,1664]{1,0:T(8,128)(2,1)}), bf16[48,1664]{1,0:T(8,128)(2,1)}) %reduce-scatter.21.cloned.1.call-update) | async-done | bytes 159760
  1461.7 75.6 %reduce-scatter.15.cloned.1.call-done = bf16[2,768,1024]{2,1,0:T(8,128)(2,1)} async-done(((bf16[2,1536,1024]{2,1,0:T(8,128)(2,1)}), bf16[2,768,1024]{2,1,0:T(8,128)(2,1)}) %reduce-scatter.15.cloned.1.call-update) | async-done | bytes 3145744 | tf_op jit(solution)/shard_map/reduce_scatter | solution.py:564
  1537.3 5.3 convert_element_type.253
  1542.6 131.8 %reduce-scatter.19.cloned.1.call-done = bf16[48,2688]{1,0:T(8,128)(2,1)} async-done(((bf16[1536,2688]{1,0:T(8,128)(2,1)}), bf16[48,2688]{1,0:T(8,128)(2,1)}) %reduce-scatter.19.cloned.1.call-update) | async-done | bytes 258064
  (269 shorter events, 167.1 us)
Async XLA Ops:
  7.2 42.2 %all-gather.17.cloned.1.call-start = ((), (), s32[]{:S(2)}) async-start(), calls=%async_computation.9 | async-start | bytes 1966080 | tf_op jit(solution)/shard_map/all_gather | solution.py:482
  7.9 79.1 %all-gather.13.cloned.1.call-start = ((), (), s32[]{:S(2)}) async-start(), calls=%async_computation.7 | async-start | bytes 1966080 | tf_op jit(solution)/shard_map/all_gather | solution.py:481
  8.7 260.5 %all-gather.19.cloned.1.call-start = ((), (), s32[]{:S(2)}) async-start(), calls=%async_computation.10 | async-start | bytes 1572864 | tf_op jit(solution)/shard_map/all_gather | solution.py:507
  10.5 266.9 %copy-start.32 = (f32[512]{0:T(512)}, f32[512]{0:T(512)S(1)}, u32[]{:S(2)}) copy-start(f32[512]{0:T(512)S(1)} %add_rsqrt_fusion.1) | copy-start | bytes 6148
  53.1 36.4 %copy-start.2 = (bf16[1,512,1536]{2,1,0:T(8,128)(2,1)S(1)}, bf16[1,512,1536]{2,1,0:T(8,128)(2,1)}, u32[]{:S(2)}) copy-start(bf16[1,512,1536]{2,1,0:T(8,128)(2,1)} %param.18) | copy-start | bytes 4718596
  53.1 36.4 %copy-start.28 = (f32[1536]{0:T(1024)S(1)}, f32[1536]{0:T(1024)}, u32[]{:S(2)}) copy-start(f32[1536]{0:T(1024)} %param.20) | copy-start | bytes 18436
  53.2 217.6 %all-gather.11.cloned.1.call-start = ((), (), s32[]{:S(2)}) async-start(), calls=%async_computation.6 | async-start | bytes 5898240 | tf_op jit(solution)/shard_map/all_gather | solution.py:480
  53.7 230.8 %all-gather.15.cloned.1.call-start = ((), (), s32[]{:S(2)}) async-start(), calls=%async_computation.8 | async-start | bytes 1572864 | tf_op jit(solution)/shard_map/all_gather | solution.py:506
  54.8 227.4 %copy-start.14 = (f32[512,32]{0,1:T(8,128)}, f32[512,32]{0,1:T(8,128)S(1)}, u32[]{:S(2)}) copy-start(f32[512,32]{0,1:T(8,128)S(1)} %get-tuple-element.310) | copy-start | bytes 196612
  92.0 2.5 copy-start.27
  92.1 2.6 copy-start.21
  92.1 3.7 copy-start.24
  93.1 282.3 %all-gather.21.cloned.1.call-start = ((), (), s32[]{:S(2)}) async-start(), calls=%async_computation.11 | async-start | bytes 5898240 | tf_op jit(solution)/shard_map/all_gather | solution.py:483
  93.7 417.5 %all-gather.23.cloned.1.call-start = ((), (), s32[]{:S(2)}) async-start(), calls=%async_computation.16 | async-start | bytes 26738688 | tf_op jit(solution)/shard_map/all_gather | solution.py:474
  94.4 1179.6 %reduce-scatter.11.cloned.1.call-start = ((), (), s32[]{:S(2)}) async-start(), calls=%async_computation.12 | async-start | bytes 1572864 | tf_op jit(solution)/shard_map/reduce_scatter | solution.py:631
  95.8 966.5 %copy-start.19 = (pred[512,32]{1,0:T(32,128)(4,1)}, pred[512,32]{1,0:T(32,128)(4,1)S(1)}, u32[]{:S(2)}) copy-start(pred[512,32]{1,0:T(32,128)(4,1)S(1)} %copy.69) | copy-start | bytes 49156
  360.6 14.7 copy-start.4
  360.6 14.8 copy-start.11
  375.4 6.1 copy-start.25
  381.4 1.5 copy-start.22
  381.8 1.1 copy-start
  383.6 678.8 %copy-start.30 = (f32[512]{0:T(512)}, f32[512]{0:T(512)S(1)}, u32[]{:S(2)}) copy-start(f32[512]{0:T(512)S(1)} %get-tuple-element.313) | copy-start | bytes 6148
  383.8 678.5 %copy-start.31 = (f32[512]{0:T(512)}, f32[512]{0:T(512)S(1)}, u32[]{:S(2)}) copy-start(f32[512]{0:T(512)S(1)} %fusion.95) | copy-start | bytes 6148
  1054.0 9.9 copy-start.23
  1054.0 9.9 copy-start.26
  1063.9 1.4 copy-start.8
  1063.9 5.4 slice-start.4
  1065.3 4.0 slice-start.5
  1067.6 1.7 copy-start.6
  1192.6 104.1 %reduce-scatter.13.cloned.1.call-start = ((), (), s32[]{:S(2)}) async-start(), calls=%async_computation.13 | async-start | bytes 1572864 | tf_op jit(solution)/shard_map/reduce_scatter | solution.py:634
  1193.4 182.8 %reduce-scatter.17.cloned.1.call-start = ((), (), s32[]{:S(2)}) async-start(), calls=%async_computation.15 | async-start | bytes 4718592 | tf_op jit(solution)/shard_map/reduce_scatter | solution.py:567
  1198.2 1.4 copy-start.1
  1198.2 1.9 copy-start.16
  1198.2 260.0 %reduce-scatter.21.cloned.1.call-start = ((), (), s32[]{:S(2)}) async-start(), calls=%async_computation.18 | async-start | bytes 5271552
  1215.2 322.1 %reduce-scatter.15.cloned.1.call-start = ((), (), s32[]{:S(2)}) async-start(), calls=%async_computation.14 | async-start | bytes 9437184 | tf_op jit(solution)/shard_map/reduce_scatter | solution.py:564
  1223.5 1.9 copy-start.10
  1223.5 1.9 copy-start.15
  1223.5 1.9 copy-start.18
  1223.6 450.9 %reduce-scatter.19.cloned.1.call-start = ((), (), s32[]{:S(2)}) async-start(), calls=%async_computation.17 | async-start | bytes 8515584
  1225.4 6.7 slice-start.2
  1225.9 1.6 copy-start.3
  1225.9 1.6 copy-start.29
  1225.9 1.6 copy-start.33
  1227.6 4.6 slice-start.3
  1236.6 39.7 %copy-start.7 = (bf16[1536,512]{1,0:T(8,128)(2,1)S(1)}, bf16[1536,512]{1,0:T(8,128)(2,1)}, u32[]{:S(2)}) copy-start(bf16[1536,512]{1,0:T(8,128)(2,1)} %all-gather.13.cloned.1.call-done) | copy-start | bytes 4718596
  1275.4 0.8 copy-start.12
  1280.9 21.9 %copy-start.13 = (bf16[512,8,64]{0,2,1:T(8,128)(2,1)S(1)}, bf16[512,8,64]{0,2,1:T(8,128)(2,1)}, u32[]{:S(2)}) copy-start(bf16[512,8,64]{0,2,1:T(8,128)(2,1)} %copy-done.12) | copy-start | bytes 1572868
  1296.7 8.3 slice-start
  1302.8 1.1 copy-start.20
  1302.8 2.3 slice-start.1
  1320.4 0.8 copy-start.34
  1320.4 49.2 %copy-start.17 = (bf16[384,512]{1,0:T(8,128)(2,1)S(1)}, bf16[384,512]{1,0:T(8,128)(2,1)}, u32[]{:S(2)}) copy-start(bf16[384,512]{1,0:T(8,128)(2,1)} %param.22) | copy-start | bytes 1179652
  1320.4 50.0 %copy-start.9 = (bf16[384,1536]{1,0:T(8,128)(2,1)S(1)}, bf16[384,1536]{1,0:T(8,128)(2,1)}, u32[]{:S(2)}) copy-start(bf16[384,1536]{1,0:T(8,128)(2,1)} %param.21) | copy-start | bytes 3538948
  1369.1 7.1 copy-start.35
  1369.6 2.5 copy-start.5
Sparse Core Ops, SparseCore 0:
  9.6 39.7 all-gather.16
  51.0 35.9 all-gather.12
  89.1 20.1 all-gather.18
  110.8 148.8 all-gather.10
  261.6 22.8 all-gather.14
  285.9 89.4 all-gather.20
  376.9 134.2 all-gather.22
  1192.7 81.2 reduce-scatter.10
  1276.4 20.3 reduce-scatter.12
  1298.8 43.8 reduce-scatter.16
  1349.2 109.0 reduce-scatter.20
  1461.0 76.2 reduce-scatter.14
  1544.2 130.2 reduce-scatter.18

commit v3 on v2

--- a/solution.py
+++ b/solution.py
@@ -1,3 +1,4 @@
+import functools
 import math
 
 import jax
@@ -69,15 +70,436 @@
     return exponent / jnp.sum(exponent, axis=-1, keepdims=True)
 
 
+def max_dp(values):
+    if lax.axis_size("dp") != 2:
+        return lax.pmax(values, "dp")
+    return jnp.maximum(values, lax.ppermute(values, "dp", [(0, 1), (1, 0)]))
+
+
+def allowed_bias(position_ref, docs_all_ref, docs_own_ref):
+    keys, rows = docs_all_ref.shape[0], docs_own_ref.shape[1]
+    key_at = lax.broadcasted_iota(jnp.int32, (keys, rows), 0)
+    row_at = lax.broadcasted_iota(jnp.int32, (keys, rows), 1) + position_ref[0]
+    allowed = (key_at <= row_at) & (docs_all_ref[...] == docs_own_ref[...])
+    return jnp.where(allowed, 0.0, EXCLUDED)
+
+
+def attend_kernel(
+    position_ref, docs_all_ref, docs_own_ref, query_ref, key_ref, value_ref,
+    mix_ref, log_ref, top_ref, bias,
+):
+    @pl.when(pl.program_id(0) == 0)
+    def _():
+        bias[...] = allowed_bias(position_ref, docs_all_ref, docs_own_ref)
+
+    rows = query_ref.shape[0]
+    mixes, logs, tops = [], [], []
+    for head in range(query_ref.shape[1] // HEAD_DIM):
+        group = head * key_ref.shape[1] // query_ref.shape[1] * HEAD_DIM
+        query = query_ref[:, head * HEAD_DIM : (head + 1) * HEAD_DIM]
+        key = key_ref[:, group : group + HEAD_DIM]
+        value = value_ref[:, group : group + HEAD_DIM]
+        scores = contract_cols(key, query) + bias[...]
+        top = jnp.max(scores, axis=0, keepdims=True)
+        exponent = jnp.exp(scores - top)
+        totals = jnp.sum(exponent, axis=0, keepdims=True)
+        probs = (exponent * (1.0 / totals)).astype(jnp.bfloat16)
+        mixes.append(contract_rows(value, probs))
+        logs.append(top + jnp.log(totals))
+        tops.append(top)
+    mix_ref[...] = jnp.concatenate(mixes, axis=0).T.astype(jnp.bfloat16)
+    blank = [jnp.zeros((8 - len(logs), rows), jnp.float32)]
+    log_ref[0] = jnp.concatenate(logs + blank, axis=0)
+    top_ref[0] = jnp.broadcast_to(
+        jnp.max(jnp.concatenate(tops + blank, axis=0), axis=1, keepdims=True), (8, 128)
+    )
+
+
+def attend_back_kernel(
+    position_ref, docs_all_ref, docs_own_ref, query_ref, key_ref, value_ref, mix_grad_ref, log_ref,
+    query_grad_ref, key_grad_ref, value_grad_ref, bias,
+):
+    @pl.when(pl.program_id(0) == 0)
+    def _():
+        bias[...] = allowed_bias(position_ref, docs_all_ref, docs_own_ref)
+
+    query_grads, key_grads, value_grads = [], {}, {}
+    for head in range(query_ref.shape[1] // HEAD_DIM):
+        group = head * key_ref.shape[1] // query_ref.shape[1] * HEAD_DIM
+        query = query_ref[:, head * HEAD_DIM : (head + 1) * HEAD_DIM]
+        mix_grad = mix_grad_ref[:, head * HEAD_DIM : (head + 1) * HEAD_DIM]
+        key = key_ref[:, group : group + HEAD_DIM]
+        value = value_ref[:, group : group + HEAD_DIM]
+        scores = contract_cols(key, query) + bias[...]
+        probs = jnp.exp(scores - log_ref[0, head : head + 1, :])
+        prob_grads = contract_cols(value, mix_grad)
+        centre = jnp.sum(probs * prob_grads, axis=0, keepdims=True)
+        score_grads = (probs * (prob_grads - centre)).astype(jnp.bfloat16)
+        query_grads.append(contract_rows(key, score_grads))
+        key_term = jnp.dot(score_grads, query, preferred_element_type=jnp.float32)
+        value_term = jnp.dot(
+            probs.astype(jnp.bfloat16), mix_grad, preferred_element_type=jnp.float32
+        )
+        key_grads[group] = key_grads[group] + key_term if group in key_grads else key_term
+        value_grads[group] = value_grads[group] + value_term if group in value_grads else value_term
+    query_grad_ref[...] = jnp.concatenate(query_grads, axis=0).T
+    for group in key_grads:
+        key_grad_ref[:, group : group + HEAD_DIM] = key_grads[group]
+        value_grad_ref[:, group : group + HEAD_DIM] = value_grads[group]
+
+
+def attention_specs(rows, keys, query_width, key_width):
+    whole = lambda shape: pl.BlockSpec(shape, lambda i: (0, 0))
+    by_head = lambda count, width: pl.BlockSpec((count, width), lambda i: (0, i))
+    steps = key_width // 128
+    in_specs = [
+        pl.BlockSpec(memory_space=pltpu.SMEM),
+        whole((keys, 1)),
+        whole((1, rows)),
+        by_head(rows, query_width // steps),
+        by_head(keys, 128),
+        by_head(keys, 128),
+    ]
+    return steps, in_specs, by_head, pl.BlockSpec((1, 8, rows), lambda i: (i, 0, 0))
+
+
+def attend(position, docs_all, docs_own, query, key, value):
+    rows, query_width = query.shape
+    keys, key_width = key.shape
+    steps, in_specs, by_head, by_log = attention_specs(rows, keys, query_width, key_width)
+    mix, logs, tops = pl.pallas_call(
+        attend_kernel,
+        grid=(steps,),
+        in_specs=in_specs,
+        out_specs=(
+            by_head(rows, query_width // steps), by_log, pl.BlockSpec((1, 8, 128), lambda i: (i, 0, 0))
+        ),
+        out_shape=(
+            jax.ShapeDtypeStruct((rows, query_width), jnp.bfloat16),
+            jax.ShapeDtypeStruct((steps, 8, rows), jnp.float32),
+            jax.ShapeDtypeStruct((steps, 8, 128), jnp.float32),
+        ),
+        scratch_shapes=[pltpu.VMEM((keys, rows), jnp.float32)],
+        compiler_params=pltpu.CompilerParams(vmem_limit_bytes=50 * 2**20),
+    )(position, docs_all[:, None], docs_own[None, :], query, key, value)
+    return mix, logs, tops[:, : QUERY_HEADS // steps, 0].reshape(QUERY_HEADS)
+
+
+def attend_back(position, docs_all, docs_own, query, key, value, mix_grad, logs):
+    rows, query_width = query.shape
+    keys, key_width = key.shape
+    steps, in_specs, by_head, by_log = attention_specs(rows, keys, query_width, key_width)
+    wide = query_width // steps
+    return pl.pallas_call(
+        attend_back_kernel,
+        grid=(steps,),
+        in_specs=in_specs + [by_head(rows, wide), by_log],
+        out_specs=(by_head(rows, wide), by_head(keys, 128), by_head(keys, 128)),
+        out_shape=(
+            jax.ShapeDtypeStruct((rows, query_width), jnp.float32),
+            jax.ShapeDtypeStruct((keys, key_width), jnp.float32),
+            jax.ShapeDtypeStruct((keys, key_width), jnp.float32),
+        ),
+        scratch_shapes=[pltpu.VMEM((keys, rows), jnp.float32)],
+        compiler_params=pltpu.CompilerParams(vmem_limit_bytes=50 * 2**20),
+    )(position, docs_all[:, None], docs_own[None, :], query, key, value, mix_grad, logs)
+
+
+def scatter_kernel(
+    whole_ref, total_ref, from_core, pair_sum, first_x, first_y, mid, last_x, last_y, sums, from_line,
+    core_send, core_recv, x_send, x_recv, y_send, y_recv, z_send, z_recv,
+):
+    half, expert, depth = lax.axis_index("dp"), lax.axis_index("expert"), lax.axis_index("shard")
+    side, core = expert // 2, expert % 2
+    partner = {"dp": 1 - half}
+    opposite = {"expert": 2 * ((side + 1) % 2) + core}
+    sibling = {"expert": 2 * side + (core + 1) % 2}
+    cols = whole_ref.shape[2] // 2
+    left, right = pl.ds(0, cols), pl.ds(cols, cols)
+
+    def along(distance):
+        return {"shard": (depth + distance) % 4}
+
+    barrier = pltpu.get_barrier_semaphore()
+    for peer in (partner, opposite, sibling, along(1), along(2), along(3)):
+        pl.semaphore_signal(barrier, inc=1, device_id=peer, device_id_type=pl.DeviceIdType.MESH)
+    pl.semaphore_wait(barrier, 6)
+
+    def remote(src, dst, send, recv, to):
+        return pltpu.make_async_remote_copy(
+            src_ref=src, dst_ref=dst, send_sem=send, recv_sem=recv, device_id=to,
+            device_id_type=pl.DeviceIdType.MESH,
+        )
+
+    def added(a, b):
+        return (a.astype(jnp.float32) + b.astype(jnp.float32)).astype(jnp.bfloat16)
+
+    def chunk(j, other_core):
+        return 4 * ((half + j // 2) % 2) + 2 * ((side + j % 2) % 2) + (core + other_core) % 2
+
+    def to_core(j):
+        return remote(
+            whole_ref.at[chunk(j, 1)], from_core.at[j], core_send.at[j], core_recv.at[j], sibling
+        )
+
+    def to_x(k):
+        return remote(
+            pair_sum.at[2 + k, :, left], first_x.at[k], x_send.at[k], x_recv.at[k], partner
+        )
+
+    def to_y(k):
+        return remote(
+            pair_sum.at[2 * k + 1, :, right], first_y.at[k], y_send.at[k], y_recv.at[k], opposite
+        )
+
+    def then_y():
+        return remote(mid.at[0], last_y, y_send.at[2], y_recv.at[2], opposite)
+
+    def then_x():
+        return remote(mid.at[1], last_x, x_send.at[2], x_recv.at[2], partner)
+
+    def to_line(zi, part):
+        return remote(
+            sums.at[part, (depth + zi) % 4], from_line.at[zi, part], z_send.at[zi, part],
+            z_recv.at[zi, part], along(zi),
+        )
+
+    order = (3, 2, 1, 0)
+    for j in order:
+        to_core(j).start()
+    for j in order:
+        to_core(j).wait_recv()
+        pair_sum[j] = added(whole_ref[chunk(j, 0)], from_core[j])
+        if j == 3:
+            to_x(1).start()
+            to_y(1).start()
+        if j == 2:
+            to_x(0).start()
+        if j == 1:
+            to_y(0).start()
+    to_x(1).wait_recv()
+    mid[0] = added(pair_sum[1, :, left], first_x[1])
+    then_y().start()
+    to_y(1).wait_recv()
+    mid[1] = added(pair_sum[2, :, right], first_y[1])
+    then_x().start()
+    share = sums.shape[2]
+    for part, first, last, last_ref, own in (
+        (0, to_x(0), then_y(), last_y, left), (1, to_y(0), then_x(), last_x, right)
+    ):
+        first.wait_recv()
+        last.wait_recv()
+        near = (first_x if part == 0 else first_y)[0]
+        full = (
+            pair_sum[0, :, own].astype(jnp.float32)
+            + near.astype(jnp.float32)
+            + last_ref[...].astype(jnp.float32)
+        ).astype(jnp.bfloat16)
+        for z in range(4):
+            sums[part, z] = full[z * share : (z + 1) * share]
+        for zi in (2, 1, 3):
+            to_line(zi, part).start()
+    for part, own in ((0, left), (1, right)):
+        result = sums[part, depth].astype(jnp.float32)
+        for zi in (1, 3, 2):
+            to_line(zi, part).wait_recv()
+            result = result + from_line[zi, part].astype(jnp.float32)
+        total_ref[:, own] = result
+    for j in order:
+        to_core(j).wait_send()
+    for k in range(2):
+        to_x(k).wait_send()
+        to_y(k).wait_send()
+    then_x().wait_send()
+    then_y().wait_send()
+    for zi in range(1, 4):
+        for part in range(2):
+            to_line(zi, part).wait_send()
+
+
+def scatter_every(whole):
+    if lax.axis_size("dp") != 2:
+        return lax.psum_scatter(whole, EVERY, scatter_dimension=0, tiled=True).astype(jnp.float32)
+    rows, width = whole.shape[0] // 8, whole.shape[1]
+    cols, low, dma = width // 2, whole.dtype, pltpu.SemaphoreType.DMA
+    return pl.pallas_call(
+        scatter_kernel,
+        out_shape=jax.ShapeDtypeStruct((rows // 4, width), jnp.float32),
+        in_specs=[pl.BlockSpec(memory_space=pltpu.VMEM)],
+        out_specs=pl.BlockSpec(memory_space=pltpu.VMEM),
+        scratch_shapes=[
+            pltpu.VMEM((4, rows, width), low),
+            pltpu.VMEM((4, rows, width), low),
+            pltpu.VMEM((2, rows, cols), low),
+            pltpu.VMEM((2, rows, cols), low),
+            pltpu.VMEM((2, rows, cols), low),
+            pltpu.VMEM((rows, cols), low),
+            pltpu.VMEM((rows, cols), low),
+            pltpu.VMEM((2, 4, rows // 4, cols), low),
+            pltpu.VMEM((4, 2, rows // 4, cols), low),
+            dma((4,)), dma((4,)), dma((3,)), dma((3,)), dma((3,)), dma((3,)), dma((4, 2)), dma((4, 2)),
+        ],
+        compiler_params=pltpu.CompilerParams(
+            collective_id=2, has_side_effects=True, vmem_limit_bytes=44 * 2**20
+        ),
+    )(whole.reshape(8, rows, width))
+
+
+def gather_dp(rows):
+    if lax.axis_size("dp") != 2:
+        return lax.all_gather(rows, "dp", axis=0, tiled=True)
+    other = lax.ppermute(rows, "dp", [(0, 1), (1, 0)])
+    early = lax.axis_index("dp") == 0
+    return jnp.concatenate(
+        [jnp.where(early, rows, other), jnp.where(early, other, rows)], axis=0
+    )
+
+
+def scatter_dp(whole, dim):
+    if lax.axis_size("dp") != 2:
+        return lax.psum_scatter(
+            whole.astype(jnp.bfloat16), "dp", scatter_dimension=dim, tiled=True
+        ).astype(jnp.float32)
+    size, at = whole.shape[dim] // 2, lax.axis_index("dp")
+    given = lax.dynamic_slice_in_dim(whole, (1 - at) * size, size, dim).astype(jnp.bfloat16)
+    taken = lax.ppermute(given, "dp", [(0, 1), (1, 0)])
+    kept = lax.dynamic_slice_in_dim(whole, at * size, size, dim)
+    return kept.astype(jnp.float32) + taken.astype(jnp.float32)
+
+
+def weights_kernel(first_ref, second_ref, first_full, second_full, own_sem, send_sem, recv_sem):
+    pair, expert, depth = lax.axis_index("dp"), lax.axis_index("expert"), lax.axis_index("shard")
+    side, core = expert // 2, expert % 2
+    half = pair % 2
+    partner = {"dp": pair + 1 - 2 * half}
+    opposite = {"expert": 2 * ((side + 1) % 2) + core}
+    sibling = {"expert": 2 * side + (core + 1) % 2}
+    rows = first_ref.shape[0]
+    part = rows // 8
+    arrays = ((first_ref, first_full), (second_ref, second_full))
+
+    def along(distance):
+        return {"shard": (depth + distance) % 4}
+
+    barrier = pltpu.get_barrier_semaphore()
+    for peer in (partner, opposite, sibling, along(1), along(2), along(3)):
+        pl.semaphore_signal(barrier, inc=1, device_id=peer, device_id_type=pl.DeviceIdType.MESH)
+    pl.semaphore_wait(barrier, 6)
+
+    def eighth(px, pa, pc):
+        return 4 * ((half + px) % 2) + 2 * ((side + pa) % 2) + (core + pc) % 2
+
+    def place(full, zi, px, pa, pc):
+        start = ((depth + zi) % 4) * rows + eighth(px, pa, pc) * part
+        return full.at[pl.ds(pl.multiple_of(start, part), part)]
+
+    def copy(which, zi, source, hop, to):
+        px, pa, pc = source
+        full = arrays[which][1]
+        there = 4 * (px ^ hop[0]) + 2 * (pa ^ hop[1]) + (pc ^ hop[2])
+        return pltpu.make_async_remote_copy(
+            src_ref=place(full, zi, px, pa, pc),
+            dst_ref=place(full, zi, px, pa, pc),
+            send_sem=send_sem.at[which, zi, there],
+            recv_sem=recv_sem.at[which, zi, there],
+            device_id=to,
+            device_id_type=pl.DeviceIdType.MESH,
+        )
+
+    def along_line(which, zi):
+        own, full = arrays[which]
+        start = eighth(0, 0, 0) * part
+        return pltpu.make_async_remote_copy(
+            src_ref=own.at[pl.ds(pl.multiple_of(start, part), part)],
+            dst_ref=full.at[pl.ds(pl.multiple_of(depth * rows + start, part), part)],
+            send_sem=send_sem.at[which, zi, 0],
+            recv_sem=recv_sem.at[which, zi, 0],
+            device_id=along(4 - zi),
+            device_id_type=pl.DeviceIdType.MESH,
+        )
+
+    own_copies = [
+        pltpu.make_async_copy(
+            own, full.at[pl.ds(pl.multiple_of(depth * rows, rows), rows)], own_sem.at[which]
+        )
+        for which, (own, full) in enumerate(arrays)
+    ]
+    near, over, by = (1, 0, 0), (0, 1, 0), (0, 0, 1)
+    for which in range(2):
+        for zi in (1, 3, 2):
+            along_line(which, zi).start()
+    for own_copy in own_copies:
+        own_copy.start()
+    for which in range(2):
+        for zi in (1, 3, 2):
+            along_line(which, zi).wait_recv()
+            copy(which, zi, (0, 0, 0), near, partner).start()
+            copy(which, zi, (0, 0, 0), over, opposite).start()
+            copy(which, zi, (0, 0, 0), by, sibling).start()
+        for zi in (1, 3, 2):
+            copy(which, zi, (0, 0, 0), near, partner).wait_recv()
+            copy(which, zi, (1, 0, 0), by, sibling).start()
+
+            @pl.when(core == 0)
+            def _():
+                copy(which, zi, (1, 0, 0), over, opposite).start()
+
+            copy(which, zi, (0, 0, 0), over, opposite).wait_recv()
+            copy(which, zi, (0, 1, 0), by, sibling).start()
+
+            @pl.when(core == 1)
+            def _():
+                copy(which, zi, (0, 1, 0), near, partner).start()
+
+    for which in range(2):
+        for zi in (1, 3, 2):
+            copy(which, zi, (1, 0, 0), over, opposite).wait_recv()
+            copy(which, zi, (1, 1, 0), by, sibling).start()
+    for which in range(2):
+        for zi in (1, 3, 2):
+            for px, pa in ((0, 0), (1, 0), (0, 1), (1, 1)):
+                copy(which, zi, (px, pa, 0), by, sibling).wait()
+            along_line(which, zi).wait_send()
+            copy(which, zi, (0, 0, 0), near, partner).wait_send()
+            copy(which, zi, (0, 0, 0), over, opposite).wait_send()
+
+            @pl.when(core == 0)
+            def _():
+                copy(which, zi, (1, 0, 0), over, opposite).wait_send()
+
+            @pl.when(core == 1)
+            def _():
+                copy(which, zi, (0, 1, 0), near, partner).wait_send()
+
+    for own_copy in own_copies:
+        own_copy.wait()
+
+
+def gather_weights(first, second):
+    anywhere = pl.BlockSpec(memory_space=pl.ANY)
+    dma = pltpu.SemaphoreType.DMA
+    return pl.pallas_call(
+        weights_kernel,
+        out_shape=tuple(
+            jax.ShapeDtypeStruct((4 * part.shape[0], part.shape[1]), part.dtype)
+            for part in (first, second)
+        ),
+        in_specs=[anywhere] * 2,
+        out_specs=(anywhere,) * 2,
+        scratch_shapes=[dma((2,)), dma((2, 4, 8)), dma((2, 4, 8))],
+        compiler_params=pltpu.CompilerParams(collective_id=1, has_side_effects=True),
+    )(first, second)
+
+
 def experts_kernel(
-    hidden_ref, cot_ref, routes_ref, router_ref, win_ref, wout_ref,
-    rows_ref, kept_ref, core_ref, across_ref, line_ref, stage_ref, dwin_ref, dwout_ref,
-    acc_in, acc_out, win, wout, router, row_tile, cot_tile, route_tile, made, parts,
+    in_pairs, hidden_ref, cot_ref, router_ref, win_ref, wout_ref,
+    rows_ref, kept_ref, core_ref, across_ref, line_ref, stage_ref, dwin_ref, dwout_ref, taken_in, taken_out,
+    acc_in, acc_out, win, wout, router, row_tile, cot_tile, made, parts,
     load_sem, tile_sem, row_recv, core_send, across_send, line_send,
-    made_sem, part_sem, core_recv, across_recv, line_recv, stage_sem, stage_send, store_sem,
+    made_sem, part_sem, core_recv, across_recv, line_recv, stage_sem, stage_send, store_sem, given_sem, taken_sem,
 ):
     own_count, width = wout_ref.shape[0], wout_ref.shape[1]
-    rows_own, model = hidden_ref.shape
+    rows_own, model = hidden_ref.shape[0] - 16, hidden_ref.shape[1]
     tile = rows_own // 2
     expert, depth = lax.axis_index("expert"), lax.axis_index("shard")
     side, core = expert // 2, expert % 2
@@ -94,9 +516,12 @@
         )
 
     barrier = pltpu.get_barrier_semaphore()
-    for peer in (sibling, opposite, along(1), along(2), along(3)):
+    half = lax.axis_index("dp")
+    partner = {"dp": 1 - half}
+    peers = [sibling, opposite, along(1), along(2), along(3)] + [partner] * in_pairs
+    for peer in peers:
         pl.semaphore_signal(barrier, inc=1, device_id=peer, device_id_type=pl.DeviceIdType.MESH)
-    pl.semaphore_wait(barrier, 5)
+    pl.semaphore_wait(barrier, len(peers))
 
     loads = [
         pltpu.make_async_copy(win_ref, win, load_sem.at[0]),
@@ -163,9 +588,6 @@
             pltpu.make_async_copy(
                 cot_ref.at[pl.ds(start, tile)], cot_tile.at[slot], tile_sem.at[1, slot]
             ),
-            pltpu.make_async_copy(
-                routes_ref.at[pl.ds(start, tile)], route_tile.at[slot], tile_sem.at[2, slot]
-            ),
         )
 
     acc_in[...] = jnp.zeros_like(acc_in)
@@ -310,10 +732,10 @@
         def _():
             made_done(step - 2)
 
-        rows, cot = row_tile[slot], cot_tile[slot]
+        rows, cot = row_tile[slot], cot_tile[slot, :, :model]
         logits = jnp.dot(rows, router[...], preferred_element_type=jnp.float32)
         lanes = lax.broadcasted_iota(jnp.int32, logits.shape, 1)
-        routes = route_tile[slot]
+        routes = cot_tile[slot, :, model:].astype(jnp.float32).astype(jnp.int32)
         picked = lanes == routes[:, 0:1]
         for k in range(1, TOP):
             picked = picked | (lanes == routes[:, k : k + 1])
@@ -369,12 +791,28 @@
         return carry
 
     lax.fori_loop(0, 32, body, 0)
-    stores = [
-        pltpu.make_async_copy(acc_in, dwin_ref, store_sem.at[0]),
-        pltpu.make_async_copy(acc_out, dwout_ref, store_sem.at[1]),
-    ]
-    for store in stores:
-        store.start()
+    win[...] = acc_in[...].astype(jnp.bfloat16)
+    wout[...] = acc_out[...].astype(jnp.bfloat16)
+    grads = ((acc_in, win, taken_in, dwin_ref), (acc_out, wout, taken_out, dwout_ref))
+
+    def half_rows(ref, at):
+        size = ref.shape[1] // 2
+        return ref.at[:, pl.ds(pl.multiple_of(at * size, size), size)]
+
+    def give(which):
+        _, sent, taken, _ = grads[which]
+        return remote(
+            half_rows(sent, 1 - half), taken, given_sem.at[which], taken_sem.at[which], partner
+        )
+
+    def store(which):
+        total, sent, _, result = grads[which]
+        return pltpu.make_async_copy(
+            half_rows(total, half) if in_pairs else sent, result, store_sem.at[which]
+        )
+
+    for which in range(2):
+        give(which).start() if in_pairs else store(which).start()
     staged(5, 1).wait()
     send_z(2, 1).start()
     for sub in range(2):
@@ -398,12 +836,24 @@
         to_opposite(hidden_ref, r).wait_send()
     for zi in range(1, 4):
         to_line(zi).wait_send()
-    for store in stores:
-        store.wait()
-
-
-def experts_pass(hidden, cotangent, routes, w_router, expert_in, expert_out):
-    rows_own, model = hidden.shape
+    if in_pairs:
+        for which in range(2):
+            total, sent, taken, _ = grads[which]
+            give(which).wait_recv()
+            fetch = pltpu.make_async_copy(taken, half_rows(sent, half), load_sem.at[which])
+            fetch.start()
+            fetch.wait()
+            size = total.shape[1] // 2
+            rows = pl.ds(pl.multiple_of(half * size, size), size)
+            total[:, rows] += sent[:, rows].astype(jnp.float32)
+            store(which).start()
+            give(which).wait_send()
+    for which in range(2):
+        store(which).wait()
+
+
+def experts_pass(hidden, cotangent, w_router, expert_in, expert_out):
+    rows_own, model = hidden.shape[0] - 16, hidden.shape[1]
     tile = rows_own // 2
     wide = 2 * model + 128
     anywhere = pl.BlockSpec(memory_space=pl.ANY)
@@ -411,20 +861,24 @@
     kept = jax.ShapeDtypeStruct((8, 2, tile, wide), low)
     quarter = jax.ShapeDtypeStruct((4, 2, tile, wide), low)
     dma = pltpu.SemaphoreType.DMA
+    in_pairs = lax.axis_size("dp") == 2
+    share = lambda w: (w.shape[0], w.shape[1] // 2 if in_pairs else w.shape[1], w.shape[2])
     results = pl.pallas_call(
-        experts_kernel,
+        functools.partial(experts_kernel, in_pairs),
         out_shape=(
-            jax.ShapeDtypeStruct((16, rows_own, model), low),
+            jax.ShapeDtypeStruct((16, rows_own + 16, model), low),
             kept,
             kept,
             quarter,
             quarter,
             jax.ShapeDtypeStruct((7, 2, tile, wide), low),
-            jax.ShapeDtypeStruct(expert_in.shape, jnp.float32),
-            jax.ShapeDtypeStruct(expert_out.shape, jnp.float32),
+            jax.ShapeDtypeStruct(share(expert_in), jnp.float32 if in_pairs else low),
+            jax.ShapeDtypeStruct(share(expert_out), jnp.float32 if in_pairs else low),
+            jax.ShapeDtypeStruct(share(expert_in), low),
+            jax.ShapeDtypeStruct(share(expert_out), low),
         ),
-        in_specs=[anywhere] * 6,
-        out_specs=(anywhere,) * 8,
+        in_specs=[anywhere] * 5,
+        out_specs=(anywhere,) * 10,
         scratch_shapes=[
             pltpu.VMEM(expert_in.shape, jnp.float32),
             pltpu.VMEM(expert_out.shape, jnp.float32),
@@ -432,23 +886,25 @@
             pltpu.VMEM(expert_out.shape, low),
             pltpu.VMEM(w_router.shape, low),
             pltpu.VMEM((2, tile, model), low),
-            pltpu.VMEM((2, tile, model), low),
-            pltpu.VMEM((2, tile, routes.shape[1]), jnp.int32),
+            pltpu.VMEM((2, tile, cotangent.shape[1]), low),
             pltpu.VMEM((2, tile, wide), low),
             pltpu.VMEM((3, tile, wide), low),
-            dma((3,)), dma((3, 2)), dma((16,)), dma((8,)), dma((4,)), dma((4,)),
-            dma((2,)), dma((3,)), dma((8, 2)), dma((4, 2)), dma((4, 2)), dma((1,)), dma((7, 2)), dma((2,)),
+            dma((3,)), dma((2, 2)), dma((16,)), dma((8,)), dma((4,)), dma((4,)),
+            dma((2,)), dma((3,)), dma((8, 2)), dma((4, 2)), dma((4, 2)), dma((1,)), dma((7, 2)), dma((2,)), dma((2,)), dma((2,)),
         ],
         compiler_params=pltpu.CompilerParams(
             collective_id=0, has_side_effects=True, vmem_limit_bytes=60 * 2**20
         ),
-    )(hidden, cotangent, routes, w_router, expert_in, expert_out)
-    _, kept, core, across, line, _, weight_in_grad, weight_out_grad = results
+    )(hidden, cotangent, w_router, expert_in, expert_out)
+    rows, kept, core, across, line, _, weight_in_grad, weight_out_grad, _, _ = results
     total = kept[0].astype(jnp.float32) + core[0].astype(jnp.float32)
     total = total + across[0].astype(jnp.float32)
     for zi in range(1, 4):
         total = total + line[zi].astype(jnp.float32)
-    return total.reshape(rows_own, wide), weight_in_grad, weight_out_grad
+    if not in_pairs:
+        weight_in_grad = scatter_dp(weight_in_grad, 1)
+        weight_out_grad = scatter_dp(weight_out_grad, 1)
+    return total.reshape(rows_own, wide), rows[:, rows_own, :128], weight_in_grad, weight_out_grad
 
 
 def on_device(
@@ -471,22 +927,25 @@
     token_matrix, model_width = inputs.shape
     query_per_key = QUERY_HEADS // KEY_VALUE_HEADS
     query_width, key_width = w_query.shape[1], key_weight.shape[1]
-    all_cotangent = lax.all_gather(cotangent[0], GROUP, axis=0, tiled=True)
-    all_routes = lax.all_gather(routes[0], GROUP, axis=0, tiled=True)
+    route_columns = jnp.pad(routes[0].astype(jnp.bfloat16), ((0, 0), (0, 128 - TOP)))
+    all_cotangent = lax.all_gather(
+        jnp.concatenate([cotangent[0], route_columns], axis=1), GROUP, axis=0, tiled=True
+    )
     scale_attn = rms_scale(inputs)
     normed_attn = inputs * scale_attn
     hidden_attn = (normed_attn * gain_attn).astype(jnp.bfloat16)
-    full_query, full_key, full_value, full_output = (
-        lax.all_gather(w_query, "shard", axis=0, tiled=True),
-        lax.all_gather(key_weight, "shard", axis=0, tiled=True),
-        lax.all_gather(value_weight, "shard", axis=0, tiled=True),
-        lax.all_gather(w_output, "shard", axis=0, tiled=True),
-    )
+    full_qkv, full_output = gather_weights(
+        jnp.concatenate([w_query, key_weight, value_weight], axis=1), w_output
+    )
+    full_query = full_qkv[:, :query_width]
+    full_key = full_qkv[:, query_width : query_width + key_width]
+    full_value = full_qkv[:, query_width + key_width :]
     own_positions = lax.axis_index("dp") * token_matrix + jnp.arange(token_matrix)
     local_cosine, local_sine = rope_tables(own_positions, HEAD_DIM)
-    query_proj = jnp.dot(hidden_attn, full_query, preferred_element_type=jnp.float32)
-    key_projected = jnp.dot(hidden_attn, full_key, preferred_element_type=jnp.float32)
-    value_proj = jnp.dot(hidden_attn, full_value, preferred_element_type=jnp.float32)
+    projected = jnp.dot(hidden_attn, full_qkv, preferred_element_type=jnp.float32)
+    query_proj = projected[:, :query_width]
+    key_projected = projected[:, query_width : query_width + key_width]
+    value_proj = projected[:, query_width + key_width :]
     query_rotated = (
         apply_rotary(
             query_proj.reshape(token_matrix, QUERY_HEADS, HEAD_DIM), local_cosine, local_sine
@@ -502,44 +961,12 @@
     )
     value_low = value_proj.astype(jnp.bfloat16)
     own_docs = doc_ids[0]
-    gathered_keys, gathered_values, docs_all = (
-        lax.all_gather(key_rotated, "dp", axis=0, tiled=True),
-        lax.all_gather(value_low, "dp", axis=0, tiled=True),
-        lax.all_gather(own_docs, "dp", axis=0, tiled=True),
-    )
-    total_keys = gathered_keys.shape[0]
-    allowed = (jnp.arange(total_keys)[None, :] <= own_positions[:, None]) & (
-        docs_all[None, :] == own_docs[:, None]
-    )
-    heads_of_query = query_rotated.reshape(
-        token_matrix, KEY_VALUE_HEADS, query_per_key, HEAD_DIM
-    ).transpose(1, 2, 0, 3)
-    heads_of_key = gathered_keys.reshape(total_keys, KEY_VALUE_HEADS, HEAD_DIM).transpose(1, 0, 2)
-    heads_of_value = gathered_values.reshape(total_keys, KEY_VALUE_HEADS, HEAD_DIM).transpose(
-        1, 0, 2
-    )
-
-    def attend(operands):
-        query_group, key_group, value_group = operands
-        scores = jnp.einsum(
-            "gtd,sd->gts", query_group, key_group, preferred_element_type=jnp.float32
-        )
-        scores = jnp.where(allowed[None], scores, EXCLUDED)
-        row_max = jnp.max(scores, axis=-1, keepdims=True)
-        exponent = jnp.exp(scores - row_max)
-        totals = jnp.sum(exponent, axis=-1, keepdims=True)
-        attn_probs = (exponent / totals).astype(jnp.bfloat16)
-        head_mix = jnp.einsum(
-            "gts,sd->gtd", attn_probs, value_group, preferred_element_type=jnp.float32
-        )
-        return (head_mix, (row_max + jnp.log(totals))[..., 0], jnp.max(row_max[..., 0], axis=-1))
-
-    head_mix, log_totals, head_max = lax.map(attend, (heads_of_query, heads_of_key, heads_of_value))
-    largest = lax.pmax(head_max.reshape(QUERY_HEADS), ("dp", "expert", "shard"))
-    attn_low = (
-        head_mix.transpose(2, 0, 1, 3)
-        .reshape(token_matrix, QUERY_HEADS * HEAD_DIM)
-        .astype(jnp.bfloat16)
+    both_gathered = gather_dp(jnp.concatenate([key_rotated, value_low], axis=1))
+    gathered_keys, gathered_values = both_gathered[:, :key_width], both_gathered[:, key_width:]
+    docs_all = lax.all_gather(own_docs, "dp", axis=0, tiled=True)
+    attn_low, log_totals, head_max = attend(
+        own_positions[:1], docs_all, own_docs, query_rotated.reshape(token_matrix, query_width),
+        gathered_keys, gathered_values,
     )
     branch_attn = contract_cols(attn_low, full_output)
     residual = inputs + branch_attn
@@ -552,22 +979,28 @@
     picked = (route_ids[:, :, None] == jnp.arange(expert_count)[None, None, :]).any(axis=1)
     gate_weights = masked_softmax(router_logits, picked)
     grad_out = cotangent[0].astype(jnp.float32)
-    summed, weight_in_grad, weight_out_grad = experts_pass(
-        hidden_ffn, all_cotangent, all_routes, w_router, expert_in, expert_out
+    high = lax.reduce_precision(head_max, 8, 7)
+    middle = lax.reduce_precision(head_max - high, 8, 7)
+    in_three = jnp.concatenate([high, middle, head_max - high - middle]).astype(jnp.bfloat16)
+    extra = jnp.broadcast_to(
+        jnp.pad(in_three, (0, hidden_ffn.shape[1] - in_three.shape[0])), (16, hidden_ffn.shape[1])
+    )
+    summed, maxima, grad_in_shard, grad_out_shard = experts_pass(
+        jnp.concatenate([hidden_ffn, extra], axis=0), all_cotangent, w_router, expert_in, expert_out
     )
     model = hidden_ffn.shape[1]
+    maxima = maxima.astype(jnp.float32)
+    largest = jnp.max(
+        maxima[:, :QUERY_HEADS]
+        + maxima[:, QUERY_HEADS : 2 * QUERY_HEADS]
+        + maxima[:, 2 * QUERY_HEADS : 3 * QUERY_HEADS],
+        axis=0,
+    )
+    largest = max_dp(largest)
     grad_hidden_ffn = summed[:, :model]
     out = (residual + summed[:, model : 2 * model]).astype(jnp.bfloat16)
     gate_cols = summed[:, 2 * model :]
     grad_gates = gate_cols[:, :expert_count] + gate_cols[:, 64 : 64 + expert_count]
-    grad_in_shard, grad_out_shard = (
-        lax.psum_scatter(
-            weight_in_grad.astype(jnp.bfloat16), "dp", scatter_dimension=1, tiled=True
-        ).astype(jnp.float32),
-        lax.psum_scatter(
-            weight_out_grad.astype(jnp.bfloat16), "dp", scatter_dimension=1, tiled=True
-        ).astype(jnp.float32),
-    )
     weighted = gate_weights * jnp.where(picked, grad_gates, 0.0)
     grad_logits = (
         weighted - gate_weights * jnp.sum(weighted, axis=-1, keepdims=True)
@@ -589,52 +1022,14 @@
     attention_gradient = jnp.dot(
         grad_branch, full_output, preferred_element_type=jnp.float32
     ).astype(jnp.bfloat16)
-    head_gradient = attention_gradient.reshape(
-        token_matrix, KEY_VALUE_HEADS, query_per_key, HEAD_DIM
-    ).transpose(1, 2, 0, 3)
-
-    def attend_back(operands):
-        query_group, key_group, value_group, grad_group, log_group = operands
-        scores = jnp.einsum(
-            "gtd,sd->gts", query_group, key_group, preferred_element_type=jnp.float32
-        )
-        attn_probs = jnp.where(allowed[None], jnp.exp(scores - log_group[..., None]), 0.0)
-        grad_probs = jnp.einsum(
-            "gtd,sd->gts", grad_group, value_group, preferred_element_type=jnp.float32
-        )
-        centre = jnp.sum(attn_probs * grad_probs, axis=-1, keepdims=True)
-        grad_scores = (attn_probs * (grad_probs - centre)).astype(jnp.bfloat16)
-        grad_query_group = jnp.einsum(
-            "gts,sd->gtd", grad_scores, key_group, preferred_element_type=jnp.float32
-        )
-        grad_key_group = jnp.einsum(
-            "gts,gtd->sd", grad_scores, query_group, preferred_element_type=jnp.float32
-        )
-        grad_value_group = jnp.einsum(
-            "gts,gtd->sd",
-            attn_probs.astype(jnp.bfloat16),
-            grad_group,
-            preferred_element_type=jnp.float32,
-        )
-        return (grad_query_group, grad_key_group, grad_value_group)
-
-    grad_query_heads, key_head_gradient, value_head_gradient = lax.map(
-        attend_back, (heads_of_query, heads_of_key, heads_of_value, head_gradient, log_totals)
-    )
-    complete_key_gradient = key_head_gradient.transpose(1, 0, 2).reshape(
-        total_keys, KEY_VALUE_HEADS * HEAD_DIM
-    )
-    complete_value_gradient = value_head_gradient.transpose(1, 0, 2).reshape(
-        total_keys, KEY_VALUE_HEADS * HEAD_DIM
-    )
-    local_key_gradient, value_grad_own = (
-        lax.psum_scatter(
-            complete_key_gradient.astype(jnp.bfloat16), "dp", scatter_dimension=0, tiled=True
-        ).astype(jnp.float32),
-        lax.psum_scatter(
-            complete_value_gradient.astype(jnp.bfloat16), "dp", scatter_dimension=0, tiled=True
-        ).astype(jnp.float32),
-    )
+    grad_query_rows, key_gradient, value_gradient = attend_back(
+        own_positions[:1], docs_all, own_docs, query_rotated.reshape(token_matrix, query_width),
+        gathered_keys, gathered_values, attention_gradient, log_totals,
+    )
+    both_own = scatter_dp(
+        jnp.concatenate([key_gradient, value_gradient], axis=1), 0
+    )
+    local_key_gradient, value_grad_own = both_own[:, :key_width], both_own[:, key_width:]
     key_grad_low = (
         apply_rotary(
             local_key_gradient.reshape(token_matrix, KEY_VALUE_HEADS, HEAD_DIM),
@@ -645,32 +1040,25 @@
         .astype(jnp.bfloat16)
     )
     value_grad_low = value_grad_own.astype(jnp.bfloat16)
-    query_grad_rows = grad_query_heads.transpose(2, 0, 1, 3).reshape(
-        token_matrix, QUERY_HEADS, HEAD_DIM
-    )
+    query_grad_rows = grad_query_rows.reshape(token_matrix, QUERY_HEADS, HEAD_DIM)
     query_grad_low = (
         (apply_rotary(query_grad_rows, local_cosine, -local_sine) * 0.125)
         .reshape(token_matrix, QUERY_HEADS * HEAD_DIM)
         .astype(jnp.bfloat16)
     )
-    query_grad = contract_rows(hidden_attn, query_grad_low)
-    key_grad = contract_rows(hidden_attn, key_grad_low)
-    value_grad = contract_rows(hidden_attn, value_grad_low)
-    grad_hidden_attn = (
-        contract_cols(query_grad_low, full_query)
-        + contract_cols(key_grad_low, full_key)
-        + contract_cols(value_grad_low, full_value)
-    )
-    gain_attn_grad = jnp.sum(grad_hidden_attn * normed_attn, axis=0)
+    all_grad_low = jnp.concatenate([query_grad_low, key_grad_low, value_grad_low], axis=1)
+    attn_sums = scatter_every(contract_rows(hidden_attn, all_grad_low).astype(jnp.bfloat16))
+    grad_hidden_attn = contract_cols(all_grad_low, full_qkv)
     grad_inputs = grad_residual + norm_back(grad_hidden_attn, normed_attn, scale_attn, gain_attn)
-    attn_sums = lax.psum_scatter(
-        jnp.concatenate(
-            [query_grad, key_grad, value_grad, as_column(gain_attn_grad)], axis=1
-        ).astype(jnp.bfloat16),
-        EVERY,
-        scatter_dimension=0,
-        tiled=True,
-    ).astype(jnp.float32)
+    share = attn_sums.shape[0]
+    first_row = (
+        (lax.axis_index("dp") * lax.axis_size("expert") + lax.axis_index("expert"))
+        * lax.axis_size("shard")
+        + lax.axis_index("shard")
+    ) * share
+    own_rows = lax.dynamic_slice_in_dim(full_qkv, first_row, share, 0)
+    own_gain = lax.dynamic_slice_in_dim(gain_attn, first_row, share, 0)
+    gain_attn_grad = jnp.sum(own_rows.astype(jnp.float32) * attn_sums, axis=1) / own_gain
     clip_limit = threshold[0].astype(jnp.float32)
     shrink_factor = clip_limit / jnp.maximum(largest, clip_limit)
     query_scale = jnp.repeat(jnp.sqrt(shrink_factor), HEAD_DIM)
@@ -682,7 +1070,7 @@
     return (
         out[None],
         grad_inputs.astype(jnp.bfloat16)[None],
-        attn_sums[:, query_width + 2 * key_width],
+        gain_attn_grad,
         attn_sums[:, :query_width],
         attn_sums[:, query_width : query_width + key_width],
         attn_sums[:, query_width + key_width : query_width + 2 * key_width],

time: 1690 us -> 1040 us (0.62)
  waiting for transfers between devices: 558 us -> 11.5 us
  Pallas kernels: 543 us -> 857 us
  blocking collectives: 220 us -> 11.1 us
  matrix products: 184 us -> 39.8 us
  other arithmetic: 101 us -> 44.2 us
    pallas_call x1 -> x5, Pallas kernels: 543 us -> 857 us  [the longest x1 555 us: experts_pass(): pl.pallas_call(functools.partial(experts_kernel, in_pairs), out_shape=(ja...]
    all_gather x7 -> x1, waiting for transfers between devices: 214 us -> 0.01 us  [on_device(): lax.all_gather(jnp.concatenate([cotangent[0], route_columns], axis=1), GR...]
    unnamed x15 -> x3, waiting for transfers between devices: 214 us -> 0.03 us
    all_gather x2 -> x1, blocking collectives: 172 us -> 11.1 us  [on_device(): docs_all = lax.all_gather(own_docs, 'dp', axis=0, tiled=True)]
    dot_general x59 -> x1, matrix products: 146 us -> 6.77 us  [on_device(): jnp.dot(hidden_attn, full_qkv, preferred_element_type=jnp.float32)]
    reduce_scatter x4 -> x0, waiting for transfers between devices: 129 us -> none  [the longest x1 75.6 us: on_device(): lax.psum_scatter(weight_in_grad.astype(jnp.bfloat16), 'dp', scatter_dimen...]
    pmax x1 -> x0, blocking collectives: 47.8 us -> none  [on_device(): largest = lax.pmax(head_max.reshape(QUERY_HEADS), ('dp', 'expert', 'shard'))]
    convert_element_type x14 -> x3, other arithmetic: 35.5 us -> 1.26 us  [the longest x1 0.77 us: on_device(): maxima = maxima.astype(jnp.float32)]
  transfers between devices with their start and end apart: 13 -> 5, of which waited for: 10 -> 1; matrix products, arithmetic and copies ran while one was open for 12% -> 10% of each run, Pallas kernels for 0% -> 29%
where the time goes in v3:
time: 1040 us
  Pallas kernels  857 us (82%)
  local copies, waits for them, and re-layouts  52.4 us (5%)
  other arithmetic  44.2 us (4%)
  matrix products  39.8 us (4%)
  between operations  15.9 us (2%)
  waiting for transfers between devices  11.5 us (1%)
  blocking collectives  11.1 us (1%)
    pallas_call x1, Pallas kernels, experts_pass(): pl.pallas_call(functools.partial(experts_kernel, in_pairs), out_shape=(ja...  555 us
    pallas_call x1, Pallas kernels, scatter_every(): pl.pallas_call(scatter_kernel, out_shape=jax.ShapeDtypeStruct((rows // 4,...  128 us
    pallas_call x1, Pallas kernels, gather_weights(): pl.pallas_call(weights_kernel, out_shape=tuple((jax.ShapeDtypeStruct((4 *...  103 us
    pallas_call x1, Pallas kernels, attend_back(): pl.pallas_call(attend_back_kernel, grid=(steps,), in_specs=in_specs + [by...  43.5 us
    unnamed x72, local copies, waits for them, and re-layouts  28.7 us
    pallas_call x1, Pallas kernels, attend(): pl.pallas_call(attend_kernel, grid=(steps,), in_specs=in_specs, out_specs...  28.4 us
  transfers between devices with their start and end apart: 5, of which 1 were waited for; matrix products, arithmetic and copies ran while one was open for 10% of the time, Pallas kernels for 29%

profile of v3, /device:TPU:0, one launch (start us, length us, event | category | flops | bytes accessed | tf_op | source)
XLA Modules:
  0.0 1035.8 jit_solution(5418694075486877525)
XLA Ops:
  7.2 0.9 copy.65
  8.2 2.8 fusion.16
  11.1 2.8 pad_maximum_fusion.1.first_ref
  13.9 102.6 %shard_map.245 = (bf16[1536,2560]{1,0:T(8,128)(2,1)}, bf16[1536,1536]{1,0:T(8,128)(2,1)}) custom-call(bf16[384,2560]{1,0:T(8,128)(2,1)} %pad_maximum_fusion.1.first_ref, bf16[384,1536]{1,0:T(8,128)(2,1)} %second_ref.1), custom_call_target="tpu_custom_call" | custom-call | tf_op jit(solution)/shard_map/pallas_call | solution.py:481
  116.9 6.8 fusion.24
  123.8 2.3 copy-done.12
  126.2 1.3 copy.61
  127.8 1.4 subtract_convert_fusion.1
  129.4 1.1 pad_maximum_fusion.6
  130.6 1.5 collective-permute-start
  132.1 3.8 slice.154
  135.8 3.6 copy.60
  139.4 2.4 multiply_subtract_fusion.1
  142.4 1.6 copy.64.query_ref
  143.9 0.5 slice.117.position_ref
  144.5 11.1 %all-gather = s32[1,1024]{1,0:T(1,128)S(1)} all-gather(s32[1,512]{1,0:T(1,128)S(1)} %copy-done), channel_id=2, replica_groups=mesh['dp'=2,'expert'=4,'shard'=4] {'dp'}, dimensions={1}, use_global_device_ids=true | all-gather | bytes 6144 | tf_op jit(solution)/shard_map/all_gather | solution.py:966
  155.8 0.9 copy.66.router_ref
  157.6 1.8 broadcast_select_fusion
  159.5 28.4 %shard_map.246 = (bf16[512,1536]{1,0:T(8,128)(2,1)}, f32[4,8,512]{2,1,0:T(8,128)S(1)}, f32[4,8,128]{2,1,0:T(8,128)S(1)}) custom-call(s32[1]{0:T(128)} %slice.117.position_ref, s32[1024,1]{1,0:T(8,128)S(1)} %copy.63.docs_all_ref, s32[1,512]{1,0:T(1,128)S(1)} %copy-done, bf16[512,1536]{1,0:T(8,128)(2,1)} %copy.64.query_ref, ...), custom_call_target="tpu_custom_call" | custom-call | tf_op jit(solution)/shard_map/pallas_call | solution.py:170
  188.2 6.0 multiply_reduce_fusion.2
  194.6 0.6 copy-done.19
  195.2 0.6 fusion.44
  195.9 0.6 copy-done.24
  196.4 0.8 fusion.29
  197.3 1.3 pad_maximum_fusion.2.hidden_ref
  198.5 554.7 %shard_map.247 = (bf16[16,528,1536]{2,1,0:T(8,128)(2,1)}, bf16[8,2,256,3200]{3,2,1,0:T(8,128)(2,1)}, bf16[8,2,256,3200]{3,2,1,0:T(8,128)(2,1)}, bf16[4,2,256,320...) custom-call(bf16[528,1536]{1,0:T(8,128)(2,1)} %pad_maximum_fusion.2., ...), custom_call_target="tpu_custom_call" | custom-call | tf_op jit(solution)/shard_map/pallas_call | solution.py:866
  753.3 8.2 add_add_fusion
  762.3 1.0 multiply_reduce_fusion
  764.1 0.8 slice_convert_fusion.2
  764.9 1.5 collective-permute-start.2
  766.4 2.2 multiply_add_fusion
  768.6 2.9 convolution_convert_fusion.1
  771.5 2.6 fusion.1
  774.2 7.7 copy.79
  781.9 7.1 convolution_convert_fusion.2.mix_grad_ref
  789.0 43.5 %shard_map.248 = (f32[512,1536]{1,0:T(8,128)}, f32[1024,512]{1,0:T(8,128)}, f32[1024,512]{1,0:T(8,128)}) custom-call(s32[1]{0:T(128)} %slice.117.position_ref, s32[1024,1]{1,0:T(8,128)S(1)} %copy.63.docs_all_ref, s32[1,512]{1,0:T(1,128)S(1)} %copy-done, bf16[512,1536]{1,0:T(8,128)(2,1)} %copy.64.query_ref, bf16[1024,512]{1,0:T(8,128)(2,1)S(1)} %get-tuple-element.112.key_ref, ...), custom_call_target="tpu_custom_call" | custom-call | tf_op jit(solution)/shard_map/pallas_call | solution.py:193
  832.5 3.8 copy.73
  836.4 1.9 constant_dynamic-update-slice_fusion.1
  838.8 2.1 copy-done.8
  841.1 0.6 collective-permute-start.1
  842.5 1.6 fusion.15
  844.1 0.5 fusion.42
  845.1 0.8 multiply_convert_fusion.2
  845.9 2.5 multiply_convert_fusion.1
  848.4 11.5 %collective-permute-done.1 = bf16[512,1024]{1,0:T(8,128)(2,1)} collective-permute-done((bf16[512,1024]{1,0:T(8,128)(2,1)S(1)}, bf16[512,1024]{1,0:T(8,128)(2,1)}, u32[]{:S(2)}, u32[]{:S(2)}) %collective-permute-start.1) | collective-permute-done | bytes 1048608 | tf_op jit(solution)/shard_map/ppermute | solution.py:365
  859.8 2.3 convert_add_fusion.1
  862.2 1.1 slice.169
  863.3 2.7 copy.74
  866.0 1.0 copy.75
  867.0 1.4 subtract_convert_fusion
  868.5 7.0 convolution_convert_fusion
  875.5 128.1 %shard_map.249 = f32[48,2560]{1,0:T(8,128)S(1)} custom-call(bf16[8,192,2560]{2,1,0:T(8,128)(2,1)S(1)} %bitcast.46), custom_call_target="tpu_custom_call" | custom-call | tf_op jit(solution)/shard_map/pallas_call | solution.py:325
  1003.6 0.7 slice.144
  1004.3 1.1 multiply_reduce_fusion.3
  1005.4 0.6 dynamic-slice_divide_fusion
  1006.0 8.1 fusion.7
  1014.1 0.7 fusion.43
  1014.8 1.9 fusion.18
  1016.7 1.2 copy.80
  1018.0 0.6 slice.175
  1018.6 1.0 copy.76
  1019.5 0.5 slice_bitcast_fusion
  1020.1 6.8 copy.88
  1026.8 1.7 copy.89
  (112 shorter events, 6.8 us)
Async XLA Ops:
  7.2 3.9 copy-start.16
  7.2 3.9 copy-start.21
  7.2 191.3 %all-gather.3.cloned.1.call-start = ((), (), s32[]{:S(2)}) async-start(), calls=%async_computation.1 | async-start | bytes 28966912 | tf_op jit(solution)/shard_map/all_gather | solution.py:931
  11.0 1005.6 %reduce-scatter.4.cloned.1.call-start = ((), (), s32[]{:S(2)}) async-start(), calls=%async_computation.2 | async-start | bytes 5271552
  11.1 105.4 %copy-start.9 = (bf16[1,512,1536]{2,1,0:T(8,128)(2,1)S(1)}, bf16[1,512,1536]{2,1,0:T(8,128)(2,1)}, u32[]{:S(2)}) copy-start(bf16[1,512,1536]{2,1,0:T(8,128)(2,1)} %param.14) | copy-start | bytes 4718596
  13.9 103.0 %copy-start.29 = (f32[1536]{0:T(1024)S(1)}, f32[1536]{0:T(1024)}, u32[]{:S(2)}) copy-start(f32[1536]{0:T(1024)} %param.16) | copy-start | bytes 18436
  116.9 6.8 copy-start.27
  123.7 2.4 copy-start.12
  130.6 27.0 %collective-permute-start = (bf16[512,1024]{1,0:T(8,128)(2,1)}, bf16[512,1024]{1,0:T(8,128)(2,1)}, u32[]{:S(2)}, u32[]{:S(2)}) collective-permute-start(bf16[512,1024]{1,0:T(8,128)(2,1)} %pad_maximum_fusion.6), channel_id=1, source_target_pairs={{0,16},{16,0},{1,17},{17,1},{2,18},{18,2},{3,19},{19,3},{4,20},{20... | collective-permute-start | bytes 3145736 | tf_op jit(solution)/shard_map/ppermute | solution.py:351
  141.9 2.6 copy-start
  141.9 13.9 %copy-start.18 = (bf16[1536,32]{0,1:T(8,128)(2,1)S(1)}, bf16[1536,32]{0,1:T(8,128)(2,1)}, u32[]{:S(2)}) copy-start(bf16[1536,32]{0,1:T(8,128)(2,1)} %param.22) | copy-start | bytes 294916
  142.4 15.0 %copy-start.23 = (s32[1,512,8]{1,2,0:T(8,128)S(1)}, s32[1,512,8]{1,2,0:T(8,128)}, u32[]{:S(2)}) copy-start(s32[1,512,8]{1,2,0:T(8,128)} %param.25) | copy-start | bytes 49156
  188.2 6.1 copy-start.22
  194.2 1.7 copy-start.1
  194.2 1.0 copy-start.19
  195.2 2.1 copy-start.3
  195.9 0.6 copy-start.24
  753.3 8.2 copy-start.25
  753.3 8.2 copy-start.26
  753.3 8.9 copy-start.2
  753.3 8.9 copy-start.20
  762.3 1.4 copy-start.4
  762.3 4.2 copy-start.11
  764.9 79.1 %collective-permute-start.2 = (f32[24]{0:T(128)S(1)}, f32[24]{0:T(128)S(1)}, u32[]{:S(2)}, u32[]{:S(2)}) collective-permute-start(f32[24]{0:T(128)S(1)} %fusion.32), channel_id=1, source_target_pairs={{0,16},{16,0},{1,17},{17,1},{2,18},{18,2},{3,19},{19,3},{4,20},{20... | collective-permute-start | bytes 296 | tf_op jit(solution)/shard_map/ppermute | solution.py:76
  766.4 2.2 copy-start.31
  768.6 2.9 copy-start.6
  836.3 2.2 copy-start.14
  838.6 3.4 copy-start.5
  838.8 2.1 copy-start.8
  841.1 18.7 %collective-permute-start.1 = (bf16[512,1024]{1,0:T(8,128)(2,1)S(1)}, bf16[512,1024]{1,0:T(8,128)(2,1)}, u32[]{:S(2)}, u32[]{:S(2)}) collective-permute-start(bf16[512,1024]{1,0:T(8,128)(2,1)S(1)} %dynamic-slice_convert_fusion), channel_id=1, source_target_pairs={{0,16},{16,0},{1,17},{17,1},{2,18},{18,2},{3,19},{19,3},{4,20},{20... | collective-permute-start | bytes 3145736 | tf_op jit(solution)/shard_map/ppermute | solution.py:365
  863.3 5.2 copy-start.10
  863.3 5.2 copy-start.28
  863.3 5.2 copy-start.30
  875.5 130.5 %copy-start.15 = (bf16[512,24,64]{0,2,1:T(8,128)(2,1)S(1)}, bf16[512,24,64]{0,2,1:T(8,128)(2,1)}, u32[]{:S(2)}) copy-start(bf16[512,24,64]{0,2,1:T(8,128)(2,1)} %fusion.15) | copy-start | bytes 4718596
  875.5 130.5 %copy-start.17 = (bf16[512,512]{0,1:T(8,128)(2,1)S(1)}, bf16[512,512]{0,1:T(8,128)(2,1)}, u32[]{:S(2)}) copy-start(bf16[512,512]{0,1:T(8,128)(2,1)} %copy.75) | copy-start | bytes 1572868
  1006.0 8.8 copy-start.7
  1020.1 6.8 copy-start.13
Sparse Core Ops, SparseCore 0:
  11.1 179.3 all-gather.2
  782.1 179.7 reduce-scatter.3

commit v4 on v3

--- a/solution.py
+++ b/solution.py
@@ -180,6 +180,10 @@
             jax.ShapeDtypeStruct((steps, 8, 128), jnp.float32),
         ),
         scratch_shapes=[pltpu.VMEM((keys, rows), jnp.float32)],
+        cost_estimate=pl.CostEstimate(
+            flops=16 * rows * keys * query_width, bytes_accessed=8 * 2**20,
+            transcendentals=rows * keys * QUERY_HEADS,
+        ),
         compiler_params=pltpu.CompilerParams(vmem_limit_bytes=50 * 2**20),
     )(position, docs_all[:, None], docs_own[None, :], query, key, value)
     return mix, logs, tops[:, : QUERY_HEADS // steps, 0].reshape(QUERY_HEADS)
@@ -201,21 +205,30 @@
             jax.ShapeDtypeStruct((keys, key_width), jnp.float32),
         ),
         scratch_shapes=[pltpu.VMEM((keys, rows), jnp.float32)],
+        cost_estimate=pl.CostEstimate(
+            flops=40 * rows * keys * query_width, bytes_accessed=16 * 2**20,
+            transcendentals=rows * keys * QUERY_HEADS,
+        ),
         compiler_params=pltpu.CompilerParams(vmem_limit_bytes=50 * 2**20),
     )(position, docs_all[:, None], docs_own[None, :], query, key, value, mix_grad, logs)
 
 
 def scatter_kernel(
-    whole_ref, total_ref, from_core, pair_sum, first_x, first_y, mid, last_x, last_y, sums, from_line,
-    core_send, core_recv, x_send, x_recv, y_send, y_recv, z_send, z_recv,
+    whole_a, whole_b, total_a, total_b, core_a, core_b, pair_a, pair_b, first_a, first_b, mid_a, mid_b,
+    last_a, last_b, sums_a, sums_b, line_a, line_b,
+    core_send, core_recv, first_send, first_recv, last_send, last_recv, line_send, line_recv,
 ):
     half, expert, depth = lax.axis_index("dp"), lax.axis_index("expert"), lax.axis_index("shard")
     side, core = expert // 2, expert % 2
     partner = {"dp": 1 - half}
     opposite = {"expert": 2 * ((side + 1) % 2) + core}
     sibling = {"expert": 2 * side + (core + 1) % 2}
-    cols = whole_ref.shape[2] // 2
-    left, right = pl.ds(0, cols), pl.ds(cols, cols)
+    whole, total, from_core, pair_sum = (
+        (whole_a, whole_b), (total_a, total_b), (core_a, core_b), (pair_a, pair_b)
+    )
+    first, mid, last, sums, from_line = (
+        (first_a, first_b), (mid_a, mid_b), (last_a, last_b), (sums_a, sums_b), (line_a, line_b)
+    )
 
     def along(distance):
         return {"shard": (depth + distance) % 4}
@@ -237,112 +250,96 @@
     def chunk(j, other_core):
         return 4 * ((half + j // 2) % 2) + 2 * ((side + j % 2) % 2) + (core + other_core) % 2
 
-    def to_core(j):
+    def to_core(w, j):
         return remote(
-            whole_ref.at[chunk(j, 1)], from_core.at[j], core_send.at[j], core_recv.at[j], sibling
-        )
-
-    def to_x(k):
+            whole[w].at[chunk(j, 1)], from_core[w].at[j], core_send.at[w, j], core_recv.at[w, j], sibling
+        )
+
+    def to_first(w, k):
+        j = 2 + k if w == 0 else 2 * k + 1
         return remote(
-            pair_sum.at[2 + k, :, left], first_x.at[k], x_send.at[k], x_recv.at[k], partner
-        )
-
-    def to_y(k):
+            pair_sum[w].at[j], first[w].at[k], first_send.at[w, k], first_recv.at[w, k],
+            (partner, opposite)[w],
+        )
+
+    def to_last(w):
+        return remote(mid[w], last[w], last_send.at[w], last_recv.at[w], (opposite, partner)[w])
+
+    def to_line(w, zi):
         return remote(
-            pair_sum.at[2 * k + 1, :, right], first_y.at[k], y_send.at[k], y_recv.at[k], opposite
-        )
-
-    def then_y():
-        return remote(mid.at[0], last_y, y_send.at[2], y_recv.at[2], opposite)
-
-    def then_x():
-        return remote(mid.at[1], last_x, x_send.at[2], x_recv.at[2], partner)
-
-    def to_line(zi, part):
-        return remote(
-            sums.at[part, (depth + zi) % 4], from_line.at[zi, part], z_send.at[zi, part],
-            z_recv.at[zi, part], along(zi),
-        )
-
-    order = (3, 2, 1, 0)
-    for j in order:
-        to_core(j).start()
-    for j in order:
-        to_core(j).wait_recv()
-        pair_sum[j] = added(whole_ref[chunk(j, 0)], from_core[j])
-        if j == 3:
-            to_x(1).start()
-            to_y(1).start()
-        if j == 2:
-            to_x(0).start()
-        if j == 1:
-            to_y(0).start()
-    to_x(1).wait_recv()
-    mid[0] = added(pair_sum[1, :, left], first_x[1])
-    then_y().start()
-    to_y(1).wait_recv()
-    mid[1] = added(pair_sum[2, :, right], first_y[1])
-    then_x().start()
-    share = sums.shape[2]
-    for part, first, last, last_ref, own in (
-        (0, to_x(0), then_y(), last_y, left), (1, to_y(0), then_x(), last_x, right)
-    ):
-        first.wait_recv()
-        last.wait_recv()
-        near = (first_x if part == 0 else first_y)[0]
+            sums[w].at[(depth + zi) % 4], from_line[w].at[zi], line_send.at[w, zi],
+            line_recv.at[w, zi], along(zi),
+        )
+
+    for j in (3, 2, 1, 0):
+        for w in range(2):
+            to_core(w, j).start()
+    for j in (3, 2, 1, 0):
+        for w in range(2):
+            to_core(w, j).wait_recv()
+            pair_sum[w][j] = added(whole[w][chunk(j, 0)], from_core[w][j])
+            if j == 3:
+                to_first(w, 1).start()
+            if j == 2 - w:
+                to_first(w, 0).start()
+    for w in range(2):
+        to_first(w, 1).wait_recv()
+        mid[w][...] = added(pair_sum[w][1 + w], first[w][1])
+        to_last(w).start()
+    share = sums_a.shape[1]
+    for w in range(2):
+        to_first(w, 0).wait_recv()
+        to_last(w).wait_recv()
         full = (
-            pair_sum[0, :, own].astype(jnp.float32)
-            + near.astype(jnp.float32)
-            + last_ref[...].astype(jnp.float32)
+            pair_sum[w][0].astype(jnp.float32)
+            + first[w][0].astype(jnp.float32)
+            + last[w][...].astype(jnp.float32)
         ).astype(jnp.bfloat16)
         for z in range(4):
-            sums[part, z] = full[z * share : (z + 1) * share]
+            sums[w][z] = full[z * share : (z + 1) * share]
         for zi in (2, 1, 3):
-            to_line(zi, part).start()
-    for part, own in ((0, left), (1, right)):
-        result = sums[part, depth].astype(jnp.float32)
+            to_line(w, zi).start()
+    for w in range(2):
+        result = sums[w][depth].astype(jnp.float32)
         for zi in (1, 3, 2):
-            to_line(zi, part).wait_recv()
-            result = result + from_line[zi, part].astype(jnp.float32)
-        total_ref[:, own] = result
-    for j in order:
-        to_core(j).wait_send()
-    for k in range(2):
-        to_x(k).wait_send()
-        to_y(k).wait_send()
-    then_x().wait_send()
-    then_y().wait_send()
-    for zi in range(1, 4):
-        for part in range(2):
-            to_line(zi, part).wait_send()
-
-
-def scatter_every(whole):
+            to_line(w, zi).wait_recv()
+            result = result + from_line[w][zi].astype(jnp.float32)
+        total[w][...] = result
+    for w in range(2):
+        for j in range(4):
+            to_core(w, j).wait_send()
+        for k in range(2):
+            to_first(w, k).wait_send()
+        to_last(w).wait_send()
+        for zi in range(1, 4):
+            to_line(w, zi).wait_send()
+
+
+def scatter_every(*arrays):
     if lax.axis_size("dp") != 2:
-        return lax.psum_scatter(whole, EVERY, scatter_dimension=0, tiled=True).astype(jnp.float32)
-    rows, width = whole.shape[0] // 8, whole.shape[1]
-    cols, low, dma = width // 2, whole.dtype, pltpu.SemaphoreType.DMA
+        return [
+            lax.psum_scatter(a, EVERY, scatter_dimension=0, tiled=True).astype(jnp.float32)
+            for a in arrays
+        ]
+    rows, low, dma = arrays[0].shape[0] // 8, arrays[0].dtype, pltpu.SemaphoreType.DMA
+    widths = [a.shape[1] for a in arrays]
+    both = lambda *shape: [pltpu.VMEM((*shape, w), low) for w in widths]
+    in_vmem = pl.BlockSpec(memory_space=pltpu.VMEM)
     return pl.pallas_call(
         scatter_kernel,
-        out_shape=jax.ShapeDtypeStruct((rows // 4, width), jnp.float32),
-        in_specs=[pl.BlockSpec(memory_space=pltpu.VMEM)],
-        out_specs=pl.BlockSpec(memory_space=pltpu.VMEM),
+        out_shape=tuple(jax.ShapeDtypeStruct((rows // 4, w), jnp.float32) for w in widths),
+        in_specs=[in_vmem] * 2,
+        out_specs=(in_vmem,) * 2,
         scratch_shapes=[
-            pltpu.VMEM((4, rows, width), low),
-            pltpu.VMEM((4, rows, width), low),
-            pltpu.VMEM((2, rows, cols), low),
-            pltpu.VMEM((2, rows, cols), low),
-            pltpu.VMEM((2, rows, cols), low),
-            pltpu.VMEM((rows, cols), low),
-            pltpu.VMEM((rows, cols), low),
-            pltpu.VMEM((2, 4, rows // 4, cols), low),
-            pltpu.VMEM((4, 2, rows // 4, cols), low),
-            dma((4,)), dma((4,)), dma((3,)), dma((3,)), dma((3,)), dma((3,)), dma((4, 2)), dma((4, 2)),
+            *both(4, rows), *both(4, rows), *both(2, rows), *both(rows), *both(rows),
+            *both(4, rows // 4), *both(4, rows // 4),
+            dma((2, 4)), dma((2, 4)), dma((2, 2)), dma((2, 2)), dma((2,)), dma((2,)),
+            dma((2, 4)), dma((2, 4)),
         ],
         compiler_params=pltpu.CompilerParams(
-            collective_id=2, has_side_effects=True, vmem_limit_bytes=44 * 2**20
+            collective_id=2, has_side_effects=True, vmem_limit_bytes=50 * 2**20
         ),
-    )(whole.reshape(8, rows, width))
+    )(*[a.reshape(8, rows, a.shape[1]) for a in arrays])
 
 
 def gather_dp(rows):
@@ -493,10 +490,11 @@
 
 def experts_kernel(
     in_pairs, hidden_ref, cot_ref, router_ref, win_ref, wout_ref,
-    rows_ref, kept_ref, core_ref, across_ref, line_ref, stage_ref, dwin_ref, dwout_ref, taken_in, taken_out,
-    acc_in, acc_out, win, wout, router, row_tile, cot_tile, made, parts,
+    rows_ref, kept_ref, core_ref, across_ref, near_ref, far_ref, stage_ref, out_ref, dwin_ref, dwout_ref, given_in, given_out,
+    acc_in, acc_out, win, wout, router, row_tile, cot_tile, made, out_tile, parts,
     load_sem, tile_sem, row_recv, core_send, across_send, line_send,
-    made_sem, part_sem, core_recv, across_recv, line_recv, stage_sem, stage_send, store_sem, given_sem, taken_sem,
+    made_sem, part_sem, core_recv, across_recv, near_recv, far_recv,
+    stage_sem, stage_send, store_sem, out_sem,
 ):
     own_count, width = wout_ref.shape[0], wout_ref.shape[1]
     rows_own, model = hidden_ref.shape[0] - 16, hidden_ref.shape[1]
@@ -506,8 +504,8 @@
     sibling = {"expert": 2 * side + (core + 1) % 2}
     opposite = {"expert": 2 * ((side + 1) % 2) + core}
 
-    def along(distance):
-        return {"shard": (depth + distance) % 4}
+    near = {"shard": depth + 1 - 2 * (depth % 2)}
+    far = {"shard": (depth + 2) % 4}
 
     def remote(src, dst, send, recv, to):
         return pltpu.make_async_remote_copy(
@@ -517,8 +515,7 @@
 
     barrier = pltpu.get_barrier_semaphore()
     half = lax.axis_index("dp")
-    partner = {"dp": 1 - half}
-    peers = [sibling, opposite, along(1), along(2), along(3)] + [partner] * in_pairs
+    peers = [sibling, opposite, near, far]
     for peer in peers:
         pl.semaphore_signal(barrier, inc=1, device_id=peer, device_id_type=pl.DeviceIdType.MESH)
     pl.semaphore_wait(barrier, len(peers))
@@ -535,18 +532,21 @@
     def to_opposite(src, r):
         return remote(src, rows_ref.at[r + 2], across_send.at[r // 4], row_recv.at[r + 2], opposite)
 
-    def to_line(zi):
-        return remote(
-            hidden_ref, rows_ref.at[4 * zi], line_send.at[zi], row_recv.at[4 * zi], along(4 - zi)
-        )
+    def to_near():
+        return remote(hidden_ref, rows_ref.at[4], line_send.at[0], row_recv.at[4], near)
+
+    def to_far():
+        return remote(hidden_ref, rows_ref.at[8], line_send.at[1], row_recv.at[8], far)
+
+    def far_to_near():
+        return remote(rows_ref.at[8], rows_ref.at[12], line_send.at[2], row_recv.at[12], near)
 
     def own_rows():
         return pltpu.make_async_copy(hidden_ref, rows_ref.at[0], row_recv.at[0])
 
     to_sibling(hidden_ref, 0).start()
     to_opposite(hidden_ref, 0).start()
-    for zi in range(1, 4):
-        to_line(zi).start()
+    to_far().start()
     own_rows().start()
     for load in loads:
         load.start()
@@ -570,16 +570,34 @@
             def _():
                 to_opposite(rows_ref.at[r], r).start()
 
+            @pl.when(r == 8)
+            def _():
+                far_to_near().start()
+
+    pair_order = (0, 1, 4, 5, 7, 6, 3, 2)
+
     def block_at(step):
-        turn = (step // 2 + 1) // 2
-        place = (turn + 7) % 8
-        return 4 * ((place + place // 4) % 4) + 2 * (1 - place // 4) + (step // 2 + 1) % 2
+        turn = step // 2
+        place = turn // 2
+        pair = 0
+        for i, value in enumerate(pair_order):
+            pair = pair + value * (1 - ((place + 8 - i) % 8 + 7) // 8)
+        return 2 * pair + (turn + (7 - place) // 7) % 2
+
+    def first_row(step):
+        r, sub = block_at(step), step % 2
+        other = 2 * ((side + (r % 4) // 2) % 2) + (core + r) % 2
+        plane = 2 * ((depth // 2 + r // 8) % 2) + (depth + r // 4) % 2
+        return pl.multiple_of((other * 4 + plane) * rows_own + sub * tile, tile)
+
+    def keep_out(step):
+        return pltpu.make_async_copy(
+            out_tile.at[step % 2], out_ref.at[pl.ds(first_row(step), tile)], out_sem.at[step % 2]
+        )
 
     def tiles(step):
         r, sub, slot = block_at(step), step % 2, step % 2
-        other = 2 * ((side + (r % 4) // 2) % 2) + (core + r) % 2
-        start = (other * 4 + (depth + r // 4) % 4) * rows_own + sub * tile
-        start = pl.multiple_of(start, tile)
+        start = first_row(step)
         return (
             pltpu.make_async_copy(
                 rows_ref.at[r, pl.ds(pl.multiple_of(sub * tile, tile), tile)],
@@ -610,7 +628,7 @@
         return pltpu.make_async_copy(made.at[slot], kept_ref.at[r // 2, sub], made_sem.at[slot])
 
     def made_done(step):
-        away = (step // 2 + 1) % 2
+        away = block_at(step) % 2
 
         @pl.when(away == 1)
         def _():
@@ -620,72 +638,82 @@
         def _():
             keep_made(step).wait()
 
-    def send_y(zi, sub):
+    def send_across(zi, slot, sub):
         return remote(
-            stage_ref.at[zi, sub], across_ref.at[zi, sub], stage_send.at[zi, sub],
+            stage_ref.at[slot, sub], across_ref.at[zi, sub], stage_send.at[slot, sub],
             across_recv.at[zi, sub], opposite,
         )
 
-    def send_z(zi, sub):
+    def send_near(zi, slot, sub):
         return remote(
-            stage_ref.at[3 + zi, sub], line_ref.at[zi, sub], stage_send.at[3 + zi, sub],
-            line_recv.at[zi, sub], along(zi),
-        )
-
-    def staged(place, sub):
-        return pltpu.make_async_copy(parts.at[0], stage_ref.at[place, sub], stage_sem.at[0])
-
-    def load_kept(pair, sub):
-        return pltpu.make_async_copy(kept_ref.at[pair, sub], parts.at[0], part_sem.at[0])
-
-    def load_core(pair, sub):
-        return pltpu.make_async_copy(core_ref.at[pair, sub], parts.at[1], part_sem.at[1])
-
-    def load_across(zi, sub):
-        return pltpu.make_async_copy(across_ref.at[zi, sub], parts.at[2], part_sem.at[2])
+            stage_ref.at[slot, sub], near_ref.at[zi // 2, sub], stage_send.at[slot, sub],
+            near_recv.at[zi // 2, sub], near,
+        )
+
+    def send_far(sub):
+        return remote(
+            stage_ref.at[5, sub], far_ref.at[sub], stage_send.at[5, sub], far_recv.at[sub], far
+        )
+
+    def staged(slot, sub):
+        return pltpu.make_async_copy(parts.at[0], stage_ref.at[slot, sub], stage_sem.at[0])
 
     def core_arrived(pair, sub):
         remote(
             made.at[0], core_ref.at[pair, sub], made_sem.at[0], core_recv.at[pair, sub], sibling
         ).wait_recv()
 
-    def begin_y(zi, sub):
-        core_arrived(2 * zi + 1, sub)
-        load_kept(2 * zi + 1, sub).start()
-        load_core(2 * zi + 1, sub).start()
-
-    def end_y(zi, sub):
-        load_kept(2 * zi + 1, sub).wait()
-        load_core(2 * zi + 1, sub).wait()
-        parts[0] = (parts[0].astype(jnp.float32) + parts[1].astype(jnp.float32)).astype(
-            jnp.bfloat16
-        )
-        staged(zi, sub).start()
-
-    def begin_z(zi, sub):
-        core_arrived(2 * zi, sub)
-        send_y(zi, sub).wait_recv()
-        load_kept(2 * zi, sub).start()
-        load_core(2 * zi, sub).start()
-        load_across(zi, sub).start()
-
-    def end_z(zi, sub):
-        load_kept(2 * zi, sub).wait()
-        load_core(2 * zi, sub).wait()
-        load_across(zi, sub).wait()
-        parts[0] = (
-            parts[0].astype(jnp.float32) + parts[1].astype(jnp.float32) + parts[2].astype(jnp.float32)
-        ).astype(jnp.bfloat16)
-        staged(3 + zi, sub).start()
+    def fetch(source, place):
+        return pltpu.make_async_copy(source, parts.at[place], part_sem.at[place])
+
+    def begin_one(kind, zi, sub):
+        pair = 2 * zi + (1 if kind == "y" else 0)
+        core_arrived(pair, sub)
+        fetch(kept_ref.at[pair, sub], 0).start()
+        fetch(core_ref.at[pair, sub], 1).start()
+        if kind != "y":
+            send_across(zi, 0, sub).wait_recv()
+            fetch(across_ref.at[zi, sub], 2).start()
+        if kind == "d":
+            send_near(zi, 0, sub).wait_recv()
+            fetch(near_ref.at[zi // 2, sub], 3).start()
+
+    def end_one(kind, zi, slot, sub):
+        pair = 2 * zi + (1 if kind == "y" else 0)
+        fetch(kept_ref.at[pair, sub], 0).wait()
+        fetch(core_ref.at[pair, sub], 1).wait()
+        total = parts[0].astype(jnp.float32) + parts[1].astype(jnp.float32)
+        if kind != "y":
+            fetch(across_ref.at[zi, sub], 2).wait()
+            total = total + parts[2].astype(jnp.float32)
+        if kind == "d":
+            fetch(near_ref.at[zi // 2, sub], 3).wait()
+            total = total + parts[3].astype(jnp.float32)
+        parts[0] = total.astype(jnp.bfloat16)
+        staged(slot, sub).start()
+
+    def send_one(kind, zi, slot, sub):
+        staged(slot, sub).wait()
+        if kind == "y":
+            send_across(zi, slot, sub).start()
+        if kind == "c":
+            send_near(zi, slot, sub).start()
+        if kind == "d":
+            send_far(sub).start()
+
+    between = (("y", 16, 2, 1), ("y", 20, 3, 0), ("y", 24, 0, 4), ("c", 26, 3, 2), ("y", 28, 1, 3))
+    after_all = (("d", 2, 5), ("c", 1, 6))
+
+    def at_stage(step, act):
+        for kind, begin, zi, slot in between:
+            @pl.when((step == begin) | (step == begin + 1))
+            def _():
+                act(kind, zi, slot)
 
     first = (expert * 4 + depth) * own_count
 
     def body(step, carry):
         slot, sub = step % 2, step % 2
-        stage_y = (step >= 10) & (step < 24) & (step % 4 >= 2)
-        zi_y = (step // 4 - 1) % 4
-        stage_z = (step == 24) | (step == 25) | (step >= 30)
-        zi_z = 1 + (step - 24) // 6
         for copy in tiles(step):
             copy.wait()
 
@@ -697,7 +725,11 @@
             def _():
                 arrive(after)
 
-            for early, r in ((2, 4), (6, 8), (10, 12)):
+            @pl.when(step == 10)
+            def _():
+                to_near().start()
+
+            for early, r in ((7, 8), (11, 12), (16, 4)):
                 @pl.when(step == early)
                 def _():
                     arrive(jnp.int32(r))
@@ -705,32 +737,13 @@
             for copy in tiles(step + 1):
                 copy.start()
 
-        before_y = (step >= 11) & (step < 25) & ((step - 1) % 4 >= 2)
-        before_z = (step == 25) | (step == 26) | (step == 31)
-
-        @pl.when(before_y)
-        def _():
-            zi = ((step - 1) // 4 - 1) % 4
-            staged(zi, 1 - sub).wait()
-            send_y(zi, 1 - sub).start()
-
-        @pl.when(before_z)
-        def _():
-            zi = 1 + (step - 25) // 6
-            staged(3 + zi, 1 - sub).wait()
-            send_z(zi, 1 - sub).start()
-
-        @pl.when(stage_y)
-        def _():
-            begin_y(zi_y, sub)
-
-        @pl.when(stage_z)
-        def _():
-            begin_z(zi_z, sub)
+        at_stage(step - 1, lambda kind, zi, slot: send_one(kind, zi, slot, 1 - sub))
+        at_stage(step, lambda kind, zi, slot: begin_one(kind, zi, sub))
 
         @pl.when(step >= 2)
         def _():
             made_done(step - 2)
+            keep_out(step - 2).wait()
 
         rows, cot = row_tile[slot], cot_tile[slot, :, :model]
         logits = jnp.dot(rows, router[...], preferred_element_type=jnp.float32)
@@ -767,10 +780,11 @@
             acc_in[e] += contract_rows(rows, d_both)
             acc_out[e] += contract_rows(gated, cot)
         made[slot, :, :model] = grad_sum.astype(jnp.bfloat16)
-        made[slot, :, model : 2 * model] = out_sum.astype(jnp.bfloat16)
-        made[slot, :, 2 * model :] = gate_grads.astype(jnp.bfloat16)
-
-        away = (step // 2 + 1) % 2
+        made[slot, :, model:] = gate_grads.astype(jnp.bfloat16)
+        out_tile[slot] = out_sum.astype(jnp.bfloat16)
+        keep_out(step).start()
+
+        away = block_at(step) % 2
 
         @pl.when(away == 1)
         def _():
@@ -780,82 +794,64 @@
         def _():
             keep_made(step).start()
 
-        @pl.when(stage_y)
-        def _():
-            end_y(zi_y, sub)
-
-        @pl.when(stage_z)
-        def _():
-            end_z(zi_z, sub)
-
+        at_stage(step, lambda kind, zi, slot: end_one(kind, zi, slot, sub))
         return carry
 
     lax.fori_loop(0, 32, body, 0)
     win[...] = acc_in[...].astype(jnp.bfloat16)
     wout[...] = acc_out[...].astype(jnp.bfloat16)
-    grads = ((acc_in, win, taken_in, dwin_ref), (acc_out, wout, taken_out, dwout_ref))
+    grads = ((acc_in, win, dwin_ref, given_in), (acc_out, wout, dwout_ref, given_out))
 
     def half_rows(ref, at):
         size = ref.shape[1] // 2
         return ref.at[:, pl.ds(pl.multiple_of(at * size, size), size)]
 
-    def give(which):
-        _, sent, taken, _ = grads[which]
-        return remote(
-            half_rows(sent, 1 - half), taken, given_sem.at[which], taken_sem.at[which], partner
-        )
-
-    def store(which):
-        total, sent, _, result = grads[which]
-        return pltpu.make_async_copy(
-            half_rows(total, half) if in_pairs else sent, result, store_sem.at[which]
-        )
-
-    for which in range(2):
-        give(which).start() if in_pairs else store(which).start()
-    staged(5, 1).wait()
-    send_z(2, 1).start()
-    for sub in range(2):
-        begin_z(3, sub)
-        end_z(3, sub)
-        staged(6, sub).wait()
-        send_z(3, sub).start()
+    stores = []
+    for which, (total, low, result, given) in enumerate(grads):
+        if in_pairs:
+            stores.append(
+                pltpu.make_async_copy(half_rows(low, 1 - half), given, store_sem.at[which, 0])
+            )
+            stores.append(
+                pltpu.make_async_copy(half_rows(total, half), result, store_sem.at[which, 1])
+            )
+        else:
+            stores.append(pltpu.make_async_copy(low, result, store_sem.at[which, 0]))
+    for store in stores:
+        store.start()
+    for kind, zi, slot in after_all:
+        for sub in range(2):
+            begin_one(kind, zi, sub)
+            end_one(kind, zi, slot, sub)
+            send_one(kind, zi, slot, sub)
     made_done(30)
     made_done(31)
+    keep_out(30).wait()
+    keep_out(31).wait()
     for sub in range(2):
         core_arrived(0, sub)
-        send_y(0, sub).wait_recv()
-        for zi in range(4):
-            send_y(zi, sub).wait_send()
-        for zi in range(1, 4):
-            send_z(zi, sub).wait_send()
-            send_z(zi, sub).wait_recv()
+        send_across(0, 4, sub).wait()
+        send_near(0, 0, sub).wait_recv()
+        send_far(sub).wait()
+        for zi, slot in ((2, 1), (3, 0), (1, 3)):
+            send_across(zi, slot, sub).wait_send()
+        send_near(3, 2, sub).wait_send()
+        send_near(1, 6, sub).wait_send()
     for r in range(0, 16, 2):
         to_sibling(hidden_ref, r).wait_send()
     for r in range(0, 16, 4):
         to_opposite(hidden_ref, r).wait_send()
-    for zi in range(1, 4):
-        to_line(zi).wait_send()
-    if in_pairs:
-        for which in range(2):
-            total, sent, taken, _ = grads[which]
-            give(which).wait_recv()
-            fetch = pltpu.make_async_copy(taken, half_rows(sent, half), load_sem.at[which])
-            fetch.start()
-            fetch.wait()
-            size = total.shape[1] // 2
-            rows = pl.ds(pl.multiple_of(half * size, size), size)
-            total[:, rows] += sent[:, rows].astype(jnp.float32)
-            store(which).start()
-            give(which).wait_send()
-    for which in range(2):
-        store(which).wait()
+    to_near().wait_send()
+    to_far().wait_send()
+    far_to_near().wait_send()
+    for store in stores:
+        store.wait()
 
 
 def experts_pass(hidden, cotangent, w_router, expert_in, expert_out):
     rows_own, model = hidden.shape[0] - 16, hidden.shape[1]
     tile = rows_own // 2
-    wide = 2 * model + 128
+    wide = model + 128
     anywhere = pl.BlockSpec(memory_space=pl.ANY)
     low = jnp.bfloat16
     kept = jax.ShapeDtypeStruct((8, 2, tile, wide), low)
@@ -870,15 +866,17 @@
             kept,
             kept,
             quarter,
-            quarter,
+            jax.ShapeDtypeStruct((2, 2, tile, wide), low),
+            jax.ShapeDtypeStruct((2, tile, wide), low),
             jax.ShapeDtypeStruct((7, 2, tile, wide), low),
+            jax.ShapeDtypeStruct((16 * rows_own, model), low),
             jax.ShapeDtypeStruct(share(expert_in), jnp.float32 if in_pairs else low),
             jax.ShapeDtypeStruct(share(expert_out), jnp.float32 if in_pairs else low),
             jax.ShapeDtypeStruct(share(expert_in), low),
             jax.ShapeDtypeStruct(share(expert_out), low),
         ),
         in_specs=[anywhere] * 5,
-        out_specs=(anywhere,) * 10,
+        out_specs=(anywhere,) * 12,
         scratch_shapes=[
             pltpu.VMEM(expert_in.shape, jnp.float32),
             pltpu.VMEM(expert_out.shape, jnp.float32),
@@ -888,23 +886,28 @@
             pltpu.VMEM((2, tile, model), low),
             pltpu.VMEM((2, tile, cotangent.shape[1]), low),
             pltpu.VMEM((2, tile, wide), low),
-            pltpu.VMEM((3, tile, wide), low),
-            dma((3,)), dma((2, 2)), dma((16,)), dma((8,)), dma((4,)), dma((4,)),
-            dma((2,)), dma((3,)), dma((8, 2)), dma((4, 2)), dma((4, 2)), dma((1,)), dma((7, 2)), dma((2,)), dma((2,)), dma((2,)),
+            pltpu.VMEM((2, tile, model), low),
+            pltpu.VMEM((4, tile, wide), low),
+            dma((3,)), dma((2, 2)), dma((16,)), dma((8,)), dma((4,)), dma((3,)),
+            dma((2,)), dma((4,)), dma((8, 2)), dma((4, 2)), dma((2, 2)), dma((2,)),
+            dma((1,)), dma((7, 2)), dma((2, 2)), dma((2,)),
         ],
         compiler_params=pltpu.CompilerParams(
             collective_id=0, has_side_effects=True, vmem_limit_bytes=60 * 2**20
         ),
     )(hidden, cotangent, w_router, expert_in, expert_out)
-    rows, kept, core, across, line, _, weight_in_grad, weight_out_grad, _, _ = results
+    rows, kept, core, across, near, far, _, partial_out, *grads = results
     total = kept[0].astype(jnp.float32) + core[0].astype(jnp.float32)
     total = total + across[0].astype(jnp.float32)
-    for zi in range(1, 4):
-        total = total + line[zi].astype(jnp.float32)
-    if not in_pairs:
-        weight_in_grad = scatter_dp(weight_in_grad, 1)
-        weight_out_grad = scatter_dp(weight_out_grad, 1)
-    return total.reshape(rows_own, wide), rows[:, rows_own, :128], weight_in_grad, weight_out_grad
+    total = total + near[0].astype(jnp.float32) + far.astype(jnp.float32)
+    if in_pairs:
+        swap = lambda given: lax.ppermute(given, "dp", [(0, 1), (1, 0)])
+        weight_in_grad, weight_out_grad = (grads[0], swap(grads[2])), (grads[1], swap(grads[3]))
+    else:
+        weight_in_grad, weight_out_grad = (scatter_dp(grads[0], 1),), (scatter_dp(grads[1], 1),)
+    branch = lax.psum_scatter(partial_out, GROUP, scatter_dimension=0, tiled=True)
+    summed = total.reshape(rows_own, wide)
+    return summed, branch, rows[:, rows_own, :128], weight_in_grad, weight_out_grad
 
 
 def on_device(
@@ -985,7 +988,7 @@
     extra = jnp.broadcast_to(
         jnp.pad(in_three, (0, hidden_ffn.shape[1] - in_three.shape[0])), (16, hidden_ffn.shape[1])
     )
-    summed, maxima, grad_in_shard, grad_out_shard = experts_pass(
+    summed, branch_ffn, maxima, in_parts, out_parts = experts_pass(
         jnp.concatenate([hidden_ffn, extra], axis=0), all_cotangent, w_router, expert_in, expert_out
     )
     model = hidden_ffn.shape[1]
@@ -998,8 +1001,7 @@
     )
     largest = max_dp(largest)
     grad_hidden_ffn = summed[:, :model]
-    out = (residual + summed[:, model : 2 * model]).astype(jnp.bfloat16)
-    gate_cols = summed[:, 2 * model :]
+    gate_cols = summed[:, model:]
     grad_gates = gate_cols[:, :expert_count] + gate_cols[:, 64 : 64 + expert_count]
     weighted = gate_weights * jnp.where(picked, grad_gates, 0.0)
     grad_logits = (
@@ -1011,14 +1013,9 @@
     grad_residual = grad_out + norm_back(grad_hidden_ffn, normed_ffn, scale_ffn, gain_ffn)
     grad_branch = grad_residual.astype(jnp.bfloat16)
     output_grad = contract_rows(grad_branch, attn_low)
-    late_sums = lax.psum_scatter(
-        jnp.concatenate(
-            [output_grad, router_grad, as_column(gain_ffn_grad, expert_count)], axis=1
-        ).astype(jnp.bfloat16),
-        EVERY,
-        scatter_dimension=0,
-        tiled=True,
-    ).astype(jnp.float32)
+    late_grads = jnp.concatenate(
+        [output_grad, router_grad, as_column(gain_ffn_grad, expert_count)], axis=1
+    ).astype(jnp.bfloat16)
     attention_gradient = jnp.dot(
         grad_branch, full_output, preferred_element_type=jnp.float32
     ).astype(jnp.bfloat16)
@@ -1047,7 +1044,15 @@
         .astype(jnp.bfloat16)
     )
     all_grad_low = jnp.concatenate([query_grad_low, key_grad_low, value_grad_low], axis=1)
-    attn_sums = scatter_every(contract_rows(hidden_attn, all_grad_low).astype(jnp.bfloat16))
+    attn_sums, late_sums = scatter_every(
+        contract_rows(hidden_attn, all_grad_low).astype(jnp.bfloat16), late_grads
+    )
+    attn_sums, late_sums, branch_ffn, in_parts, out_parts = lax.optimization_barrier(
+        (attn_sums, late_sums, branch_ffn, in_parts, out_parts)
+    )
+    out = (residual + branch_ffn.astype(jnp.float32)).astype(jnp.bfloat16)
+    grad_in_shard = sum(p.astype(jnp.float32) for p in in_parts)
+    grad_out_shard = sum(p.astype(jnp.float32) for p in out_parts)
     grad_hidden_attn = contract_cols(all_grad_low, full_qkv)
     grad_inputs = grad_residual + norm_back(grad_hidden_attn, normed_attn, scale_attn, gain_attn)
     share = attn_sums.shape[0]

time: 1040 us -> 955 us (0.918)
  Pallas kernels: 857 us -> 782 us
  local copies, waits for them, and re-layouts: 52.4 us -> 41.9 us
    pallas_call x1, Pallas kernels: 555 us -> 433 us  [experts_pass(): pl.pallas_call(functools.partial(experts_kernel, in_pairs), out_shape=(ja...]
    pallas_call x1, Pallas kernels: 128 us -> 174 us  [scatter_every(): pl.pallas_call(scatter_kernel, out_shape=tuple((jax.ShapeDtypeStruct((row...]
    unnamed x72 -> x80, local copies, waits for them, and re-layouts: 28.7 us -> 14.4 us
  transfers between devices with their start and end apart: 5 -> 7, of which waited for: 1 -> 1; matrix products, arithmetic and copies ran while one was open for 10% -> 10% of each run, Pallas kernels for 29% -> 37%
where the time goes in v4:
time: 955 us; the launch traced here: 948 us
  Pallas kernels  782 us (82%)
  other arithmetic  43.9 us (5%)
  matrix products  43 us (5%)
  local copies, waits for them, and re-layouts  41.9 us (4%)
  between operations  15.6 us (2%)
  blocking collectives  14.2 us (1%)
    pallas_call x1, Pallas kernels, experts_pass(): pl.pallas_call(functools.partial(experts_kernel, in_pairs), out_shape=(ja...  433 us
    pallas_call x1, Pallas kernels, scatter_every(): pl.pallas_call(scatter_kernel, out_shape=tuple((jax.ShapeDtypeStruct((row...  174 us
    pallas_call x1, Pallas kernels, gather_weights(): pl.pallas_call(weights_kernel, out_shape=tuple((jax.ShapeDtypeStruct((4 *...  103 us
    pallas_call x1, Pallas kernels, attend_back(): pl.pallas_call(attend_back_kernel, grid=(steps,), in_specs=in_specs + [by...  43.6 us
    pallas_call x1, Pallas kernels, attend(): pl.pallas_call(attend_kernel, grid=(steps,), in_specs=in_specs, out_specs...  28.3 us
  transfers between devices with their start and end apart: 7, of which 1 were waited for; matrix products, arithmetic and copies ran while one was open for 10% of the time, Pallas kernels for 37%

profile of v4, /device:TPU:0, one launch (start us, length us, event | category | flops | bytes accessed | tf_op | source)
XLA Modules:
  0.0 948.3 jit_solution(1016585763519163567)
XLA Ops:
  7.3 1.0 copy.54
  8.3 2.7 fusion.13
  11.1 1.4 pad_maximum_fusion.1.first_ref
  12.5 102.6 %shard_map.245 = (bf16[1536,2560]{1,0:T(8,128)(2,1)}, bf16[1536,1536]{1,0:T(8,128)(2,1)}) custom-call(bf16[384,2560]{1,0:T(8,128)(2,1)} %pad_maximum_fusion.1.first_ref, bf16[384,1536]{1,0:T(8,128)(2,1)} %second_ref.1), custom_call_target="tpu_custom_call" | custom-call | tf_op jit(solution)/shard_map/pallas_call | solution.py:478
  115.5 6.7 fusion.21
  122.3 2.3 copy-done.19
  125.8 1.1 pad_maximum_fusion.6
  126.9 1.5 collective-permute-start
  128.4 3.9 slice.142
  132.3 2.4 copy.49
  134.7 0.5 multiply_subtract_fusion.1
  135.2 0.5 fusion.11
  135.7 1.6 copy.53.query_ref
  137.3 0.5 slice.108.position_ref
  137.8 14.2 %all-gather = s32[1,1024]{1,0:T(1,128)S(1)} all-gather(s32[1,512]{1,0:T(1,128)S(1)} %copy-done), channel_id=2, replica_groups=mesh['dp'=2,'expert'=4,'shard'=4] {'dp'}, dimensions={1}, use_global_device_ids=true | all-gather | bytes 6144 | tf_op jit(solution)/shard_map/all_gather | solution.py:969
  152.2 0.9 copy.55.router_ref
  153.2 1.7 broadcast_select_fusion
  155.0 28.3 %shard_map.246 = (bf16[512,1536]{1,0:T(8,128)(2,1)}, f32[4,8,512]{2,1,0:T(8,128)S(1)}, f32[4,8,128]{2,1,0:T(8,128)S(1)}) custom-call(s32[1]{0:T(128)} %slice.108.position_ref, s32[1024,1]{1,0:T(8,128)S(1)} %copy.52.docs_all_ref, s32[1,512]{1,0:T(1,128)S(1)} %copy-done, bf16[512,1536]{1,0:T(8,128)(2,1)} %copy.53.query_ref, ...), custom_call_target="tpu_custom_call" | custom-call | flops 12884901888 | bytes 8388608 | tf_op jit(solution)/shard_map/pallas_call | solution.py:170
  183.6 6.0 multiply_reduce_fusion.2
  189.7 1.6 copy-done.1
  191.7 1.2 copy-done.4
  192.9 1.3 pad_maximum_fusion.2.hidden_ref
  194.2 432.6 %shard_map.247 = (bf16[16,528,1536]{2,1,0:T(8,128)(2,1)}, bf16[8,2,256,1664]{3,2,1,0:T(8,128)(2,1)}, bf16[8,2,256,1664]{3,2,1,0:T(8,128)(2,1)}, bf16[4,2,256,166...) custom-call(bf16[528,1536]{1,0:T(8,128)(2,1)} %pad_maximum_fusion.2., ...), custom_call_target="tpu_custom_call" | custom-call | tf_op jit(solution)/shard_map/pallas_call | solution.py:862
  627.7 2.2 fusion.41
  630.1 0.8 slice_convert_fusion.2
  631.0 2.2 collective-permute-start.4
  633.1 4.9 bitcast_add_fusion
  638.8 1.1 multiply_reduce_fusion
  639.9 0.7 copy-done.12
  640.6 0.8 multiply_add_fusion
  641.5 1.4 slice-done
  643.1 3.7 convolution_convert_fusion.2.mix_grad_ref
  646.8 43.6 %shard_map.248 = (f32[512,1536]{1,0:T(8,128)}, f32[1024,512]{1,0:T(8,128)}, f32[1024,512]{1,0:T(8,128)}) custom-call(s32[1]{0:T(128)} %slice.108.position_ref, s32[1024,1]{1,0:T(8,128)S(1)} %copy.52.docs_all_ref, s32[1,512]{1,0:T(1,128)S(1)} %copy-done, bf16[512,1536]{1,0:T(8,128)(2,1)} %copy.53.query_ref, bf16[1024,512]{1,0:T(8,128)(2,1)S(1)} %get-tuple-element.122.key_ref, ...), custom_call_target="tpu_custom_call" | custom-call | flops 32212254720 | bytes 16777216 | tf_op jit(solution)/shard_map/pallas_call | solution.py:197
  690.4 2.4 copy.62
  692.8 1.9 constant_dynamic-update-slice_fusion.1
  695.3 1.1 dynamic-slice_convert_fusion
  696.8 1.6 collective-permute-start.2
  698.8 1.1 convolution_convert_fusion.3
  699.9 0.5 multiply_subtract_fusion
  700.4 1.5 copy-done.7
  701.9 0.5 copy-done.35
  702.4 4.5 convolution_convert_fusion.1
  706.8 1.6 fusion.12
  709.1 8.7 concatenate.65.whole_b
  717.7 0.5 fusion.39
  718.8 1.2 multiply_convert_fusion.1
  720.0 0.8 multiply_convert_fusion.2
  720.8 2.0 collective-permute-done.1
  722.8 2.2 convert_add_fusion.3
  725.3 1.3 copy.63
  726.8 1.4 subtract_convert_fusion
  728.2 8.3 convolution_convert_fusion
  736.6 174.4 %shard_map.249 = (f32[48,2560]{1,0:T(8,128)S(1)}, f32[48,1664]{1,0:T(8,128)S(1)}) custom-call(bf16[8,192,2560]{2,1,0:T(8,128)(2,1)} %bitcast.53, bf16[8,192,1664]{2,1,0:T(8,128)(2,1)} %concatenate.65.whole_b), custom_call_target="tpu_custom_call" | custom-call | tf_op jit(solution)/shard_map/pallas_call | solution.py:328
  911.0 9.5 %fusion.5 = (f32[512]{0:T(512)S(1)}, f32[512,1536]{1,0:T(8,128)}) fusion(bf16[1,512,1536]{2,1,0:T(8,128)(2,1)S(1)} %copy-done.11, f32[512]{0:T(512)S(1)} %add_rsqrt_fusion.1, f32[1536]{0:T(1024)S(1)} %copy-done.34, bf16[1536,2560]{1,0:T(8,128)(2,1)} %get-tuple-element.42, bf16[512,512]{0,1:T(8,128)(2,1)S(1)} %copy.64, bf16[512,512]{0,1:T(8,128)(2,1)S(1)} %bitcast.65, ...), kind=kOutput, calls=%fused_computation.15 | convolution fusion | flops 4038327808 | bytes 15214592 | tf_op jit(solution)/shard_map/dot_general | solution.py:58
  920.5 0.7 slice.132
  921.3 0.7 fusion.40
  921.9 0.7 slice.135
  922.7 0.7 slice_reduce_fusion
  923.4 1.1 multiply_reduce_fusion.3
  924.5 0.6 dynamic-slice_divide_fusion
  925.1 0.7 copy.67
  925.8 4.5 convert_add_fusion.2
  930.3 8.2 convert_add_fusion
  938.5 2.7 fusion.14
  (128 shorter events, 7.3 us)
Async XLA Ops:
  7.2 3.9 copy-start.17
  7.2 3.9 copy-start.25
  7.2 3.9 copy-start.31
  7.2 186.9 %all-gather.3.cloned.1.call-start = ((), (), s32[]{:S(2)}) async-start(), calls=%async_computation.1 | async-start | bytes 28966912 | tf_op jit(solution)/shard_map/all_gather | solution.py:934
  11.0 909.5 %reduce-scatter.2.cloned.1.call-start = ((), (), s32[]{:S(2)}) async-start(), calls=%async_computation.2 | async-start | bytes 26738688 | tf_op jit(solution)/shard_map/reduce_scatter | solution.py:908
  11.1 104.0 %copy-start.10 = (bf16[1,512,1536]{2,1,0:T(8,128)(2,1)S(1)}, bf16[1,512,1536]{2,1,0:T(8,128)(2,1)}, u32[]{:S(2)}) copy-start(bf16[1,512,1536]{2,1,0:T(8,128)(2,1)} %param.14) | copy-start | bytes 4718596
  12.5 103.0 %copy-start.34 = (f32[1536]{0:T(1024)S(1)}, f32[1536]{0:T(1024)}, u32[]{:S(2)}) copy-start(f32[1536]{0:T(1024)} %param.16) | copy-start | bytes 18436
  122.2 2.4 copy-start.19
  124.7 2.3 copy-start.13
  125.4 574.5 %copy-start.27 = (f32[512,32]{0,1:T(8,128)}, f32[512,32]{0,1:T(8,128)S(1)}, u32[]{:S(2)}) copy-start(f32[512,32]{0,1:T(8,128)S(1)} %get-tuple-element.131) | copy-start | bytes 196612
  125.8 6.5 copy-start.15
  126.9 26.2 %collective-permute-start = (bf16[512,1024]{1,0:T(8,128)(2,1)}, bf16[512,1024]{1,0:T(8,128)(2,1)}, u32[]{:S(2)}, u32[]{:S(2)}) collective-permute-start(bf16[512,1024]{1,0:T(8,128)(2,1)} %pad_maximum_fusion.6), channel_id=1, source_target_pairs={{0,16},{16,0},{1,17},{17,1},{2,18},{18,2},{3,19},{19,3},{4,20},{20... | collective-permute-start | bytes 3145736 | tf_op jit(solution)/shard_map/ppermute | solution.py:348
  135.2 2.6 copy-start
  135.2 17.0 %copy-start.29 = (bf16[1536,32]{0,1:T(8,128)(2,1)S(1)}, bf16[1536,32]{0,1:T(8,128)(2,1)}, u32[]{:S(2)}) copy-start(bf16[1536,32]{0,1:T(8,128)(2,1)} %param.22) | copy-start | bytes 294916
  135.7 17.4 %copy-start.14 = (bf16[512,512]{1,0:T(8,128)(2,1)S(1)}, bf16[512,512]{1,0:T(8,128)(2,1)}, u32[]{:S(2)}) copy-start(bf16[512,512]{1,0:T(8,128)(2,1)} %copy-done.13) | copy-start | bytes 1572868
  135.7 17.4 %copy-start.16 = (bf16[512,512]{1,0:T(8,128)(2,1)S(1)}, bf16[512,512]{1,0:T(8,128)(2,1)}, u32[]{:S(2)}) copy-start(bf16[512,512]{1,0:T(8,128)(2,1)} %copy-done.15) | copy-start | bytes 1572868
  183.6 7.7 copy-start.32
  189.7 1.7 copy-start.1
  191.7 1.2 copy-start.4
  626.7 0.7 copy-start.33
  627.7 5.4 copy-start.22
  631.0 86.8 %collective-permute-start.4 = (f32[24]{0:T(128)S(1)}, f32[24]{0:T(128)S(1)}, u32[]{:S(2)}, u32[]{:S(2)}) collective-permute-start(f32[24]{0:T(128)S(1)} %fusion.29), channel_id=1, source_target_pairs={{0,16},{16,0},{1,17},{17,1},{2,18},{18,2},{3,19},{19,3},{4,20},{20... | collective-permute-start | bytes 296 | tf_op jit(solution)/shard_map/ppermute | solution.py:76
  633.1 5.7 copy-start.2
  638.8 1.8 copy-start.12
  638.8 4.0 slice-start
  640.6 2.5 slice-start.1
  643.1 3.7 copy-start.6
  692.8 2.2 copy-start.21
  695.0 3.8 copy-start.5
  695.3 4.6 copy-start.9
  696.4 26.4 %collective-permute-start.1 = (bf16[512,1024]{1,0:T(8,128)(2,1)}, bf16[512,1024]{1,0:T(8,128)(2,1)}, u32[]{:S(2)}, u32[]{:S(2)}) collective-permute-start(bf16[512,1024]{1,0:T(8,128)(2,1)} %dynamic-slice_convert_fusion), channel_id=1, source_target_pairs={{0,16},{16,0},{1,17},{17,1},{2,18},{18,2},{3,19},{19,3},{4,20},{20... | collective-permute-start | bytes 3145736 | tf_op jit(solution)/shard_map/ppermute | solution.py:362
  696.8 223.7 %collective-permute-start.2 = (bf16[2,768,1024]{2,1,0:T(8,128)(2,1)}, bf16[2,768,1024]{2,1,0:T(8,128)(2,1)}, u32[]{:S(2)}, u32[]{:S(2)}) collective-permute-start(bf16[2,768,1024]{2,1,0:T(8,128)(2,1)} %get-tuple-element.59), channel_id=1, source_target_pairs={{0,16},{16,0},{1,17},{17,1},{2,18},{18,2},{3,19},{19,3},{4,20},{20... | collective-permute-start | bytes 9437192 | tf_op jit(solution)/shard_map/ppermute | solution.py:904
  698.4 222.0 %collective-permute-start.3 = (bf16[2,256,1536]{2,1,0:T(8,128)(2,1)}, bf16[2,256,1536]{2,1,0:T(8,128)(2,1)}, u32[]{:S(2)}, u32[]{:S(2)}) collective-permute-start(bf16[2,256,1536]{2,1,0:T(8,128)(2,1)} %get-tuple-element.61), channel_id=1, source_target_pairs={{0,16},{16,0},{1,17},{17,1},{2,18},{18,2},{3,19},{19,3},{4,20},{20... | collective-permute-start | bytes 4718600 | tf_op jit(solution)/shard_map/ppermute | solution.py:904
  699.9 2.0 copy-start.7
  699.9 2.5 copy-start.35
  706.8 1.6 copy-start.30
  709.0 9.7 %copy-start.18 = (bf16[384,1536]{1,0:T(8,128)(2,1)S(1)}, bf16[384,1536]{1,0:T(8,128)(2,1)}, u32[]{:S(2)}) copy-start(bf16[384,1536]{1,0:T(8,128)(2,1)} %param.17) | copy-start | bytes 3538948
  709.1 10.9 %copy-start.26 = (bf16[384,512]{1,0:T(8,128)(2,1)S(1)}, bf16[384,512]{1,0:T(8,128)(2,1)}, u32[]{:S(2)}) copy-start(bf16[384,512]{1,0:T(8,128)(2,1)} %param.18) | copy-start | bytes 1179652
  725.1 1.7 copy-start.28
  725.2 3.0 copy-start.11
  736.6 174.4 %copy-start.24 = (bf16[512,24,64]{0,2,1:T(8,128)(2,1)S(1)}, bf16[512,24,64]{0,2,1:T(8,128)(2,1)}, u32[]{:S(2)}) copy-start(bf16[512,24,64]{0,2,1:T(8,128)(2,1)} %fusion.12) | copy-start | bytes 4718596
  930.3 8.2 copy-start.3
  930.3 8.2 copy-start.8
  930.3 8.2 copy-start.20
  930.3 8.2 copy-start.23
Sparse Core Ops, SparseCore 0:
  11.1 179.3 all-gather.2
  626.9 276.0 reduce-scatter.1

commit v5 on v4

--- a/solution.py
+++ b/solution.py
@@ -214,9 +214,9 @@
 
 
 def scatter_kernel(
-    whole_a, whole_b, total_a, total_b, core_a, core_b, pair_a, pair_b, first_a, first_b, mid_a, mid_b,
+    whole_a, whole_b, grads_ref, weights_ref, total_a, total_b, product, grads, weights, core_a, core_b, pair_a, pair_b, first_a, first_b, mid_a, mid_b,
     last_a, last_b, sums_a, sums_b, line_a, line_b,
-    core_send, core_recv, first_send, first_recv, last_send, last_recv, line_send, line_recv,
+    core_send, core_recv, first_send, first_recv, last_send, last_recv, line_send, line_recv, load_sem,
 ):
     half, expert, depth = lax.axis_index("dp"), lax.axis_index("expert"), lax.axis_index("shard")
     side, core = expert // 2, expert % 2
@@ -274,6 +274,12 @@
     for j in (3, 2, 1, 0):
         for w in range(2):
             to_core(w, j).start()
+    loads = [
+        pltpu.make_async_copy(grads_ref, grads, load_sem.at[0]),
+        pltpu.make_async_copy(weights_ref, weights, load_sem.at[1]),
+    ]
+    for load in loads:
+        load.start()
     for j in (3, 2, 1, 0):
         for w in range(2):
             to_core(w, j).wait_recv()
@@ -282,6 +288,15 @@
                 to_first(w, 1).start()
             if j == 2 - w:
                 to_first(w, 0).start()
+    for load in loads:
+        load.wait()
+
+    def columns(i, carry):
+        own = pl.ds(pl.multiple_of(i * 256, 256), 256)
+        product[:, own] = contract_cols(grads[...], weights[own])
+        return carry
+
+    lax.fori_loop(0, weights.shape[0] // 256, columns, 0)
     for w in range(2):
         to_first(w, 1).wait_recv()
         mid[w][...] = added(pair_sum[w][1 + w], first[w][1])
@@ -315,31 +330,34 @@
             to_line(w, zi).wait_send()
 
 
-def scatter_every(*arrays):
+def scatter_every(grads, weights, *arrays):
     if lax.axis_size("dp") != 2:
         return [
             lax.psum_scatter(a, EVERY, scatter_dimension=0, tiled=True).astype(jnp.float32)
             for a in arrays
-        ]
+        ] + [contract_cols(grads, weights)]
     rows, low, dma = arrays[0].shape[0] // 8, arrays[0].dtype, pltpu.SemaphoreType.DMA
     widths = [a.shape[1] for a in arrays]
     both = lambda *shape: [pltpu.VMEM((*shape, w), low) for w in widths]
     in_vmem = pl.BlockSpec(memory_space=pltpu.VMEM)
     return pl.pallas_call(
         scatter_kernel,
-        out_shape=tuple(jax.ShapeDtypeStruct((rows // 4, w), jnp.float32) for w in widths),
-        in_specs=[in_vmem] * 2,
-        out_specs=(in_vmem,) * 2,
+        out_shape=tuple(jax.ShapeDtypeStruct((rows // 4, w), jnp.float32) for w in widths)
+        + (jax.ShapeDtypeStruct((grads.shape[0], weights.shape[0]), jnp.float32),),
+        in_specs=[in_vmem] * 2 + [pl.BlockSpec(memory_space=pl.ANY)] * 2,
+        out_specs=(in_vmem,) * 3,
         scratch_shapes=[
+            pltpu.VMEM(grads.shape, low),
+            pltpu.VMEM(weights.shape, low),
             *both(4, rows), *both(4, rows), *both(2, rows), *both(rows), *both(rows),
             *both(4, rows // 4), *both(4, rows // 4),
             dma((2, 4)), dma((2, 4)), dma((2, 2)), dma((2, 2)), dma((2,)), dma((2,)),
-            dma((2, 4)), dma((2, 4)),
+            dma((2, 4)), dma((2, 4)), dma((2,)),
         ],
         compiler_params=pltpu.CompilerParams(
-            collective_id=2, has_side_effects=True, vmem_limit_bytes=50 * 2**20
+            collective_id=2, has_side_effects=True, vmem_limit_bytes=58 * 2**20
         ),
-    )(*[a.reshape(8, rows, a.shape[1]) for a in arrays])
+    )(*[a.reshape(8, rows, a.shape[1]) for a in arrays], grads, weights)
 
 
 def gather_dp(rows):
@@ -490,11 +508,11 @@
 
 def experts_kernel(
     in_pairs, hidden_ref, cot_ref, router_ref, win_ref, wout_ref,
-    rows_ref, kept_ref, core_ref, across_ref, near_ref, far_ref, stage_ref, out_ref, dwin_ref, dwout_ref, given_in, given_out,
+    rows_ref, kept_ref, core_ref, across_ref, near_ref, far_ref, stage_ref, out_ref, dwin_ref, dwout_ref, taken_in, taken_out,
     acc_in, acc_out, win, wout, router, row_tile, cot_tile, made, out_tile, parts,
     load_sem, tile_sem, row_recv, core_send, across_send, line_send,
     made_sem, part_sem, core_recv, across_recv, near_recv, far_recv,
-    stage_sem, stage_send, store_sem, out_sem,
+    stage_sem, stage_send, store_sem, out_sem, given_sem, taken_sem,
 ):
     own_count, width = wout_ref.shape[0], wout_ref.shape[1]
     rows_own, model = hidden_ref.shape[0] - 16, hidden_ref.shape[1]
@@ -515,7 +533,8 @@
 
     barrier = pltpu.get_barrier_semaphore()
     half = lax.axis_index("dp")
-    peers = [sibling, opposite, near, far]
+    partner = {"dp": 1 - half}
+    peers = [sibling, opposite, near, far] + [partner] * in_pairs
     for peer in peers:
         pl.semaphore_signal(barrier, inc=1, device_id=peer, device_id_type=pl.DeviceIdType.MESH)
     pl.semaphore_wait(barrier, len(peers))
@@ -701,8 +720,8 @@
         if kind == "d":
             send_far(sub).start()
 
-    between = (("y", 16, 2, 1), ("y", 20, 3, 0), ("y", 24, 0, 4), ("c", 26, 3, 2), ("y", 28, 1, 3))
-    after_all = (("d", 2, 5), ("c", 1, 6))
+    between = (("y", 16, 2, 1), ("y", 20, 3, 0), ("y", 22, 0, 4), ("c", 26, 3, 2), ("y", 28, 1, 3), ("d", 30, 2, 5))
+    after_all = (("c", 1, 6),)
 
     def at_stage(step, act):
         for kind, begin, zi, slot in between:
@@ -800,25 +819,27 @@
     lax.fori_loop(0, 32, body, 0)
     win[...] = acc_in[...].astype(jnp.bfloat16)
     wout[...] = acc_out[...].astype(jnp.bfloat16)
-    grads = ((acc_in, win, dwin_ref, given_in), (acc_out, wout, dwout_ref, given_out))
+    grads = ((acc_in, win, taken_in, dwin_ref), (acc_out, wout, taken_out, dwout_ref))
 
     def half_rows(ref, at):
         size = ref.shape[1] // 2
         return ref.at[:, pl.ds(pl.multiple_of(at * size, size), size)]
 
-    stores = []
-    for which, (total, low, result, given) in enumerate(grads):
-        if in_pairs:
-            stores.append(
-                pltpu.make_async_copy(half_rows(low, 1 - half), given, store_sem.at[which, 0])
-            )
-            stores.append(
-                pltpu.make_async_copy(half_rows(total, half), result, store_sem.at[which, 1])
-            )
-        else:
-            stores.append(pltpu.make_async_copy(low, result, store_sem.at[which, 0]))
-    for store in stores:
-        store.start()
+    def give(which):
+        _, sent, taken, _ = grads[which]
+        return remote(
+            half_rows(sent, 1 - half), taken, given_sem.at[which], taken_sem.at[which], partner
+        )
+
+    def store(which):
+        total, sent, _, result = grads[which]
+        return pltpu.make_async_copy(
+            half_rows(total, half) if in_pairs else sent, result, store_sem.at[which, 0]
+        )
+
+    for which in range(2):
+        give(which).start() if in_pairs else store(which).start()
+    send_one("d", 2, 5, 1)
     for kind, zi, slot in after_all:
         for sub in range(2):
             begin_one(kind, zi, sub)
@@ -844,8 +865,20 @@
     to_near().wait_send()
     to_far().wait_send()
     far_to_near().wait_send()
-    for store in stores:
-        store.wait()
+    if in_pairs:
+        for which in range(2):
+            total, sent, taken, _ = grads[which]
+            give(which).wait_recv()
+            fetch = pltpu.make_async_copy(taken, half_rows(sent, half), load_sem.at[which])
+            fetch.start()
+            fetch.wait()
+            size = total.shape[1] // 2
+            rows = pl.ds(pl.multiple_of(half * size, size), size)
+            total[:, rows] += sent[:, rows].astype(jnp.float32)
+            store(which).start()
+            give(which).wait_send()
+    for which in range(2):
+        store(which).wait()
 
 
 def experts_pass(hidden, cotangent, w_router, expert_in, expert_out):
@@ -890,7 +923,7 @@
             pltpu.VMEM((4, tile, wide), low),
             dma((3,)), dma((2, 2)), dma((16,)), dma((8,)), dma((4,)), dma((3,)),
             dma((2,)), dma((4,)), dma((8, 2)), dma((4, 2)), dma((2, 2)), dma((2,)),
-            dma((1,)), dma((7, 2)), dma((2, 2)), dma((2,)),
+            dma((1,)), dma((7, 2)), dma((2, 2)), dma((2,)), dma((2,)), dma((2,)),
         ],
         compiler_params=pltpu.CompilerParams(
             collective_id=0, has_side_effects=True, vmem_limit_bytes=60 * 2**20
@@ -901,8 +934,7 @@
     total = total + across[0].astype(jnp.float32)
     total = total + near[0].astype(jnp.float32) + far.astype(jnp.float32)
     if in_pairs:
-        swap = lambda given: lax.ppermute(given, "dp", [(0, 1), (1, 0)])
-        weight_in_grad, weight_out_grad = (grads[0], swap(grads[2])), (grads[1], swap(grads[3]))
+        weight_in_grad, weight_out_grad = (grads[0],), (grads[1],)
     else:
         weight_in_grad, weight_out_grad = (scatter_dp(grads[0], 1),), (scatter_dp(grads[1], 1),)
     branch = lax.psum_scatter(partial_out, GROUP, scatter_dimension=0, tiled=True)
@@ -1044,8 +1076,8 @@
         .astype(jnp.bfloat16)
     )
     all_grad_low = jnp.concatenate([query_grad_low, key_grad_low, value_grad_low], axis=1)
-    attn_sums, late_sums = scatter_every(
-        contract_rows(hidden_attn, all_grad_low).astype(jnp.bfloat16), late_grads
+    attn_sums, late_sums, grad_hidden_attn = scatter_every(
+        all_grad_low, full_qkv, contract_rows(hidden_attn, all_grad_low).astype(jnp.bfloat16), late_grads
     )
     attn_sums, late_sums, branch_ffn, in_parts, out_parts = lax.optimization_barrier(
         (attn_sums, late_sums, branch_ffn, in_parts, out_parts)
@@ -1053,7 +1085,6 @@
     out = (residual + branch_ffn.astype(jnp.float32)).astype(jnp.bfloat16)
     grad_in_shard = sum(p.astype(jnp.float32) for p in in_parts)
     grad_out_shard = sum(p.astype(jnp.float32) for p in out_parts)
-    grad_hidden_attn = contract_cols(all_grad_low, full_qkv)
     grad_inputs = grad_residual + norm_back(grad_hidden_attn, normed_attn, scale_attn, gain_attn)
     share = attn_sums.shape[0]
     first_row = (

time: 955 us -> 966 us (1.012)
  waiting for transfers between devices: 2.09 us -> 37.3 us
  Pallas kernels: 782 us -> 756 us
  local copies, waits for them, and re-layouts: 41.9 us -> 58 us
  matrix products: 43 us -> 31.4 us
    pallas_call x1, Pallas kernels: 174 us -> 124 us  [scatter_every(): pl.pallas_call(scatter_kernel, out_shape=tuple((jax.ShapeDtypeStruct((row...]
    reduce_scatter x1, waiting for transfers between devices: 0.02 us -> 36.4 us  [experts_pass(): lax.psum_scatter(partial_out, GROUP, scatter_dimension=0, tiled=True)]
    pallas_call x1, Pallas kernels: 433 us -> 458 us  [experts_pass(): pl.pallas_call(functools.partial(experts_kernel, in_pairs), out_shape=(ja...]
    add x2 -> x0, other arithmetic: 12.7 us -> none  [the longest x1 8.2 us: on_device(): grad_in_shard = sum((p.astype(jnp.float32) for p in in_parts))]
    unnamed x80 -> x82, local copies, waits for them, and re-layouts: 14.4 us -> 23.6 us
  transfers between devices with their start and end apart: 7 -> 5, of which waited for: 1 -> 2; matrix products, arithmetic and copies ran while one was open for 10% -> 10% of each run, Pallas kernels for 37% -> 31%
where the time goes in v5:
time: 966 us; the launch traced here: 957 us
  Pallas kernels  756 us (78%)
  local copies, waits for them, and re-layouts  58 us (6%)
  other arithmetic  40.7 us (4%)
  waiting for transfers between devices  37.3 us (4%)
  matrix products  31.4 us (3%)
  between operations  15.6 us (2%)
  blocking collectives  14.2 us (1%)
    pallas_call x1, Pallas kernels, experts_pass(): pl.pallas_call(functools.partial(experts_kernel, in_pairs), out_shape=(ja...  458 us
    pallas_call x1, Pallas kernels, scatter_every(): pl.pallas_call(scatter_kernel, out_shape=tuple((jax.ShapeDtypeStruct((row...  124 us
    pallas_call x1, Pallas kernels, gather_weights(): pl.pallas_call(weights_kernel, out_shape=tuple((jax.ShapeDtypeStruct((4 *...  103 us
    pallas_call x1, Pallas kernels, attend_back(): pl.pallas_call(attend_back_kernel, grid=(steps,), in_specs=in_specs + [by...  43.6 us
    reduce_scatter x1, waiting for transfers between devices, experts_pass(): lax.psum_scatter(partial_out, GROUP, scatter_dimension=0, tiled=True)  36.4 us
    pallas_call x1, Pallas kernels, attend(): pl.pallas_call(attend_kernel, grid=(steps,), in_specs=in_specs, out_specs...  28.3 us
    unnamed x82, local copies, waits for them, and re-layouts  23.6 us
  transfers between devices with their start and end apart: 5, of which 2 were waited for; matrix products, arithmetic and copies ran while one was open for 10% of the time, Pallas kernels for 31%

profile of v5, /device:TPU:0, one launch (start us, length us, event | category | flops | bytes accessed | tf_op | source)
XLA Modules:
  0.0 956.5 jit_solution(509887925323763515)
XLA Ops:
  7.3 1.0 copy.55
  8.3 2.8 fusion.13
  11.1 1.4 pad_maximum_fusion.1.first_ref
  12.5 102.6 %shard_map.245 = (bf16[1536,2560]{1,0:T(8,128)(2,1)}, bf16[1536,1536]{1,0:T(8,128)(2,1)}) custom-call(bf16[384,2560]{1,0:T(8,128)(2,1)} %pad_maximum_fusion.1.first_ref, bf16[384,1536]{1,0:T(8,128)(2,1)} %second_ref.1), custom_call_target="tpu_custom_call" | custom-call | tf_op jit(solution)/shard_map/pallas_call | solution.py:496
  115.6 6.7 fusion.21
  122.3 2.3 copy-done.20
  125.8 1.1 pad_maximum_fusion.4
  127.0 1.5 collective-permute-start
  128.4 3.9 slice.142
  132.3 2.4 copy.50
  135.7 1.6 copy.54.query_ref
  137.8 14.2 %all-gather = s32[1,1024]{1,0:T(1,128)S(1)} all-gather(s32[1,512]{1,0:T(1,128)S(1)} %copy-done), channel_id=2, replica_groups=mesh['dp'=2,'expert'=4,'shard'=4] {'dp'}, dimensions={1}, use_global_device_ids=true | all-gather | bytes 6144 | tf_op jit(solution)/shard_map/all_gather | solution.py:1001
  152.2 0.9 copy.56.router_ref
  153.2 1.7 broadcast_select_fusion
  155.0 28.3 %shard_map.246 = (bf16[512,1536]{1,0:T(8,128)(2,1)}, f32[4,8,512]{2,1,0:T(8,128)S(1)}, f32[4,8,128]{2,1,0:T(8,128)S(1)}) custom-call(s32[1]{0:T(128)} %slice.108.position_ref, s32[1024,1]{1,0:T(8,128)S(1)} %copy.53.docs_all_ref, s32[1,512]{1,0:T(1,128)S(1)} %copy-done, bf16[512,1536]{1,0:T(8,128)(2,1)} %copy.54.query_ref, ...), custom_call_target="tpu_custom_call" | custom-call | flops 12884901888 | bytes 8388608 | tf_op jit(solution)/shard_map/pallas_call | solution.py:170
  183.6 6.0 multiply_reduce_fusion.2
  189.7 1.6 copy-done.1
  191.7 1.2 copy-done.7
  192.9 1.3 pad_maximum_fusion.2.hidden_ref
  194.1 458.0 %shard_map.247 = (bf16[16,528,1536]{2,1,0:T(8,128)(2,1)}, bf16[8,2,256,1664]{3,2,1,0:T(8,128)(2,1)}, bf16[8,2,256,1664]{3,2,1,0:T(8,128)(2,1)}, bf16[4,2,256,166...) custom-call(bf16[528,1536]{1,0:T(8,128)(2,1)} %pad_maximum_fusion.2., ...), custom_call_target="tpu_custom_call" | custom-call | tf_op jit(solution)/shard_map/pallas_call | solution.py:895
  653.0 2.2 fusion.39
  655.5 0.8 slice_convert_fusion.2
  656.3 0.9 collective-permute-start.2
  657.2 5.8 bitcast_add_fusion
  663.8 1.1 multiply_reduce_fusion
  664.9 0.7 copy-done.13
  665.6 0.9 multiply_add_fusion
  666.4 1.5 slice-done
  668.1 3.7 convolution_convert_fusion.2.mix_grad_ref
  671.8 43.6 %shard_map.248 = (f32[512,1536]{1,0:T(8,128)}, f32[1024,512]{1,0:T(8,128)}, f32[1024,512]{1,0:T(8,128)}) custom-call(s32[1]{0:T(128)} %slice.108.position_ref, s32[1024,1]{1,0:T(8,128)S(1)} %copy.53.docs_all_ref, s32[1,512]{1,0:T(1,128)S(1)} %copy-done, bf16[512,1536]{1,0:T(8,128)(2,1)} %copy.54.query_ref, bf16[1024,512]{1,0:T(8,128)(2,1)S(1)} %get-tuple-element.116.key_ref, ...), custom_call_target="tpu_custom_call" | custom-call | flops 32212254720 | bytes 16777216 | tf_op jit(solution)/shard_map/pallas_call | solution.py:197
  715.4 2.4 copy.63
  717.8 2.0 constant_dynamic-update-slice_fusion.1
  720.4 1.1 dynamic-slice_convert_fusion
  721.5 0.8 collective-permute-start.1
  723.3 1.5 copy-done.10
  725.3 4.5 convolution_convert_fusion.1
  730.2 0.7 copy.65
  730.9 0.9 copy.67
  732.1 0.8 pad.15.clone
  733.0 8.7 concatenate.65.whole_b
  742.7 0.8 multiply_convert_fusion.2
  743.5 1.2 multiply_convert_fusion.1
  744.7 0.9 collective-permute-done.1
  745.6 2.2 convert_add_fusion.1
  747.9 0.9 slice.216
  748.8 1.3 copy.64
  750.1 1.4 subtract_convert_fusion
  751.4 0.8 pad_maximum_fusion.6
  752.3 2.2 copy.66
  754.4 3.0 pad_maximum_fusion.grads_ref
  757.4 6.9 convolution_convert_fusion
  764.3 123.6 %shard_map.249 = (f32[48,2560]{1,0:T(8,128)}, f32[48,1664]{1,0:T(8,128)}, f32[512,1536]{1,0:T(8,128)}) custom-call(bf16[8,192,2560]{2,1,0:T(8,128)(2,1)} %bitcast.52, bf16[8,192,1664]{2,1,0:T(8,128)(2,1)} %concatenate.65.whole_b, bf16[512,2560]{1,0:T(8,128)(2,1)} %pad_maximum_fusion.grads_ref, bf16[1536,2560]{1,0:T(8,128)(2,1)} %get-tuple-element.39.weights_ref), custom_call_target="tpu_custom_call" | custom-call | tf_op jit(solution)/shard_map/pallas_call | solution.py:343
  887.9 2.7 fusion.5
  891.3 4.1 fusion.15
  895.4 36.4 %reduce-scatter.2.cloned.1.call-done = bf16[512,1536]{1,0:T(8,128)(2,1)} async-done(((bf16[8192,1536]{1,0:T(8,128)(2,1)}), bf16[512,1536]{1,0:T(8,128)(2,1)}) %reduce-scatter.2.cloned.1.call-update) | async-done | bytes 1572880 | tf_op jit(solution)/shard_map/reduce_scatter | solution.py:940
  931.9 1.8 slice.132
  933.7 1.6 fusion.38
  935.3 0.7 slice.135
  936.0 0.7 slice_reduce_fusion
  936.7 1.2 multiply_reduce_fusion.3
  938.6 1.7 fusion.14
  940.3 0.7 copy.69
  941.0 6.8 copy.80
  947.7 1.7 copy.81
  (127 shorter events, 10.8 us)
Async XLA Ops:
  7.2 3.9 copy-start.18
  7.2 3.9 copy-start.27
  7.2 3.9 copy-start.30
  7.2 186.9 %all-gather.3.cloned.1.call-start = ((), (), s32[]{:S(2)}) async-start(), calls=%async_computation.1 | async-start | bytes 28966912 | tf_op jit(solution)/shard_map/all_gather | solution.py:966
  11.0 920.8 %reduce-scatter.2.cloned.1.call-start = ((), (), s32[]{:S(2)}) async-start(), calls=%async_computation.2 | async-start | bytes 26738688 | tf_op jit(solution)/shard_map/reduce_scatter | solution.py:940
  11.1 104.0 %copy-start.4 = (bf16[1,512,1536]{2,1,0:T(8,128)(2,1)S(1)}, bf16[1,512,1536]{2,1,0:T(8,128)(2,1)}, u32[]{:S(2)}) copy-start(bf16[1,512,1536]{2,1,0:T(8,128)(2,1)} %param.14) | copy-start | bytes 4718596
  12.5 103.0 %copy-start.34 = (f32[1536]{0:T(1024)S(1)}, f32[1536]{0:T(1024)}, u32[]{:S(2)}) copy-start(f32[1536]{0:T(1024)} %param.16) | copy-start | bytes 18436
  122.3 2.4 copy-start.20
  124.7 2.3 copy-start.14
  125.8 6.5 copy-start.16
  127.0 26.2 %collective-permute-start = (bf16[512,1024]{1,0:T(8,128)(2,1)}, bf16[512,1024]{1,0:T(8,128)(2,1)}, u32[]{:S(2)}, u32[]{:S(2)}) collective-permute-start(bf16[512,1024]{1,0:T(8,128)(2,1)} %pad_maximum_fusion.4), channel_id=1, source_target_pairs={{0,16},{16,0},{1,17},{17,1},{2,18},{18,2},{3,19},{19,3},{4,20},{20... | collective-permute-start | bytes 3145736 | tf_op jit(solution)/shard_map/ppermute | solution.py:366
  135.2 2.6 copy-start
  135.2 17.0 %copy-start.29 = (bf16[1536,32]{0,1:T(8,128)(2,1)S(1)}, bf16[1536,32]{0,1:T(8,128)(2,1)}, u32[]{:S(2)}) copy-start(bf16[1536,32]{0,1:T(8,128)(2,1)} %param.22) | copy-start | bytes 294916
  135.7 17.4 %copy-start.15 = (bf16[512,512]{1,0:T(8,128)(2,1)S(1)}, bf16[512,512]{1,0:T(8,128)(2,1)}, u32[]{:S(2)}) copy-start(bf16[512,512]{1,0:T(8,128)(2,1)} %copy-done.14) | copy-start | bytes 1572868
  135.7 17.4 %copy-start.17 = (bf16[512,512]{1,0:T(8,128)(2,1)S(1)}, bf16[512,512]{1,0:T(8,128)(2,1)}, u32[]{:S(2)}) copy-start(bf16[512,512]{1,0:T(8,128)(2,1)} %copy-done.16) | copy-start | bytes 1572868
  183.6 7.7 copy-start.32
  189.7 1.7 copy-start.1
  191.7 1.2 copy-start.7
  652.1 0.7 copy-start.33
  653.0 4.2 copy-start.25
  656.3 85.3 %collective-permute-start.2 = (f32[24]{0:T(128)S(1)}, f32[24]{0:T(128)S(1)}, u32[]{:S(2)}, u32[]{:S(2)}) collective-permute-start(f32[24]{0:T(128)S(1)} %fusion.29), channel_id=1, source_target_pairs={{0,16},{16,0},{1,17},{17,1},{2,18},{18,2},{3,19},{19,3},{4,20},{20... | collective-permute-start | bytes 296 | tf_op jit(solution)/shard_map/ppermute | solution.py:76
  657.2 6.5 copy-start.2
  663.8 1.8 copy-start.13
  663.8 4.2 slice-start
  665.6 2.6 slice-start.1
  668.1 3.7 copy-start.9
  717.8 2.3 copy-start.24
  720.1 2.2 copy-start.8
  720.4 2.4 copy-start.12
  721.5 24.1 %collective-permute-start.1 = (bf16[512,1024]{1,0:T(8,128)(2,1)}, bf16[512,1024]{1,0:T(8,128)(2,1)}, u32[]{:S(2)}, u32[]{:S(2)}) collective-permute-start(bf16[512,1024]{1,0:T(8,128)(2,1)} %dynamic-slice_convert_fusion), channel_id=1, source_target_pairs={{0,16},{16,0},{1,17},{17,1},{2,18},{18,2},{3,19},{19,3},{4,20},{20... | collective-permute-start | bytes 3145736 | tf_op jit(solution)/shard_map/ppermute | solution.py:380
  722.8 2.0 copy-start.10
  722.8 2.5 copy-start.35
  733.0 9.7 %copy-start.28 = (bf16[384,512]{1,0:T(8,128)(2,1)S(1)}, bf16[384,512]{1,0:T(8,128)(2,1)}, u32[]{:S(2)}) copy-start(bf16[384,512]{1,0:T(8,128)(2,1)} %param.18) | copy-start | bytes 1179652
  733.0 10.6 %copy-start.19 = (bf16[384,1536]{1,0:T(8,128)(2,1)S(1)}, bf16[384,1536]{1,0:T(8,128)(2,1)}, u32[]{:S(2)}) copy-start(bf16[384,1536]{1,0:T(8,128)(2,1)} %param.17) | copy-start | bytes 3538948
  752.3 5.2 copy-start.5
  754.4 3.0 copy-start.22
  754.4 3.0 copy-start.23
  887.9 2.7 copy-start.6
  887.9 3.3 copy-start.11
  891.3 44.0 %copy-start.31 = (f32[48,1664]{1,0:T(8,128)S(1)}, f32[48,1664]{1,0:T(8,128)}, u32[]{:S(2)}) copy-start(f32[48,1664]{1,0:T(8,128)} %get-tuple-element.60) | copy-start | bytes 958468
  891.3 47.3 %copy-start.3 = (f32[512,1536]{1,0:T(8,128)S(1)}, f32[512,1536]{1,0:T(8,128)}, u32[]{:S(2)}) copy-start(f32[512,1536]{1,0:T(8,128)} %copy-done.1) | copy-start | bytes 9437188
  931.9 6.7 copy-start.26
  941.0 6.8 copy-start.21
Sparse Core Ops, SparseCore 0:
  11.2 179.3 all-gather.2
  652.3 279.5 reduce-scatter.1
